TPU v7x, 32 devices: a whole 2x2x4 slice. The times are simulated.
32 devices in a mesh: grp: 2 (over y), blk: 16 (over z, x, core).
Axes of the slice: x: 2, y: 2, z: 4, core: 2. Of those that a mesh axis runs over, the one named last changes fastest.
Arguments:
- couplings: bfloat16 [64, 2, 32, 30720], P('blk', None, 'grp'), parts along dimension 2, may hold values from -2 to 2
- elec_vectors: int32 [3, 64], P(None, 'blk'), may hold values from -8 to 8
- phon_vectors: int32 [3, 32], P(None, 'grp'), parts along dimension 1, may hold values from -4 to 4
- degeneracy: int32 [32], P('grp'), parts along dimension 0, may hold values from 1 to 8
- k_point: float32 [6], P('grp'), parts along dimension 0, may hold values from 0 to 1
- q_index: int32 [3, 512], P(None, 'blk'), may hold values from 0 to 15
Outputs:
- bloch_coupling: bfloat16 [2, 1024, 30720], P(None, ('grp', 'blk')), parts along dimension 1
There are 2 independent parts, one for each index of `grp`. A program takes and returns all parts, laid end to end along the dimension named above; an argument that names none is the same for every part. Nothing has to cross between parts.
All inputs are finite; a program needn't handle non-finite values.
Results may differ from a plain program's by a relative error of at most 0.0059.
Values may be sent and summed in bfloat16 or wider, within the bound.
No kernel may reach another device: no remote copies, remote signals or barrier semaphores. Data moves between devices by JAX's collectives and lax.ppermute only.
A program may use at most 64 MiB of HBM per device.

v0:
```python
import math

import jax
import jax.numpy as jnp
from jax import lax
from jax.sharding import PartitionSpec as P

NG = 16


def k_matrix(k_point, elec_vectors):
    theta = 2.0 * math.pi * jnp.sum(k_point[:, None] * elec_vectors.astype(jnp.float32), axis=0)
    kcos = jnp.cos(theta).astype(jnp.bfloat16)
    ksin = jnp.sin(theta).astype(jnp.bfloat16)
    upper = jnp.stack([kcos, -ksin], axis=1).reshape(-1)
    lower = jnp.stack([ksin, kcos], axis=1).reshape(-1)
    return jnp.stack([upper, lower], axis=0)


def q_matrix(q_index, phon_vectors, degeneracy):
    dots = jnp.sum(q_index[:, :, None] * phon_vectors[:, None, :], axis=0)
    wound = jnp.mod(dots, NG).astype(jnp.float32)
    angle = 2.0 * math.pi * wound / NG
    weight = 1.0 / degeneracy.astype(jnp.float32)
    qcos = jnp.cos(angle) * weight[None, :]
    qsin = jnp.sin(angle) * weight[None, :]
    top = jnp.concatenate([qcos, -qsin], axis=1)
    bottom = jnp.concatenate([qsin, qcos], axis=1)
    return jnp.concatenate([top, bottom], axis=0).astype(jnp.bfloat16)


def on_device(couplings, elec_vectors, phon_vectors, degeneracy, k_point, q_index):
    re_here = couplings.shape[0]
    slab = couplings.shape[2]
    width = couplings.shape[3]
    points = q_index.shape[1]
    kmat = k_matrix(k_point, elec_vectors)
    flat = couplings.reshape(re_here * 2, slab * width)
    partial_slab = jnp.dot(kmat, flat, preferred_element_type=jnp.float32).reshape(2, slab, width)
    summed = lax.psum(partial_slab, "blk").astype(jnp.bfloat16)
    qmat = q_matrix(q_index, phon_vectors, degeneracy)
    result = jnp.dot(qmat, summed.reshape(2 * slab, width), preferred_element_type=jnp.float32)
    return result.astype(jnp.bfloat16).reshape(2, points, width)


def solution(mesh):
    placed = (
        P("blk", None, "grp", None),
        P(None, "blk"),
        P(None, "grp"),
        P("grp"),
        P("grp"),
        P(None, "blk"),
    )
    return jax.shard_map(
        on_device,
        mesh=mesh,
        in_specs=placed,
        out_specs=P(None, ("grp", "blk"), None),
        check_vma=False,
    )
```

profile of v0, /device:TPU:0, one launch (start us, length us, event | category | flops | bytes accessed | tf_op | source)
XLA Modules:
  0.0 112.9 jit_solution(4074509989969183084)
XLA Ops:
  0.0 0.8 multiply_reduce_fusion.1
  0.9 0.1 copy.12
  1.0 0.1 stack_reshape.6
  1.1 0.1 copy.13
  1.2 0.1 stack_reshape.7
  1.3 14.6 %fusion.11 = f32[2,16,30720]{2,0,1:T(2,128)} fusion(bf16[1,8]{1,0:T(2,128)(2,1)S(1)} %stack_reshape.7, bf16[1,8]{1,0:T(2,128)(2,1)S(1)} %stack_reshape.6, bf16[1,8,16,30720]{3,2,1,0:T(8,128)(2,1)} %bitcast.21), kind=kOutput, calls=%fused_computation.23 | convolution fusion | flops 15728704 | bytes 11796512 | tf_op jit(solution)/shard_map/dot_general | solution.py:39
  15.8 0.0 copy-start
  15.8 0.0 copy-start.1
  15.8 0.0 copy-start.2
  15.8 93.1 %all-reduce.1 = bf16[2,16,30720]{2,0,1:T(2,128)(2,1)S(1)} all-reduce(f32[2,16,30720]{2,0,1:T(2,128)} %fusion.11), channel_id=1, replica_groups=mesh['grp'=2,'blk'=16] {'blk'}, use_global_device_ids=true, to_apply=%region_2.0 | all-reduce | flops 983040 | bytes 5898240 | tf_op jit(solution)/shard_map/psum | solution.py:40
  108.9 0.6 copy.14
  109.5 0.0 copy-done
  109.5 0.0 copy-done.1
  109.5 0.1 multiply_reduce_fusion
  109.6 0.0 copy-done.2
  109.6 0.1 negate_convert_fusion
  109.7 3.2 %convolution_convert_fusion = bf16[64,30720]{1,0:T(8,128)(2,1)} fusion(bf16[32,30720]{1,0:T(8,128)(2,1)S(1)} %bitcast.22, bf16[32,16]{0,1:T(8,128)(2,1)S(1)} %get-tuple-element.7, bf16[32,16]{0,1:T(8,128)(2,1)S(1)} %get-tuple-element.6, bf16[32,16]{0,1:T(8,128)(2,1)S(1)} %get-tuple-element.5), kind=kOutput, calls=%fused_computation | convolution fusion | flops 127811584 | bytes 5901312 | tf_op jit(solution)/shard_map/dot_general | solution.py:42
  (4 shorter events, 0.1 us)
Async XLA Ops:
  15.8 93.7 %copy-start = (s32[3,16]{1,0:T(4,128)S(1)}, s32[3,16]{1,0:T(4,128)}, u32[]{:S(2)}) copy-start(s32[3,16]{1,0:T(4,128)} %param.8) | copy-start | bytes 580
  15.8 93.7 %copy-start.1 = (s32[3,32]{1,0:T(4,128)S(1)}, s32[3,32]{1,0:T(4,128)}, u32[]{:S(2)}) copy-start(s32[3,32]{1,0:T(4,128)} %param.11) | copy-start | bytes 1156
  15.8 93.8 %copy-start.2 = (s32[16]{0:T(128)S(1)}, s32[16]{0:T(128)}, u32[]{:S(2)}) copy-start(s32[16]{0:T(128)} %param.9) | copy-start | bytes 196
where the time goes:
time: 114 us; the launch traced here: 113 us
  blocking collectives  93.1 us (82%)
  matrix products  17.8 us (16%)
    psum x1, blocking collectives, on_device(): summed = lax.psum(partial_slab, 'blk').astype(jnp.bfloat16)  93.1 us
    dot_general x1, matrix products, on_device(): jnp.dot(kmat, flat, preferred_element_type=jnp.float32)  14.6 us
    dot_general x1, matrix products, on_device(): jnp.dot(qmat, summed.reshape(2 * slab, width), preferred_element_type=jnp...  3.21 us

commit v1 on v0

v1 whole, which is shorter than its diff:
```python
import math

import jax
import jax.numpy as jnp
from jax import lax
from jax.experimental import pallas as pl
from jax.experimental.pallas import tpu as pltpu
from jax.sharding import PartitionSpec as P

NG = 16
BLOCKS = 8
HALF = 4


def block_of(me, position):
    core = me % 2
    first, second = (me // 2) % 2, (me // 4) % 2
    flip = 7 - position
    owner = (core + flip // 4) % 2
    high = jnp.where(owner == 0, first, second)
    low = jnp.where(owner == 0, second, first)
    high = (high + (flip // 2) % 2) % 2
    low = (low + flip % 2) % 2
    return owner * 4 + high * 2 + low


def partial_kernel(me_ref, k_ref, elec_ref, couplings_ref, out_ref, kmat):
    re_here = couplings_ref.shape[0]
    slab = couplings_ref.shape[2]
    rows, depth = kmat.shape

    @pl.when(pl.program_id(0) == 0)
    def _():
        row = lax.broadcasted_iota(jnp.int32, (rows, depth), 0)
        col = lax.broadcasted_iota(jnp.int32, (rows, depth), 1)
        vector = col // (2 * slab)
        theta = jnp.zeros((rows, depth), jnp.float32)
        for e in range(re_here):
            total = k_ref[0] * elec_ref[0, e].astype(jnp.float32)
            total += k_ref[1] * elec_ref[1, e].astype(jnp.float32)
            total += k_ref[2] * elec_ref[2, e].astype(jnp.float32)
            theta = jnp.where(vector == e, 2.0 * math.pi * total, theta)
        cos, sin = jnp.cos(theta), jnp.sin(theta)
        out_part, in_part = row // slab, (col // slab) % 2
        value = jnp.where(out_part == in_part, cos, jnp.where(out_part == 1, sin, -sin))
        kmat[...] = jnp.where(row % slab == col % slab, value, 0.0).astype(kmat.dtype)

    table = couplings_ref[...].reshape(depth, couplings_ref.shape[3])
    out_ref[0] = jnp.dot(kmat[...], table, preferred_element_type=jnp.float32).astype(out_ref.dtype)


def partial_sums(me, k_point, elec_vectors, couplings, offset, dtype):
    re_here, parts, slab, width = couplings.shape
    columns = width // BLOCKS
    return pl.pallas_call(
        partial_kernel,
        grid_spec=pltpu.PrefetchScalarGridSpec(
            num_scalar_prefetch=3,
            grid=(HALF,),
            in_specs=[
                pl.BlockSpec(
                    (re_here, parts, slab, columns),
                    lambda j, me_ref, *_: (0, 0, 0, block_of(me_ref[0], j + offset)),
                )
            ],
            out_specs=pl.BlockSpec((1, parts * slab, columns), lambda j, *_: (j, 0, 0)),
            scratch_shapes=[pltpu.VMEM((parts * slab, re_here * parts * slab), jnp.bfloat16)],
        ),
        out_shape=jax.ShapeDtypeStruct((HALF, parts * slab, columns), dtype),
        compiler_params=pltpu.CompilerParams(vmem_limit_bytes=24 * 2**20),
        cost_estimate=pl.CostEstimate(
            flops=2 * (parts * slab) ** 2 * re_here * width // 2, bytes_accessed=couplings.size, transcendentals=0
        ),
    )(me, k_point, elec_vectors, couplings)


def q_matrix(q_index, phon_vectors, degeneracy):
    dots = jnp.sum(q_index[:, :, None] * phon_vectors[:, None, :], axis=0)
    wound = jnp.mod(dots, NG).astype(jnp.float32)
    angle = 2.0 * math.pi * wound / NG
    weight = 1.0 / degeneracy.astype(jnp.float32)
    qcos = jnp.cos(angle) * weight[None, :]
    qsin = jnp.sin(angle) * weight[None, :]
    top = jnp.concatenate([qcos, -qsin], axis=1)
    bottom = jnp.concatenate([qsin, qcos], axis=1)
    return jnp.concatenate([top, bottom], axis=0).astype(jnp.bfloat16)


def bloch_kernel(me_ref, qmat_ref, *refs):
    slab_ref, out_ref = refs[0], refs[-1]
    points = out_ref.shape[1]
    result = jnp.dot(qmat_ref[...], slab_ref[0], preferred_element_type=jnp.float32).astype(out_ref.dtype)
    out_ref[0] = result[:points]
    out_ref[1] = result[points:]


def bloch(me, qmat, slab, offset, width, out=None):
    blocks, rows, columns = slab.shape
    points = qmat.shape[0] // 2
    in_specs = [
        pl.BlockSpec(qmat.shape, lambda j, *_: (0, 0)),
        pl.BlockSpec((1, rows, columns), lambda j, *_: (j, 0, 0)),
    ]
    operands = [me, qmat, slab]
    aliases = {}
    if out is not None:
        in_specs.append(pl.BlockSpec(memory_space=pl.ANY))
        operands.append(out)
        aliases = {3: 0}
    return pl.pallas_call(
        bloch_kernel,
        grid_spec=pltpu.PrefetchScalarGridSpec(
            num_scalar_prefetch=1,
            grid=(blocks,),
            in_specs=in_specs,
            out_specs=pl.BlockSpec(
                (2, points, columns), lambda j, me_ref, *_: (0, 0, block_of(me_ref[0], j + offset))
            ),
        ),
        out_shape=jax.ShapeDtypeStruct((2, points, width), jnp.bfloat16),
        input_output_aliases=aliases,
        compiler_params=pltpu.CompilerParams(vmem_limit_bytes=24 * 2**20),
        cost_estimate=pl.CostEstimate(
            flops=4 * points * rows * blocks * columns,
            bytes_accessed=4 * points * blocks * columns,
            transcendentals=0,
        ),
    )(*operands)


def on_device(devices, couplings, elec_vectors, phon_vectors, degeneracy, k_point, q_index):
    width = couplings.shape[3]
    wire = jnp.bfloat16
    me = lax.axis_index("blk").astype(jnp.int32).reshape(1)

    def send(array, even, odd):
        return lax.ppermute(array, "blk", [(i, i ^ (odd if i % 2 else even)) for i in range(devices)])

    theirs = partial_sums(me, k_point, elec_vectors, couplings, 0, wire)
    got = send(theirs, 1, 1)
    own = partial_sums(me, k_point, elec_vectors, couplings, HALF, jnp.float32)
    qmat = q_matrix(q_index, phon_vectors, degeneracy)

    first = send((own[:2] + got[:2].astype(jnp.float32)).astype(wire), 2, 4)
    own = own[2:] + got[2:].astype(jnp.float32)
    second = send((own[:1] + first[:1].astype(jnp.float32)).astype(wire), 4, 2)
    own = own[1:] + first[1:].astype(jnp.float32) + second.astype(jnp.float32)
    step = 8
    while step < devices:
        own = own + send(own.astype(wire), step, step).astype(jnp.float32)
        step *= 2
    block = own.astype(wire)
    pair = jnp.concatenate([send(block, 4, 2), block])
    quad = jnp.concatenate([send(pair, 2, 4), pair])
    rest = send(quad, 1, 1)
    out = bloch(me, qmat, quad, HALF, width)
    return bloch(me, qmat, rest, 0, width, out)


def solution(mesh):
    placed = (
        P("blk", None, "grp", None),
        P(None, "blk"),
        P(None, "grp"),
        P("grp"),
        P("grp"),
        P(None, "blk"),
    )
    devices = mesh.shape["blk"]
    return jax.shard_map(
        lambda *arrays: on_device(devices, *arrays),
        mesh=mesh,
        in_specs=placed,
        out_specs=P(None, ("grp", "blk"), None),
        check_vma=False,
    )
```

time: 114 us -> 60.5 us (0.53)
  blocking collectives: 93.1 us -> 0 us
  waiting for transfers between devices: 0 us -> 33.8 us
  matrix products: 17.8 us -> 0 us
  starting transfers between devices: 0 us -> 10.9 us
  Pallas kernels: 0 us -> 9.92 us
  local copies, waits for them, and re-layouts: 0.97 us -> 4.66 us
    psum x1 -> x0, blocking collectives: 93.1 us -> none  [on_device(): summed = lax.psum(partial_slab, 'blk').astype(jnp.bfloat16)]
    ppermute x0 -> x7, waiting for transfers between devices: none -> 33.8 us  [send(): lax.ppermute(array, 'blk', [(i, i ^ (odd if i % 2 else even)) for i in ra...]
    dot_general x2 -> x0, matrix products: 17.8 us -> none  [the longest x1 14.6 us: on_device(): jnp.dot(kmat, flat, preferred_element_type=jnp.float32)]
    ppermute x0 -> x7, starting transfers between devices: none -> 10.9 us  [send(): lax.ppermute(array, 'blk', [(i, i ^ (odd if i % 2 else even)) for i in ra...]
    pallas_call x0 -> x4, Pallas kernels: none -> 9.92 us  [the longest x2 5.06 us: bloch(): pl.pallas_call(bloch_kernel, grid_spec=pltpu.PrefetchScalarGridSpec(num_s...]
    unnamed x6 -> x12, local copies, waits for them, and re-layouts: 0.01 us -> 4.59 us
  transfers between devices with their start and end apart: 0 -> 7, of which waited for: 0 -> 5; matrix products, arithmetic and copies ran while one was open for 0% -> 1% of each run, Pallas kernels for 0% -> 8%
where the time goes in v1:
time: 60.5 us; the launch traced here: 60.3 us
  waiting for transfers between devices  33.8 us (56%)
  starting transfers between devices  10.9 us (18%)
  Pallas kernels  9.92 us (16%)
  local copies, waits for them, and re-layouts  4.66 us (8%)
  other arithmetic  0.84 us (1%)
    ppermute x7, waiting for transfers between devices, send(): lax.ppermute(array, 'blk', [(i, i ^ (odd if i % 2 else even)) for i in ra...  33.8 us
    ppermute x7, starting transfers between devices, send(): lax.ppermute(array, 'blk', [(i, i ^ (odd if i % 2 else even)) for i in ra...  10.9 us
    pallas_call x2, Pallas kernels, bloch(): pl.pallas_call(bloch_kernel, grid_spec=pltpu.PrefetchScalarGridSpec(num_s...  5.06 us
    pallas_call x2, Pallas kernels, partial_sums(): pl.pallas_call(partial_kernel, grid_spec=pltpu.PrefetchScalarGridSpec(num...  4.86 us
    unnamed x12, local copies, waits for them, and re-layouts  4.59 us
  transfers between devices with their start and end apart: 7, of which 5 were waited for; matrix products, arithmetic and copies ran while one was open for 1% of the time, Pallas kernels for 8%

profile of v1, /device:TPU:0, one launch (start us, length us, event | category | flops | bytes accessed | tf_op | source)
XLA Modules:
  0.0 60.3 jit_solution(14968631336407105807)
XLA Ops:
  0.0 3.2 %copy-done = bf16[4,2,16,30720]{3,2,1,0:T(8,128)(2,1)S(1)} copy-done((bf16[4,2,16,30720]{3,2,1,0:T(8,128)(2,1)S(1)}, bf16[4,2,16,30720]{3,2,1,0:T(8,128)(2,1)}, u32[]{:S(2)}) %copy-start) | copy-done | bytes 7864344
  3.2 0.7 %copy-done.1 = s32[3,4]{1,0:T(4,128)S(1)} copy-done((s32[3,4]{1,0:T(4,128)S(1)}, s32[3,4]{1,0:T(4,128)}, u32[]{:S(2)}) %copy-start.1) | copy-done | bytes 72
  3.9 0.7 %copy-done.2 = f32[3]{0:T(128)S(1)} copy-done((f32[3]{0:T(128)S(1)}, f32[3]{0:T(128)}, u32[]{:S(2)}) %copy-start.2) | copy-done | bytes 36
  4.6 2.4 %shard_map.65 = bf16[4,32,3840]{2,1,0:T(8,128)(2,1)S(1)} custom-call(s32[1]{0:T(128)} %bitcast.me_ref, f32[3]{0:T(128)S(1)} %copy-done.2, s32[3,4]{1,0:T(4,128)S(1)} %copy-done.1, bf16[4,2,16,30720]{3,2,1,0:T(8,128)(2,1)S(1)} %copy-done), custom_call_target="tpu_custom_call" | custom-call | flops 125829120 | bytes 3932160 | tf_op jit(solution)/shard_map/pallas_call | solution.py:55
  7.0 0.5 collective-permute-start
  7.5 2.4 %shard_map.64 = f32[4,32,3840]{2,1,0:T(8,128)S(1)} custom-call(s32[1]{0:T(128)} %bitcast.me_ref, f32[3]{0:T(128)S(1)} %copy-done.2, s32[3,4]{1,0:T(4,128)S(1)} %copy-done.1, bf16[4,2,16,30720]{3,2,1,0:T(8,128)(2,1)S(1)} %copy-done), custom_call_target="tpu_custom_call" | custom-call | flops 125829120 | bytes 3932160 | tf_op jit(solution)/shard_map/pallas_call | solution.py:55
  10.0 0.0 collective-permute-done
  10.0 0.1 fusion
  10.1 0.0 copy-start.3
  10.1 0.0 copy-start.4
  10.2 0.0 copy-start.5
  10.2 2.7 %collective-permute-start.1 = (bf16[2,32,3840]{2,1,0:T(8,128)(2,1)S(1)}, bf16[2,32,3840]{2,1,0:T(8,128)(2,1)S(1)}, u32[]{:S(2)}, u32[]{:S(2)}) collective-permute-start(bf16[2,32,3840]{2,1,0:T(8,128)(2,1)S(1)} %get-tuple-element.5), channel_id=1, source_target_pairs={{0,2},{1,5},{2,0},{3,7},{4,6},{5,1},{6,4},{7,3},{8,10},{9,13},{10,... | collective-permute-start | bytes 1474568 | tf_op jit(solution)/shard_map/ppermute | solution.py:137
  12.8 6.8 %collective-permute-done.1 = bf16[2,32,3840]{2,1,0:T(8,128)(2,1)S(1)} collective-permute-done((bf16[2,32,3840]{2,1,0:T(8,128)(2,1)S(1)}, bf16[2,32,3840]{2,1,0:T(8,128)(2,1)S(1)}, u32[]{:S(2)}, u32[]{:S(2)}) %collective-permute-start.1) | collective-permute-done | bytes 491552 | tf_op jit(solution)/shard_map/ppermute | solution.py:137
  19.7 0.1 fusion.1
  19.7 2.2 %collective-permute-start.2 = (bf16[1,32,3840]{2,1,0:T(8,128)(2,1)S(1)}, bf16[1,32,3840]{2,1,0:T(8,128)(2,1)S(1)}, u32[]{:S(2)}, u32[]{:S(2)}) collective-permute-start(bf16[1,32,3840]{2,1,0:T(8,128)(2,1)S(1)} %fusion.1), channel_id=1, source_target_pairs={{0,4},{1,3},{2,6},{3,1},{4,0},{5,7},{6,2},{7,5},{8,12},{9,11},{10,... | collective-permute-start | bytes 737288 | tf_op jit(solution)/shard_map/ppermute | solution.py:137
  21.9 4.2 %collective-permute-done.2 = bf16[1,32,3840]{2,1,0:T(8,128)(2,1)S(1)} collective-permute-done((bf16[1,32,3840]{2,1,0:T(8,128)(2,1)S(1)}, bf16[1,32,3840]{2,1,0:T(8,128)(2,1)S(1)}, u32[]{:S(2)}, u32[]{:S(2)}) %collective-permute-start.2) | collective-permute-done | bytes 245792 | tf_op jit(solution)/shard_map/ppermute | solution.py:137
  26.1 0.1 fusion.3
  26.2 3.1 %collective-permute-start.3 = (bf16[1,32,3840]{2,1,0:T(8,128)(2,1)S(1)}, bf16[1,32,3840]{2,1,0:T(8,128)(2,1)S(1)}, u32[]{:S(2)}, u32[]{:S(2)}) collective-permute-start(bf16[1,32,3840]{2,1,0:T(8,128)(2,1)S(1)} %fusion.3), channel_id=1, source_target_pairs={{0,8},{1,9},{2,10},{3,11},{4,12},{5,13},{6,14},{7,15},{8,0},{9,1},... | collective-permute-start | bytes 737288 | tf_op jit(solution)/shard_map/ppermute | solution.py:137
  29.3 10.1 %collective-permute-done.3 = bf16[1,32,3840]{2,1,0:T(8,128)(2,1)S(1)} collective-permute-done((bf16[1,32,3840]{2,1,0:T(8,128)(2,1)S(1)}, bf16[1,32,3840]{2,1,0:T(8,128)(2,1)S(1)}, u32[]{:S(2)}, u32[]{:S(2)}) %collective-permute-start.3) | collective-permute-done | bytes 245792 | tf_op jit(solution)/shard_map/ppermute | solution.py:137
  39.3 0.1 add_convert_fusion
  39.5 0.8 %collective-permute-start.4 = (bf16[1,32,3840]{2,1,0:T(8,128)(2,1)S(1)}, bf16[1,32,3840]{2,1,0:T(8,128)(2,1)S(1)}, u32[]{:S(2)}, u32[]{:S(2)}) collective-permute-start(bf16[1,32,3840]{2,1,0:T(8,128)(2,1)S(1)} %add_convert_fusion), channel_id=1, source_target_pairs={{0,4},{1,3},{2,6},{3,1},{4,0},{5,7},{6,2},{7,5},{8,12},{9,11},{10,... | collective-permute-start | bytes 737288 | tf_op jit(solution)/shard_map/ppermute | solution.py:137
  40.2 5.5 %collective-permute-done.4 = bf16[1,32,3840]{2,1,0:T(8,128)(2,1)S(1)} collective-permute-done((bf16[1,32,3840]{2,1,0:T(8,128)(2,1)S(1)}, bf16[1,32,3840]{2,1,0:T(8,128)(2,1)S(1)}, u32[]{:S(2)}, u32[]{:S(2)}) %collective-permute-start.4) | collective-permute-done | bytes 245792 | tf_op jit(solution)/shard_map/ppermute | solution.py:137
  45.8 1.6 %collective-permute-start.5 = (bf16[2,32,3840]{2,1,0:T(8,128)(2,1)S(1)}, bf16[2,32,3840]{2,1,0:T(8,128)(2,1)S(1)}, u32[]{:S(2)}, u32[]{:S(2)}) collective-permute-start(bf16[2,32,3840]{2,1,0:T(8,128)(2,1)S(1)} %pad_maximum_fusion.1), channel_id=1, source_target_pairs={{0,2},{1,5},{2,0},{3,7},{4,6},{5,1},{6,4},{7,3},{8,10},{9,13},{10,... | collective-permute-start | bytes 1474568 | tf_op jit(solution)/shard_map/ppermute | solution.py:137
  47.4 7.3 %collective-permute-done.5 = bf16[2,32,3840]{2,1,0:T(8,128)(2,1)S(1)} collective-permute-done((bf16[2,32,3840]{2,1,0:T(8,128)(2,1)S(1)}, bf16[2,32,3840]{2,1,0:T(8,128)(2,1)S(1)}, u32[]{:S(2)}, u32[]{:S(2)}) %collective-permute-start.5) | collective-permute-done | bytes 491552 | tf_op jit(solution)/shard_map/ppermute | solution.py:137
  54.7 0.1 pad_maximum_fusion.refs_0_
  54.8 0.1 collective-permute-start.6
  54.9 0.1 multiply_reduce_fusion
  55.0 0.1 copy.11
  55.1 0.1 negate_convert_fusion
  55.1 0.1 maximum_maximum_fusion.qmat_ref
  55.2 2.6 %shard_map.66.refs_1_ = bf16[2,32,30720]{2,1,0:T(8,128)(2,1)} custom-call(s32[1]{0:T(128)} %bitcast.me_ref, bf16[64,32]{1,0:T(8,128)(2,1)S(1)} %maximum_maximum_fusion.qmat_ref, bf16[4,32,3840]{2,1,0:T(8,128)(2,1)S(1)} %pad_maximum_fusion.refs_0_), custom_call_target="tpu_custom_call" | custom-call | flops 62914560 | bytes 1966080 | tf_op jit(solution)/shard_map/pallas_call | solution.py:110
  57.8 2.5 %shard_map.67 = bf16[2,32,30720]{2,1,0:T(8,128)(2,1)} custom-call(s32[1]{0:T(128)} %bitcast.me_ref, bf16[64,32]{1,0:T(8,128)(2,1)S(1)} %maximum_maximum_fusion.qmat_ref, bf16[4,32,3840]{2,1,0:T(8,128)(2,1)S(1)} %collective-permute-done.6.refs_0_, bf16[2,32,30720]{2,1,0:T(8,128)(2,1)} %shard_map.66.refs_1_), custom_call_target="tpu_custom_call", output_to_operand_aliasing={{}: (3, {})} | custom-call | flops 62914560 | bytes 1966080 | tf_op jit(solution)/shard_map/pallas_call | solution.py:110
  (10 shorter events, 0.1 us)
Async XLA Ops:
  0.0 3.2 %copy-start = (bf16[4,2,16,30720]{3,2,1,0:T(8,128)(2,1)S(1)}, bf16[4,2,16,30720]{3,2,1,0:T(8,128)(2,1)}, u32[]{:S(2)}) copy-start(bf16[4,2,16,30720]{3,2,1,0:T(8,128)(2,1)} %couplings_ref.3) | copy-start | bytes 23592964
  3.2 0.7 %copy-start.1 = (s32[3,4]{1,0:T(4,128)S(1)}, s32[3,4]{1,0:T(4,128)}, u32[]{:S(2)}) copy-start(s32[3,4]{1,0:T(4,128)} %elec_ref.3) | copy-start | bytes 148
  3.9 0.7 %copy-start.2 = (f32[3]{0:T(128)S(1)}, f32[3]{0:T(128)}, u32[]{:S(2)}) copy-start(f32[3]{0:T(128)} %k_ref.3) | copy-start | bytes 40
  7.0 3.0 %collective-permute-start = (bf16[4,32,3840]{2,1,0:T(8,128)(2,1)S(1)}, bf16[4,32,3840]{2,1,0:T(8,128)(2,1)S(1)}, u32[]{:S(2)}, u32[]{:S(2)}) collective-permute-start(bf16[4,32,3840]{2,1,0:T(8,128)(2,1)S(1)} %shard_map.65), channel_id=1, source_target_pairs={{0,1},{1,0},{2,3},{3,2},{4,5},{5,4},{6,7},{7,6},{8,9},{9,8},{10,11... | collective-permute-start | bytes 2949128 | tf_op jit(solution)/shard_map/ppermute | solution.py:137
  10.1 44.7 %copy-start.3 = (s32[3,16]{1,0:T(4,128)S(1)}, s32[3,16]{1,0:T(4,128)}, u32[]{:S(2)}) copy-start(s32[3,16]{1,0:T(4,128)} %param.8) | copy-start | bytes 580
  10.1 44.7 %copy-start.4 = (s32[3,32]{1,0:T(4,128)S(1)}, s32[3,32]{1,0:T(4,128)}, u32[]{:S(2)}) copy-start(s32[3,32]{1,0:T(4,128)} %param.11) | copy-start | bytes 1156
  10.2 44.9 %copy-start.5 = (s32[16]{0:T(128)S(1)}, s32[16]{0:T(128)}, u32[]{:S(2)}) copy-start(s32[16]{0:T(128)} %param.9) | copy-start | bytes 196
  10.2 9.5 %collective-permute-start.1 = (bf16[2,32,3840]{2,1,0:T(8,128)(2,1)S(1)}, bf16[2,32,3840]{2,1,0:T(8,128)(2,1)S(1)}, u32[]{:S(2)}, u32[]{:S(2)}) collective-permute-start(bf16[2,32,3840]{2,1,0:T(8,128)(2,1)S(1)} %get-tuple-element.5), channel_id=1, source_target_pairs={{0,2},{1,5},{2,0},{3,7},{4,6},{5,1},{6,4},{7,3},{8,10},{9,13},{10,... | collective-permute-start | bytes 1474568 | tf_op jit(solution)/shard_map/ppermute | solution.py:137
  19.7 6.3 %collective-permute-start.2 = (bf16[1,32,3840]{2,1,0:T(8,128)(2,1)S(1)}, bf16[1,32,3840]{2,1,0:T(8,128)(2,1)S(1)}, u32[]{:S(2)}, u32[]{:S(2)}) collective-permute-start(bf16[1,32,3840]{2,1,0:T(8,128)(2,1)S(1)} %fusion.1), channel_id=1, source_target_pairs={{0,4},{1,3},{2,6},{3,1},{4,0},{5,7},{6,2},{7,5},{8,12},{9,11},{10,... | collective-permute-start | bytes 737288 | tf_op jit(solution)/shard_map/ppermute | solution.py:137
  26.2 13.2 %collective-permute-start.3 = (bf16[1,32,3840]{2,1,0:T(8,128)(2,1)S(1)}, bf16[1,32,3840]{2,1,0:T(8,128)(2,1)S(1)}, u32[]{:S(2)}, u32[]{:S(2)}) collective-permute-start(bf16[1,32,3840]{2,1,0:T(8,128)(2,1)S(1)} %fusion.3), channel_id=1, source_target_pairs={{0,8},{1,9},{2,10},{3,11},{4,12},{5,13},{6,14},{7,15},{8,0},{9,1},... | collective-permute-start | bytes 737288 | tf_op jit(solution)/shard_map/ppermute | solution.py:137
  39.5 6.3 %collective-permute-start.4 = (bf16[1,32,3840]{2,1,0:T(8,128)(2,1)S(1)}, bf16[1,32,3840]{2,1,0:T(8,128)(2,1)S(1)}, u32[]{:S(2)}, u32[]{:S(2)}) collective-permute-start(bf16[1,32,3840]{2,1,0:T(8,128)(2,1)S(1)} %add_convert_fusion), channel_id=1, source_target_pairs={{0,4},{1,3},{2,6},{3,1},{4,0},{5,7},{6,2},{7,5},{8,12},{9,11},{10,... | collective-permute-start | bytes 737288 | tf_op jit(solution)/shard_map/ppermute | solution.py:137
  45.8 8.9 %collective-permute-start.5 = (bf16[2,32,3840]{2,1,0:T(8,128)(2,1)S(1)}, bf16[2,32,3840]{2,1,0:T(8,128)(2,1)S(1)}, u32[]{:S(2)}, u32[]{:S(2)}) collective-permute-start(bf16[2,32,3840]{2,1,0:T(8,128)(2,1)S(1)} %pad_maximum_fusion.1), channel_id=1, source_target_pairs={{0,2},{1,5},{2,0},{3,7},{4,6},{5,1},{6,4},{7,3},{8,10},{9,13},{10,... | collective-permute-start | bytes 1474568 | tf_op jit(solution)/shard_map/ppermute | solution.py:137
  54.8 3.0 %collective-permute-start.6 = (bf16[4,32,3840]{2,1,0:T(8,128)(2,1)S(1)}, bf16[4,32,3840]{2,1,0:T(8,128)(2,1)S(1)}, u32[]{:S(2)}, u32[]{:S(2)}) collective-permute-start(bf16[4,32,3840]{2,1,0:T(8,128)(2,1)S(1)} %pad_maximum_fusion.refs_0_), channel_id=1, source_target_pairs={{0,1},{1,0},{2,3},{3,2},{4,5},{5,4},{6,7},{7,6},{8,9},{9,8},{10,11... | collective-permute-start | bytes 2949128 | tf_op jit(solution)/shard_map/ppermute | solution.py:137

commit v2 on v0

v2 whole, which is shorter than its diff:
```python
import math

import jax
import jax.numpy as jnp
from jax import lax
from jax.experimental import pallas as pl
from jax.experimental.pallas import tpu as pltpu
from jax.sharding import PartitionSpec as P

NG = 16
STREAMS = 1
HALF = 4
BLOCKS = 2 * HALF * STREAMS
VMEM_LIMIT = 24 * 2**20


def block_of(me, position):
    core = me % 2
    first, second = (me // 2) % 2, (me // 4) % 2
    flip = 7 - position
    owner = (core + flip // 4) % 2
    high = jnp.where(owner == 0, first, second)
    low = jnp.where(owner == 0, second, first)
    high = (high + (flip // 2) % 2) % 2
    low = (low + flip % 2) % 2
    return owner * 4 + high * 2 + low


def columns_at(me, position, stream, columns):
    start = (stream * 2 * HALF + block_of(me, position)) * columns
    return pl.ds(pl.multiple_of(start, 128), columns)


def partial_kernel(offset, stream, me_ref, k_hbm, elec_hbm, couplings_hbm, out_ref, k_buf, elec_buf, table, small, sems):
    blocks, rows, columns = out_ref.shape
    re_here, parts, slab = couplings_hbm.shape[:3]
    depth = re_here * parts * slab
    small_copies = [
        pltpu.make_async_copy(k_hbm, k_buf, small.at[0]),
        pltpu.make_async_copy(elec_hbm, elec_buf, small.at[1]),
    ]
    for copy in small_copies:
        copy.start()
    copies = []
    for j in range(blocks):
        place = columns_at(me_ref[0], offset + j, stream, columns)
        copies.append(pltpu.make_async_copy(couplings_hbm.at[:, :, :, place], table.at[j], sems.at[j]))
        copies[-1].start()
    for copy in small_copies:
        copy.wait()

    terms = [k_buf[:, d : d + 1] * elec_buf[d : d + 1, :].astype(jnp.float32) for d in range(3)]
    theta_here = 2.0 * math.pi * (terms[0] + terms[1] + terms[2])
    vector = lax.broadcasted_iota(jnp.int32, (8, depth), 1) // (parts * slab)
    theta = jnp.zeros((8, depth), jnp.float32)
    for e in range(re_here):
        theta = jnp.where(vector == e, theta_here[:, e : e + 1], theta)
    cos = jnp.cos(theta)[:1]
    sin = jnp.sin(theta)[:1]
    row = lax.broadcasted_iota(jnp.int32, (rows, depth), 0)
    col = lax.broadcasted_iota(jnp.int32, (rows, depth), 1)
    out_part, in_part = row // slab, (col // slab) % parts
    value = jnp.where(out_part == in_part, cos, jnp.where(out_part == 1, sin, -sin))
    kmat = jnp.where(row % slab == col % slab, value, 0.0).astype(table.dtype)

    for j in range(blocks):
        copies[j].wait()
        flat = table[j].reshape(depth, columns)
        out_ref[j] = jnp.dot(kmat, flat, preferred_element_type=jnp.float32).astype(out_ref.dtype)


def partial_sums(me, k_point, elec_vectors, couplings, offset, stream, dtype):
    re_here, parts, slab, width = couplings.shape
    columns = width // BLOCKS
    hbm = pl.BlockSpec(memory_space=pltpu.HBM)
    k_row = k_point.reshape(1, 3)
    return pl.pallas_call(
        lambda *refs: partial_kernel(offset, stream, *refs),
        in_specs=[pl.BlockSpec(memory_space=pltpu.SMEM), hbm, hbm, hbm],
        out_specs=pl.BlockSpec(memory_space=pltpu.VMEM),
        out_shape=jax.ShapeDtypeStruct((HALF, parts * slab, columns), dtype),
        scratch_shapes=[
            pltpu.VMEM((1, 3), jnp.float32),
            pltpu.VMEM(elec_vectors.shape, jnp.int32),
            pltpu.VMEM((HALF, re_here, parts, slab, columns), couplings.dtype),
            pltpu.SemaphoreType.DMA((2,)),
            pltpu.SemaphoreType.DMA((HALF,)),
        ],
        compiler_params=pltpu.CompilerParams(vmem_limit_bytes=VMEM_LIMIT),
        cost_estimate=pl.CostEstimate(
            flops=2 * (parts * slab) ** 2 * re_here * HALF * columns,
            bytes_accessed=2 * parts * slab * re_here * HALF * columns,
            transcendentals=0,
        ),
    )(
        me,
        pltpu.with_memory_space_constraint(k_row, pltpu.HBM),
        pltpu.with_memory_space_constraint(elec_vectors, pltpu.HBM),
        pltpu.with_memory_space_constraint(couplings, pltpu.HBM),
    )


def q_matrix(q_index, phon_vectors, degeneracy):
    dots = jnp.sum(q_index[:, :, None] * phon_vectors[:, None, :], axis=0)
    wound = jnp.mod(dots, NG).astype(jnp.float32)
    angle = 2.0 * math.pi * wound / NG
    weight = 1.0 / degeneracy.astype(jnp.float32)
    qcos = jnp.cos(angle) * weight[None, :]
    qsin = jnp.sin(angle) * weight[None, :]
    top = jnp.concatenate([qcos, -qsin], axis=1)
    bottom = jnp.concatenate([qsin, qcos], axis=1)
    return jnp.concatenate([top, bottom], axis=0).astype(jnp.bfloat16)


def bloch_kernel(offset, stream, me_ref, qmat_ref, slab_ref, *refs):
    out_hbm, buffer, sems = refs[-3:]
    blocks, rows, columns = slab_ref.shape
    points = out_hbm.shape[1]
    copies = []
    for j in range(blocks):
        result = jnp.dot(qmat_ref[...], slab_ref[j], preferred_element_type=jnp.float32).astype(buffer.dtype)
        buffer[j, 0] = result[:points]
        buffer[j, 1] = result[points:]
        place = columns_at(me_ref[0], offset + j, stream, columns)
        copies.append(pltpu.make_async_copy(buffer.at[j], out_hbm.at[:, :, place], sems.at[j]))
        copies[-1].start()
    for copy in copies:
        copy.wait()


def bloch(me, qmat, slab, offset, stream, width, out=None):
    blocks, rows, columns = slab.shape
    points = qmat.shape[0] // 2
    vmem, hbm = pl.BlockSpec(memory_space=pltpu.VMEM), pl.BlockSpec(memory_space=pltpu.HBM)
    before = () if out is None else (out,)
    return pl.pallas_call(
        lambda *refs: bloch_kernel(offset, stream, *refs),
        in_specs=[pl.BlockSpec(memory_space=pltpu.SMEM), vmem, vmem] + [hbm] * len(before),
        out_specs=hbm,
        out_shape=jax.ShapeDtypeStruct((2, points, width), jnp.bfloat16),
        scratch_shapes=[
            pltpu.VMEM((blocks, 2, points, columns), jnp.bfloat16),
            pltpu.SemaphoreType.DMA((blocks,)),
        ],
        input_output_aliases={3: 0} if before else {},
        compiler_params=pltpu.CompilerParams(vmem_limit_bytes=VMEM_LIMIT),
        cost_estimate=pl.CostEstimate(
            flops=4 * points * rows * blocks * columns,
            bytes_accessed=4 * points * blocks * columns,
            transcendentals=0,
        ),
    )(me, qmat, slab, *before)


def on_device(devices, couplings, elec_vectors, phon_vectors, degeneracy, k_point, q_index):
    width = couplings.shape[3]
    wire = jnp.bfloat16
    me = lax.axis_index("blk").astype(jnp.int32).reshape(1)

    def send(array, even, odd):
        return lax.ppermute(array, "blk", [(i, i ^ (odd if i % 2 else even)) for i in range(devices)])

    qmat = q_matrix(q_index, phon_vectors, degeneracy)
    out = None
    for stream in range(STREAMS):
        theirs = partial_sums(me, k_point, elec_vectors, couplings, 0, stream, wire)
        got = send(theirs, 1, 1)
        own = partial_sums(me, k_point, elec_vectors, couplings, HALF, stream, jnp.float32)

        first = send((own[:2] + got[:2].astype(jnp.float32)).astype(wire), 2, 4)
        own = own[2:] + got[2:].astype(jnp.float32)
        second = send((own[:1] + first[:1].astype(jnp.float32)).astype(wire), 4, 2)
        own = own[1:] + first[1:].astype(jnp.float32) + second.astype(jnp.float32)
        step = 8
        while step < devices:
            own = own + send(own.astype(wire), step, step).astype(jnp.float32)
            step *= 2
        block = own.astype(wire)
        pair = jnp.concatenate([send(block, 4, 2), block])
        quad = jnp.concatenate([send(pair, 2, 4), pair])
        rest = send(quad, 1, 1)
        out = bloch(me, qmat, quad, HALF, stream, width, out)
        out = bloch(me, qmat, rest, 0, stream, width, out)
    return out


def solution(mesh):
    placed = (
        P("blk", None, "grp", None),
        P(None, "blk"),
        P(None, "grp"),
        P("grp"),
        P("grp"),
        P(None, "blk"),
    )
    devices = mesh.shape["blk"]
    return jax.shard_map(
        lambda *arrays: on_device(devices, *arrays),
        mesh=mesh,
        in_specs=placed,
        out_specs=P(None, ("grp", "blk"), None),
        check_vma=False,
    )
```

time: 114 us -> 55.6 us (0.49)
  blocking collectives: 93.1 us -> 0 us
  waiting for transfers between devices: 0 us -> 34.3 us
  matrix products: 17.8 us -> 0 us
  starting transfers between devices: 0 us -> 10.8 us
  Pallas kernels: 0 us -> 9.22 us
    psum x1 -> x0, blocking collectives: 93.1 us -> none  [on_device(): summed = lax.psum(partial_slab, 'blk').astype(jnp.bfloat16)]
    ppermute x0 -> x7, waiting for transfers between devices: none -> 34.3 us  [send(): lax.ppermute(array, 'blk', [(i, i ^ (odd if i % 2 else even)) for i in ra...]
    dot_general x2 -> x0, matrix products: 17.8 us -> none  [the longest x1 14.6 us: on_device(): jnp.dot(kmat, flat, preferred_element_type=jnp.float32)]
    ppermute x0 -> x7, starting transfers between devices: none -> 10.8 us  [send(): lax.ppermute(array, 'blk', [(i, i ^ (odd if i % 2 else even)) for i in ra...]
    pallas_call x0 -> x4, Pallas kernels: none -> 9.22 us  [the longest x2 6.07 us: partial_sums(): pl.pallas_call(lambda *refs: partial_kernel(offset, stream, *refs), in_sp...]
  transfers between devices with their start and end apart: 0 -> 7, of which waited for: 0 -> 6; matrix products, arithmetic and copies ran while one was open for 0% -> 1% of each run, Pallas kernels for 0% -> 9%
where the time goes in v2:
time: 55.6 us; the launch traced here: 55.4 us
  waiting for transfers between devices  34.3 us (62%)
  starting transfers between devices  10.8 us (19%)
  Pallas kernels  9.22 us (17%)
  other arithmetic  0.84 us (2%)
    ppermute x7, waiting for transfers between devices, send(): lax.ppermute(array, 'blk', [(i, i ^ (odd if i % 2 else even)) for i in ra...  34.3 us
    ppermute x7, starting transfers between devices, send(): lax.ppermute(array, 'blk', [(i, i ^ (odd if i % 2 else even)) for i in ra...  10.8 us
    pallas_call x2, Pallas kernels, partial_sums(): pl.pallas_call(lambda *refs: partial_kernel(offset, stream, *refs), in_sp...  6.07 us
    pallas_call x2, Pallas kernels, bloch(): pl.pallas_call(lambda *refs: bloch_kernel(offset, stream, *refs), in_spec...  3.16 us
  transfers between devices with their start and end apart: 7, of which 6 were waited for; matrix products, arithmetic and copies ran while one was open for 1% of the time, Pallas kernels for 9%

profile of v2, /device:TPU:0, one launch (start us, length us, event | category | flops | bytes accessed | tf_op | source)
XLA Modules:
  0.0 55.4 jit_solution(11150580819612002777)
XLA Ops:
  0.0 2.9 %shard_map.65 = bf16[4,32,3840]{2,1,0:T(8,128)(2,1)S(1)} custom-call(s32[1]{0:T(128)} %bitcast.refs_0_, f32[1,3]{1,0:T(1,128)} %bitcast.2, s32[3,4]{1,0:T(4,128)} %refs_2_.3, bf16[4,2,16,30720]{3,2,1,0:T(8,128)(2,1)} %refs_3_.3), custom_call_target="tpu_custom_call" | custom-call | flops 125829120 | bytes 3932160 | tf_op jit(solution)/shard_map/pallas_call | solution.py:77
  2.9 0.7 %collective-permute-start = (bf16[4,32,3840]{2,1,0:T(8,128)(2,1)S(1)}, bf16[4,32,3840]{2,1,0:T(8,128)(2,1)S(1)}, u32[]{:S(2)}, u32[]{:S(2)}) collective-permute-start(bf16[4,32,3840]{2,1,0:T(8,128)(2,1)S(1)} %shard_map.65), channel_id=1, source_target_pairs={{0,1},{1,0},{2,3},{3,2},{4,5},{5,4},{6,7},{7,6},{8,9},{9,8},{10,11... | collective-permute-start | bytes 2949128 | tf_op jit(solution)/shard_map/ppermute | solution.py:161
  3.7 3.1 %shard_map.64 = f32[4,32,3840]{2,1,0:T(8,128)S(1)} custom-call(s32[1]{0:T(128)} %bitcast.refs_0_, f32[1,3]{1,0:T(1,128)} %bitcast.3, s32[3,4]{1,0:T(4,128)} %refs_2_.3, bf16[4,2,16,30720]{3,2,1,0:T(8,128)(2,1)} %refs_3_.3), custom_call_target="tpu_custom_call" | custom-call | flops 125829120 | bytes 3932160 | tf_op jit(solution)/shard_map/pallas_call | solution.py:77
  6.8 0.0 collective-permute-done
  6.8 0.1 fusion
  7.0 0.0 copy-start
  7.0 0.0 copy-start.1
  7.0 0.0 copy-start.2
  7.0 2.3 %collective-permute-start.1 = (bf16[2,32,3840]{2,1,0:T(8,128)(2,1)S(1)}, bf16[2,32,3840]{2,1,0:T(8,128)(2,1)S(1)}, u32[]{:S(2)}, u32[]{:S(2)}) collective-permute-start(bf16[2,32,3840]{2,1,0:T(8,128)(2,1)S(1)} %get-tuple-element.5), channel_id=1, source_target_pairs={{0,2},{1,5},{2,0},{3,7},{4,6},{5,1},{6,4},{7,3},{8,10},{9,13},{10,... | collective-permute-start | bytes 1474568 | tf_op jit(solution)/shard_map/ppermute | solution.py:161
  9.3 6.8 %collective-permute-done.1 = bf16[2,32,3840]{2,1,0:T(8,128)(2,1)S(1)} collective-permute-done((bf16[2,32,3840]{2,1,0:T(8,128)(2,1)S(1)}, bf16[2,32,3840]{2,1,0:T(8,128)(2,1)S(1)}, u32[]{:S(2)}, u32[]{:S(2)}) %collective-permute-start.1) | collective-permute-done | bytes 491552 | tf_op jit(solution)/shard_map/ppermute | solution.py:161
  16.1 0.1 fusion.1
  16.1 2.2 %collective-permute-start.2 = (bf16[1,32,3840]{2,1,0:T(8,128)(2,1)S(1)}, bf16[1,32,3840]{2,1,0:T(8,128)(2,1)S(1)}, u32[]{:S(2)}, u32[]{:S(2)}) collective-permute-start(bf16[1,32,3840]{2,1,0:T(8,128)(2,1)S(1)} %fusion.1), channel_id=1, source_target_pairs={{0,4},{1,3},{2,6},{3,1},{4,0},{5,7},{6,2},{7,5},{8,12},{9,11},{10,... | collective-permute-start | bytes 737288 | tf_op jit(solution)/shard_map/ppermute | solution.py:161
  18.3 4.2 %collective-permute-done.2 = bf16[1,32,3840]{2,1,0:T(8,128)(2,1)S(1)} collective-permute-done((bf16[1,32,3840]{2,1,0:T(8,128)(2,1)S(1)}, bf16[1,32,3840]{2,1,0:T(8,128)(2,1)S(1)}, u32[]{:S(2)}, u32[]{:S(2)}) %collective-permute-start.2) | collective-permute-done | bytes 245792 | tf_op jit(solution)/shard_map/ppermute | solution.py:161
  22.5 0.1 fusion.3
  22.6 3.2 %collective-permute-start.3 = (bf16[1,32,3840]{2,1,0:T(8,128)(2,1)S(1)}, bf16[1,32,3840]{2,1,0:T(8,128)(2,1)S(1)}, u32[]{:S(2)}, u32[]{:S(2)}) collective-permute-start(bf16[1,32,3840]{2,1,0:T(8,128)(2,1)S(1)} %fusion.3), channel_id=1, source_target_pairs={{0,8},{1,9},{2,10},{3,11},{4,12},{5,13},{6,14},{7,15},{8,0},{9,1},... | collective-permute-start | bytes 737288 | tf_op jit(solution)/shard_map/ppermute | solution.py:161
  25.8 10.0 %collective-permute-done.3 = bf16[1,32,3840]{2,1,0:T(8,128)(2,1)S(1)} collective-permute-done((bf16[1,32,3840]{2,1,0:T(8,128)(2,1)S(1)}, bf16[1,32,3840]{2,1,0:T(8,128)(2,1)S(1)}, u32[]{:S(2)}, u32[]{:S(2)}) %collective-permute-start.3) | collective-permute-done | bytes 245792 | tf_op jit(solution)/shard_map/ppermute | solution.py:161
  35.8 0.1 add_convert_fusion
  35.9 0.8 %collective-permute-start.4 = (bf16[1,32,3840]{2,1,0:T(8,128)(2,1)S(1)}, bf16[1,32,3840]{2,1,0:T(8,128)(2,1)S(1)}, u32[]{:S(2)}, u32[]{:S(2)}) collective-permute-start(bf16[1,32,3840]{2,1,0:T(8,128)(2,1)S(1)} %add_convert_fusion), channel_id=1, source_target_pairs={{0,4},{1,3},{2,6},{3,1},{4,0},{5,7},{6,2},{7,5},{8,12},{9,11},{10,... | collective-permute-start | bytes 737288 | tf_op jit(solution)/shard_map/ppermute | solution.py:161
  36.7 5.5 %collective-permute-done.4 = bf16[1,32,3840]{2,1,0:T(8,128)(2,1)S(1)} collective-permute-done((bf16[1,32,3840]{2,1,0:T(8,128)(2,1)S(1)}, bf16[1,32,3840]{2,1,0:T(8,128)(2,1)S(1)}, u32[]{:S(2)}, u32[]{:S(2)}) %collective-permute-start.4) | collective-permute-done | bytes 245792 | tf_op jit(solution)/shard_map/ppermute | solution.py:161
  42.2 1.6 %collective-permute-start.5 = (bf16[2,32,3840]{2,1,0:T(8,128)(2,1)S(1)}, bf16[2,32,3840]{2,1,0:T(8,128)(2,1)S(1)}, u32[]{:S(2)}, u32[]{:S(2)}) collective-permute-start(bf16[2,32,3840]{2,1,0:T(8,128)(2,1)S(1)} %pad_maximum_fusion.1), channel_id=1, source_target_pairs={{0,2},{1,5},{2,0},{3,7},{4,6},{5,1},{6,4},{7,3},{8,10},{9,13},{10,... | collective-permute-start | bytes 1474568 | tf_op jit(solution)/shard_map/ppermute | solution.py:161
  43.8 7.3 %collective-permute-done.5 = bf16[2,32,3840]{2,1,0:T(8,128)(2,1)S(1)} collective-permute-done((bf16[2,32,3840]{2,1,0:T(8,128)(2,1)S(1)}, bf16[2,32,3840]{2,1,0:T(8,128)(2,1)S(1)}, u32[]{:S(2)}, u32[]{:S(2)}) %collective-permute-start.5) | collective-permute-done | bytes 491552 | tf_op jit(solution)/shard_map/ppermute | solution.py:161
  51.1 0.1 pad_maximum_fusion.refs_2_
  51.2 0.1 collective-permute-start.6
  51.3 0.0 copy-done
  51.3 0.0 copy-done.1
  51.3 0.1 multiply_reduce_fusion
  51.4 0.1 copy.11
  51.5 0.1 negate_convert_fusion
  51.6 0.1 maximum_maximum_fusion.refs_1_
  51.7 1.6 %shard_map.66.refs_3_ = bf16[2,32,30720]{2,1,0:T(8,128)(2,1)} custom-call(s32[1]{0:T(128)} %bitcast.refs_0_, bf16[64,32]{1,0:T(8,128)(2,1)S(1)} %maximum_maximum_fusion.refs_1_, bf16[4,32,3840]{2,1,0:T(8,128)(2,1)S(1)} %pad_maximum_fusion.refs_2_), custom_call_target="tpu_custom_call" | custom-call | flops 62914560 | bytes 1966080 | tf_op jit(solution)/shard_map/pallas_call | solution.py:136
  53.3 0.6 %collective-permute-done.6.refs_2_ = bf16[4,32,3840]{2,1,0:T(8,128)(2,1)S(1)} collective-permute-done((bf16[4,32,3840]{2,1,0:T(8,128)(2,1)S(1)}, bf16[4,32,3840]{2,1,0:T(8,128)(2,1)S(1)}, u32[]{:S(2)}, u32[]{:S(2)}) %collective-permute-start.6) | collective-permute-done | bytes 983072 | tf_op jit(solution)/shard_map/ppermute | solution.py:161
  53.9 1.6 %shard_map.67 = bf16[2,32,30720]{2,1,0:T(8,128)(2,1)} custom-call(s32[1]{0:T(128)} %bitcast.refs_0_, bf16[64,32]{1,0:T(8,128)(2,1)S(1)} %maximum_maximum_fusion.refs_1_, bf16[4,32,3840]{2,1,0:T(8,128)(2,1)S(1)} %collective-permute-done.6.refs_2_, bf16[2,32,30720]{2,1,0:T(8,128)(2,1)} %shard_map.66.refs_3_), custom_call_target="tpu_custom_call", output_to_operand_aliasing={{}: (3, {})} | custom-call | flops 62914560 | bytes 1966080 | tf_op jit(solution)/shard_map/pallas_call | solution.py:136
  (4 shorter events, 0.1 us)
Async XLA Ops:
  2.9 3.9 %collective-permute-start = (bf16[4,32,3840]{2,1,0:T(8,128)(2,1)S(1)}, bf16[4,32,3840]{2,1,0:T(8,128)(2,1)S(1)}, u32[]{:S(2)}, u32[]{:S(2)}) collective-permute-start(bf16[4,32,3840]{2,1,0:T(8,128)(2,1)S(1)} %shard_map.65), channel_id=1, source_target_pairs={{0,1},{1,0},{2,3},{3,2},{4,5},{5,4},{6,7},{7,6},{8,9},{9,8},{10,11... | collective-permute-start | bytes 2949128 | tf_op jit(solution)/shard_map/ppermute | solution.py:161
  7.0 44.3 %copy-start = (s32[3,16]{1,0:T(4,128)S(1)}, s32[3,16]{1,0:T(4,128)}, u32[]{:S(2)}) copy-start(s32[3,16]{1,0:T(4,128)} %param.8) | copy-start | bytes 580
  7.0 44.3 %copy-start.1 = (s32[3,32]{1,0:T(4,128)S(1)}, s32[3,32]{1,0:T(4,128)}, u32[]{:S(2)}) copy-start(s32[3,32]{1,0:T(4,128)} %param.11) | copy-start | bytes 1156
  7.0 44.5 %copy-start.2 = (s32[16]{0:T(128)S(1)}, s32[16]{0:T(128)}, u32[]{:S(2)}) copy-start(s32[16]{0:T(128)} %param.9) | copy-start | bytes 196
  7.0 9.1 %collective-permute-start.1 = (bf16[2,32,3840]{2,1,0:T(8,128)(2,1)S(1)}, bf16[2,32,3840]{2,1,0:T(8,128)(2,1)S(1)}, u32[]{:S(2)}, u32[]{:S(2)}) collective-permute-start(bf16[2,32,3840]{2,1,0:T(8,128)(2,1)S(1)} %get-tuple-element.5), channel_id=1, source_target_pairs={{0,2},{1,5},{2,0},{3,7},{4,6},{5,1},{6,4},{7,3},{8,10},{9,13},{10,... | collective-permute-start | bytes 1474568 | tf_op jit(solution)/shard_map/ppermute | solution.py:161
  16.1 6.3 %collective-permute-start.2 = (bf16[1,32,3840]{2,1,0:T(8,128)(2,1)S(1)}, bf16[1,32,3840]{2,1,0:T(8,128)(2,1)S(1)}, u32[]{:S(2)}, u32[]{:S(2)}) collective-permute-start(bf16[1,32,3840]{2,1,0:T(8,128)(2,1)S(1)} %fusion.1), channel_id=1, source_target_pairs={{0,4},{1,3},{2,6},{3,1},{4,0},{5,7},{6,2},{7,5},{8,12},{9,11},{10,... | collective-permute-start | bytes 737288 | tf_op jit(solution)/shard_map/ppermute | solution.py:161
  22.6 13.2 %collective-permute-start.3 = (bf16[1,32,3840]{2,1,0:T(8,128)(2,1)S(1)}, bf16[1,32,3840]{2,1,0:T(8,128)(2,1)S(1)}, u32[]{:S(2)}, u32[]{:S(2)}) collective-permute-start(bf16[1,32,3840]{2,1,0:T(8,128)(2,1)S(1)} %fusion.3), channel_id=1, source_target_pairs={{0,8},{1,9},{2,10},{3,11},{4,12},{5,13},{6,14},{7,15},{8,0},{9,1},... | collective-permute-start | bytes 737288 | tf_op jit(solution)/shard_map/ppermute | solution.py:161
  35.9 6.3 %collective-permute-start.4 = (bf16[1,32,3840]{2,1,0:T(8,128)(2,1)S(1)}, bf16[1,32,3840]{2,1,0:T(8,128)(2,1)S(1)}, u32[]{:S(2)}, u32[]{:S(2)}) collective-permute-start(bf16[1,32,3840]{2,1,0:T(8,128)(2,1)S(1)} %add_convert_fusion), channel_id=1, source_target_pairs={{0,4},{1,3},{2,6},{3,1},{4,0},{5,7},{6,2},{7,5},{8,12},{9,11},{10,... | collective-permute-start | bytes 737288 | tf_op jit(solution)/shard_map/ppermute | solution.py:161
  42.2 8.9 %collective-permute-start.5 = (bf16[2,32,3840]{2,1,0:T(8,128)(2,1)S(1)}, bf16[2,32,3840]{2,1,0:T(8,128)(2,1)S(1)}, u32[]{:S(2)}, u32[]{:S(2)}) collective-permute-start(bf16[2,32,3840]{2,1,0:T(8,128)(2,1)S(1)} %pad_maximum_fusion.1), channel_id=1, source_target_pairs={{0,2},{1,5},{2,0},{3,7},{4,6},{5,1},{6,4},{7,3},{8,10},{9,13},{10,... | collective-permute-start | bytes 1474568 | tf_op jit(solution)/shard_map/ppermute | solution.py:161
  51.2 2.6 %collective-permute-start.6 = (bf16[4,32,3840]{2,1,0:T(8,128)(2,1)S(1)}, bf16[4,32,3840]{2,1,0:T(8,128)(2,1)S(1)}, u32[]{:S(2)}, u32[]{:S(2)}) collective-permute-start(bf16[4,32,3840]{2,1,0:T(8,128)(2,1)S(1)} %pad_maximum_fusion.refs_2_), channel_id=1, source_target_pairs={{0,1},{1,0},{2,3},{3,2},{4,5},{5,4},{6,7},{7,6},{8,9},{9,8},{10,11... | collective-permute-start | bytes 2949128 | tf_op jit(solution)/shard_map/ppermute | solution.py:161

commit v3 on v0

v3 whole, which is shorter than its diff:
```python
import math

import jax
import jax.numpy as jnp
from jax import lax
from jax.experimental import pallas as pl
from jax.experimental.pallas import tpu as pltpu
from jax.sharding import PartitionSpec as P

NG = 16
STREAMS = 2
HALF = 4
BLOCKS = 2 * HALF * STREAMS
VMEM_LIMIT = 24 * 2**20


def block_of(me, position):
    flip = 7 - position
    core = (me % 2 + flip // 4) % 2
    first = ((me // 2) % 2 + (flip // 2) % 2) % 2
    second = ((me // 4) % 2 + flip % 2) % 2
    return core * 4 + first * 2 + second


def columns_at(me, position, stream, columns):
    start = (stream * 2 * HALF + block_of(me, position)) * columns
    return pl.ds(pl.multiple_of(start, 128), columns)


def phase_matrix(k_row, elec_vectors, shape, slab, parts):
    rows, depth = shape
    terms = [k_row[:, d : d + 1] * elec_vectors[d : d + 1, :].astype(jnp.float32) for d in range(3)]
    theta_here = 2.0 * math.pi * (terms[0] + terms[1] + terms[2])
    vector = lax.broadcasted_iota(jnp.int32, (8, depth), 1) // (parts * slab)
    theta = jnp.zeros((8, depth), jnp.float32)
    for e in range(elec_vectors.shape[1]):
        theta = jnp.where(vector == e, theta_here[:, e : e + 1], theta)
    cos = jnp.cos(theta)[:1]
    sin = jnp.sin(theta)[:1]
    row = lax.broadcasted_iota(jnp.int32, shape, 0)
    col = lax.broadcasted_iota(jnp.int32, shape, 1)
    out_part, in_part = row // slab, (col // slab) % parts
    value = jnp.where(out_part == in_part, cos, jnp.where(out_part == 1, sin, -sin))
    return jnp.where(row % slab == col % slab, value, 0.0).astype(jnp.bfloat16)


def partial_kernel(pieces, given, me_ref, *refs):
    table, sems = refs[-2:]
    if given:
        kmat_in, couplings_hbm, *outs = refs[:-2]
    else:
        k_hbm, elec_hbm, couplings_hbm, kmat_out, *outs, k_buf, elec_buf, small = refs[:-2]
        small_copies = [
            pltpu.make_async_copy(k_hbm, k_buf, small.at[0]),
            pltpu.make_async_copy(elec_hbm, elec_buf, small.at[1]),
        ]
        for copy in small_copies:
            copy.start()
    re_here, parts, slab = couplings_hbm.shape[:3]
    rows, depth = parts * slab, re_here * parts * slab
    columns = table.shape[-1]
    copies = []
    for offset, stream, _ in pieces:
        for j in range(HALF):
            place = columns_at(me_ref[0], offset + j, stream, columns)
            n = len(copies)
            copies.append(pltpu.make_async_copy(couplings_hbm.at[:, :, :, place], table.at[n], sems.at[n]))
            copies[-1].start()
    if given:
        kmat = kmat_in[...]
    else:
        for copy in small_copies:
            copy.wait()
        kmat = phase_matrix(k_buf[...], elec_buf[...], (rows, depth), slab, parts)
        kmat_out[...] = kmat
    for n, copy in enumerate(copies):
        out_ref = outs[n // HALF]
        copy.wait()
        flat = table[n].reshape(depth, columns)
        out_ref[n % HALF] = jnp.dot(kmat, flat, preferred_element_type=jnp.float32).astype(out_ref.dtype)


def partial_sums(me, phases, couplings, pieces):
    re_here, parts, slab, width = couplings.shape
    columns = width // BLOCKS
    rows, depth = parts * slab, re_here * parts * slab
    hbm, vmem = pl.BlockSpec(memory_space=pltpu.HBM), pl.BlockSpec(memory_space=pltpu.VMEM)
    given = not isinstance(phases, tuple)
    if given:
        operands, specs, first_out, small = [phases], [vmem], [], []
    else:
        k_point, elec_vectors = phases
        operands = [pltpu.with_memory_space_constraint(a, pltpu.HBM) for a in (k_point.reshape(1, 3), elec_vectors)]
        specs, first_out = [hbm, hbm], [jax.ShapeDtypeStruct((rows, depth), jnp.bfloat16)]
        small = [
            pltpu.VMEM((1, 3), jnp.float32),
            pltpu.VMEM(elec_vectors.shape, jnp.int32),
            pltpu.SemaphoreType.DMA((2,)),
        ]
    copies = HALF * len(pieces)
    outs = first_out + [jax.ShapeDtypeStruct((HALF, rows, columns), dtype) for _, _, dtype in pieces]
    return pl.pallas_call(
        lambda *refs: partial_kernel(pieces, given, *refs),
        in_specs=[pl.BlockSpec(memory_space=pltpu.SMEM), *specs, hbm],
        out_specs=[vmem] * len(outs),
        out_shape=outs,
        scratch_shapes=small
        + [
            pltpu.VMEM((copies, re_here, parts, slab, columns), couplings.dtype),
            pltpu.SemaphoreType.DMA((copies,)),
        ],
        compiler_params=pltpu.CompilerParams(vmem_limit_bytes=VMEM_LIMIT),
        cost_estimate=pl.CostEstimate(
            flops=2 * rows * depth * copies * columns,
            bytes_accessed=2 * depth * copies * columns,
            transcendentals=0,
        ),
    )(me, *operands, pltpu.with_memory_space_constraint(couplings, pltpu.HBM))


def q_matrix_kernel(q_ref, phon_ref, degeneracy_ref, out_ref):
    points, slab = out_ref.shape[0] // 2, out_ref.shape[1] // 2
    dots = lax.dot_general(
        q_ref[...].astype(jnp.float32),
        phon_ref[...].astype(jnp.float32),
        (((0,), (0,)), ((), ())),
        preferred_element_type=jnp.float32,
    )
    wound = jnp.bitwise_and(dots.astype(jnp.int32), NG - 1).astype(jnp.float32)
    angle = 2.0 * math.pi * wound / NG
    weight = 1.0 / degeneracy_ref[...].astype(jnp.float32)
    qcos = jnp.cos(angle) * weight
    qsin = jnp.sin(angle) * weight
    out_ref[:points, :slab] = qcos.astype(out_ref.dtype)
    out_ref[:points, slab:] = (-qsin).astype(out_ref.dtype)
    out_ref[points:, :slab] = qsin.astype(out_ref.dtype)
    out_ref[points:, slab:] = qcos.astype(out_ref.dtype)


def q_matrix(q_index, phon_vectors, degeneracy):
    points, slab = q_index.shape[1], phon_vectors.shape[1]
    return pl.pallas_call(
        q_matrix_kernel,
        out_shape=jax.ShapeDtypeStruct((2 * points, 2 * slab), jnp.bfloat16),
        compiler_params=pltpu.CompilerParams(vmem_limit_bytes=VMEM_LIMIT),
    )(q_index, phon_vectors, degeneracy.reshape(1, slab))


def bloch_kernel(pieces, me_ref, qmat_ref, *refs):
    slabs, (out_hbm, buffer, sems) = refs[: len(pieces)], refs[-3:]
    points, columns = out_hbm.shape[1], buffer.shape[-1]
    copies = []
    for (offset, stream), slab_ref in zip(pieces, slabs):
        for j in range(slab_ref.shape[0]):
            n = len(copies)
            result = jnp.dot(qmat_ref[...], slab_ref[j], preferred_element_type=jnp.float32).astype(buffer.dtype)
            buffer[n, 0] = result[:points]
            buffer[n, 1] = result[points:]
            place = columns_at(me_ref[0], offset + j, stream, columns)
            copies.append(pltpu.make_async_copy(buffer.at[n], out_hbm.at[:, :, place], sems.at[n]))
            copies[-1].start()
    for copy in copies:
        copy.wait()


def bloch(me, qmat, pieces, width, out=None):
    slabs = [slab for slab, _, _ in pieces]
    rows, columns = slabs[0].shape[1:]
    blocks = sum(slab.shape[0] for slab in slabs)
    points = qmat.shape[0] // 2
    vmem, hbm = pl.BlockSpec(memory_space=pltpu.VMEM), pl.BlockSpec(memory_space=pltpu.HBM)
    before = () if out is None else (out,)
    places = [(offset, stream) for _, offset, stream in pieces]
    return pl.pallas_call(
        lambda *refs: bloch_kernel(places, *refs),
        in_specs=[pl.BlockSpec(memory_space=pltpu.SMEM), vmem] + [vmem] * len(slabs) + [hbm] * len(before),
        out_specs=hbm,
        out_shape=jax.ShapeDtypeStruct((2, points, width), jnp.bfloat16),
        scratch_shapes=[
            pltpu.VMEM((blocks, 2, points, columns), jnp.bfloat16),
            pltpu.SemaphoreType.DMA((blocks,)),
        ],
        input_output_aliases={2 + len(slabs): 0} if before else {},
        compiler_params=pltpu.CompilerParams(vmem_limit_bytes=VMEM_LIMIT),
        cost_estimate=pl.CostEstimate(
            flops=4 * points * rows * blocks * columns,
            bytes_accessed=4 * points * blocks * columns,
            transcendentals=0,
        ),
    )(me, qmat, *slabs, *before)


def after(value, *others):
    return lax.optimization_barrier((value, *others))[0]


def on_device(devices, couplings, elec_vectors, phon_vectors, degeneracy, k_point, q_index):
    width = couplings.shape[3]
    wire, full = jnp.bfloat16, jnp.float32
    me = lax.axis_index("blk").astype(jnp.int32).reshape(1)

    def send(array, bits, name):
        with jax.named_scope(name):
            return lax.ppermute(array, "blk", [(i, i ^ bits) for i in range(devices)])

    def to_core(array, name):
        return send(array, 1, name)

    def square(arrays, name):
        return [send(a, bits, name) for a, bits in zip(arrays, (2, 4, 6))]

    def added(own, got):
        for array in got:
            own = own + array.astype(full)
        return own

    def far_sum(own, name):
        step = 8
        while step < devices:
            own = own + send(own.astype(wire), step, name).astype(full)
            step *= 2
        return own.astype(wire)

    kmat, p_theirs = partial_sums(me, (k_point, elec_vectors), couplings, [(0, 0, wire)])
    p_got = to_core(p_theirs, "p_core")
    p_own, q_theirs = partial_sums(me, kmat, couplings, [(HALF, 0, full), (0, 1, wire)])
    q_got = to_core(q_theirs, "q_core")
    p_sum = p_own + p_got.astype(full)
    p_first = [p_sum[i : i + 1].astype(wire) for i in (1, 2, 0)]
    p_got = square(p_first, "p_rs")

    (q_own,) = partial_sums(after(me, p_first[0]), kmat, couplings, [(HALF, 1, full)])
    qmat = q_matrix(after(q_index, p_first[0]), phon_vectors, degeneracy)
    q_own = after(q_own, qmat)
    q_sum = q_own + q_got.astype(full)
    q_first = [q_sum[i : i + 1].astype(wire) for i in (1, 2, 0)]
    q_got = square(q_first, "q_rs")

    p_block = far_sum(added(p_sum[3:], p_got), "p_far")
    q_block = far_sum(added(q_sum[3:], q_got), "q_far")

    p_got = square([p_block] * 3, "p_ag")
    q_got = square([q_block] * 3, "q_ag")

    p_quad = jnp.concatenate([p_got[2], p_got[0], p_got[1], p_block])
    out = bloch(me, qmat, [(p_quad, HALF, 0)], width)
    p_rest = to_core(p_quad, "p_core2")

    q_got[0] = after(q_got[0], out)
    q_quad = jnp.concatenate([q_got[2], q_got[0], q_got[1], q_block])
    q_rest = to_core(q_quad, "q_core2")
    out = bloch(me, qmat, [(p_rest, 0, 0), (q_quad, HALF, 1)], width, out)
    return bloch(me, qmat, [(q_rest, 0, 1)], width, out)


def solution(mesh):
    placed = (
        P("blk", None, "grp", None),
        P(None, "blk"),
        P(None, "grp"),
        P("grp"),
        P("grp"),
        P(None, "blk"),
    )
    devices = mesh.shape["blk"]
    return jax.shard_map(
        lambda *arrays: on_device(devices, *arrays),
        mesh=mesh,
        in_specs=placed,
        out_specs=P(None, ("grp", "blk"), None),
        check_vma=False,
    )
```

time: 114 us -> 44.4 us (0.39)
  blocking collectives: 93.1 us -> 0 us
  starting transfers between devices: 0 us -> 21.9 us
  matrix products: 17.8 us -> 0 us
  Pallas kernels: 0 us -> 11.2 us
  waiting for transfers between devices: 0 us -> 10.2 us
    psum x1 -> x0, blocking collectives: 93.1 us -> none  [on_device(): summed = lax.psum(partial_slab, 'blk').astype(jnp.bfloat16)]
    ppermute x0 -> x18, starting transfers between devices: none -> 21.9 us  [send(): return lax.ppermute(array, 'blk', [(i, i ^ bits) for i in range(devices)])]
    dot_general x2 -> x0, matrix products: 17.8 us -> none  [the longest x1 14.6 us: on_device(): jnp.dot(kmat, flat, preferred_element_type=jnp.float32)]
    pallas_call x0 -> x7, Pallas kernels: none -> 11.2 us  [the longest x3 6.97 us: partial_sums(): pl.pallas_call(lambda *refs: partial_kernel(pieces, given, *refs), in_spe...]
    ppermute x0 -> x18, waiting for transfers between devices: none -> 10.2 us  [send(): return lax.ppermute(array, 'blk', [(i, i ^ bits) for i in range(devices)])]
  transfers between devices with their start and end apart: 0 -> 18, of which waited for: 0 -> 9; matrix products, arithmetic and copies ran while one was open for 0% -> 2% of each run, Pallas kernels for 0% -> 17%
where the time goes in v3:
time: 44.4 us; the launch traced here: 44.2 us
  starting transfers between devices  21.9 us (49%)
  Pallas kernels  11.2 us (25%)
  waiting for transfers between devices  10.2 us (23%)
  other arithmetic  0.7 us (2%)
    ppermute x18, starting transfers between devices, send(): return lax.ppermute(array, 'blk', [(i, i ^ bits) for i in range(devices)])  21.9 us
    ppermute x18, waiting for transfers between devices, send(): return lax.ppermute(array, 'blk', [(i, i ^ bits) for i in range(devices)])  10.2 us
    pallas_call x3, Pallas kernels, partial_sums(): pl.pallas_call(lambda *refs: partial_kernel(pieces, given, *refs), in_spe...  6.97 us
    pallas_call x3, Pallas kernels, bloch(): pl.pallas_call(lambda *refs: bloch_kernel(places, *refs), in_specs=[pl.Bl...  3.87 us
  transfers between devices with their start and end apart: 18, of which 9 were waited for; matrix products, arithmetic and copies ran while one was open for 2% of the time, Pallas kernels for 17%

profile of v3, /device:TPU:0, one launch (start us, length us, event | category | flops | bytes accessed | tf_op | source)
XLA Modules:
  0.0 44.2 jit_solution(4261594679912971135)
XLA Ops:
  0.0 2.3 %shard_map.64 = (bf16[32,128]{1,0:T(8,128)(2,1)S(1)}, bf16[4,32,1920]{2,1,0:T(8,128)(2,1)S(1)}) custom-call(s32[1]{0:T(128)} %bitcast.refs_0_, f32[1,3]{1,0:T(1,128)} %bitcast.4, s32[3,4]{1,0:T(4,128)} %refs_2_.3, bf16[4,2,16,30720]{3,2,1,0:T(8,128)(2,1)} %refs_2_.5), custom_call_target="tpu_custom_call" | custom-call | flops 62914560 | bytes 1966080 | tf_op jit(solution)/shard_map/pallas_call | solution.py:102
  2.3 0.5 %collective-permute-start = (bf16[4,32,1920]{2,1,0:T(8,128)(2,1)S(1)}, bf16[4,32,1920]{2,1,0:T(8,128)(2,1)S(1)}, u32[]{:S(2)}, u32[]{:S(2)}) collective-permute-start(bf16[4,32,1920]{2,1,0:T(8,128)(2,1)S(1)} %get-tuple-element.15), channel_id=1, source_target_pairs={{0,1},{1,0},{2,3},{3,2},{4,5},{5,4},{6,7},{7,6},{8,9},{9,8},{10,11... | collective-permute-start | bytes 1474568 | tf_op jit(solution)/shard_map/p_core/ppermute | solution.py:204
  2.8 2.8 %shard_map.65 = (f32[4,32,1920]{2,1,0:T(8,128)S(1)}, bf16[4,32,1920]{2,1,0:T(8,128)(2,1)S(1)}) custom-call(s32[1]{0:T(128)} %bitcast.refs_0_, bf16[32,128]{1,0:T(8,128)(2,1)S(1)} %get-tuple-element.13.refs_1_, bf16[4,2,16,30720]{3,2,1,0:T(8,128)(2,1)} %refs_2_.5), custom_call_target="tpu_custom_call" | custom-call | flops 125829120 | bytes 3932160 | tf_op jit(solution)/shard_map/pallas_call | solution.py:102
  5.6 0.2 collective-permute-start.1
  5.7 0.1 fusion.7
  5.9 3.1 %collective-permute-start.8 = (bf16[1,32,1920]{2,1,0:T(8,128)(2,1)S(1)}, bf16[1,32,1920]{2,1,0:T(8,128)(2,1)S(1)}, u32[]{:S(2)}, u32[]{:S(2)}) collective-permute-start(bf16[1,32,1920]{2,1,0:T(8,128)(2,1)S(1)} %get-tuple-element.27), channel_id=1, source_target_pairs={{0,2},{1,3},{2,0},{3,1},{4,6},{5,7},{6,4},{7,5},{8,10},{9,11},{10,... | collective-permute-start | bytes 368648 | tf_op jit(solution)/shard_map/p_rs/ppermute | solution.py:204
  9.0 1.5 %collective-permute-start.9 = (bf16[1,32,1920]{2,1,0:T(8,128)(2,1)S(1)}, bf16[1,32,1920]{2,1,0:T(8,128)(2,1)S(1)}, u32[]{:S(2)}, u32[]{:S(2)}) collective-permute-start(bf16[1,32,1920]{2,1,0:T(8,128)(2,1)S(1)} %get-tuple-element.25), channel_id=1, source_target_pairs={{0,4},{1,5},{2,6},{3,7},{4,0},{5,1},{6,2},{7,3},{8,12},{9,13},{10,... | collective-permute-start | bytes 368648 | tf_op jit(solution)/shard_map/p_rs/ppermute | solution.py:204
  10.6 0.3 shard_map.66.refs_1_
  10.9 1.9 %shard_map.67 = f32[4,32,1920]{2,1,0:T(8,128)S(1)} custom-call(s32[1]{0:T(128)} %bitcast.refs_0_, bf16[32,128]{1,0:T(8,128)(2,1)S(1)} %get-tuple-element.13.refs_1_, bf16[4,2,16,30720]{3,2,1,0:T(8,128)(2,1)} %refs_2_.5), custom_call_target="tpu_custom_call" | custom-call | flops 62914560 | bytes 1966080 | tf_op jit(solution)/shard_map/pallas_call | solution.py:102
  13.0 2.0 %collective-permute-start.2 = (bf16[1,32,1920]{2,1,0:T(8,128)(2,1)S(1)}, bf16[1,32,1920]{2,1,0:T(8,128)(2,1)S(1)}, u32[]{:S(2)}, u32[]{:S(2)}) collective-permute-start(bf16[1,32,1920]{2,1,0:T(8,128)(2,1)S(1)} %get-tuple-element.28), channel_id=1, source_target_pairs={{0,2},{1,3},{2,0},{3,1},{4,6},{5,7},{6,4},{7,5},{8,10},{9,11},{10,... | collective-permute-start | bytes 368648 | tf_op jit(solution)/shard_map/q_rs/ppermute | solution.py:204
  15.0 1.5 %collective-permute-start.4 = (bf16[1,32,1920]{2,1,0:T(8,128)(2,1)S(1)}, bf16[1,32,1920]{2,1,0:T(8,128)(2,1)S(1)}, u32[]{:S(2)}, u32[]{:S(2)}) collective-permute-start(bf16[1,32,1920]{2,1,0:T(8,128)(2,1)S(1)} %get-tuple-element.29), channel_id=1, source_target_pairs={{0,6},{1,7},{2,4},{3,5},{4,2},{5,3},{6,0},{7,1},{8,14},{9,15},{10,... | collective-permute-start | bytes 368648 | tf_op jit(solution)/shard_map/q_rs/ppermute | solution.py:204
  16.5 0.3 collective-permute-start.3
  16.8 2.8 %collective-permute-start.11 = (bf16[1,32,1920]{2,1,0:T(8,128)(2,1)S(1)}, bf16[1,32,1920]{2,1,0:T(8,128)(2,1)S(1)}, u32[]{:S(2)}, u32[]{:S(2)}) collective-permute-start(bf16[1,32,1920]{2,1,0:T(8,128)(2,1)S(1)} %fusion.5), channel_id=1, source_target_pairs={{0,8},{1,9},{2,10},{3,11},{4,12},{5,13},{6,14},{7,15},{8,0},{9,1},... | collective-permute-start | bytes 368648 | tf_op jit(solution)/shard_map/p_far/ppermute | solution.py:204
  19.6 1.0 %collective-permute-done.2 = bf16[1,32,1920]{2,1,0:T(8,128)(2,1)S(1)} collective-permute-done((bf16[1,32,1920]{2,1,0:T(8,128)(2,1)S(1)}, bf16[1,32,1920]{2,1,0:T(8,128)(2,1)S(1)}, u32[]{:S(2)}, u32[]{:S(2)}) %collective-permute-start.2) | collective-permute-done | bytes 122912 | tf_op jit(solution)/shard_map/q_rs/ppermute | solution.py:204
  20.7 2.4 %collective-permute-done.4 = bf16[1,32,1920]{2,1,0:T(8,128)(2,1)S(1)} collective-permute-done((bf16[1,32,1920]{2,1,0:T(8,128)(2,1)S(1)}, bf16[1,32,1920]{2,1,0:T(8,128)(2,1)S(1)}, u32[]{:S(2)}, u32[]{:S(2)}) %collective-permute-start.4) | collective-permute-done | bytes 122912 | tf_op jit(solution)/shard_map/q_rs/ppermute | solution.py:204
  23.0 1.5 %collective-permute-done.3 = bf16[1,32,1920]{2,1,0:T(8,128)(2,1)S(1)} collective-permute-done((bf16[1,32,1920]{2,1,0:T(8,128)(2,1)S(1)}, bf16[1,32,1920]{2,1,0:T(8,128)(2,1)S(1)}, u32[]{:S(2)}, u32[]{:S(2)}) %collective-permute-start.3) | collective-permute-done | bytes 122912 | tf_op jit(solution)/shard_map/q_rs/ppermute | solution.py:204
  24.6 1.5 %collective-permute-start.5 = (bf16[1,32,1920]{2,1,0:T(8,128)(2,1)S(1)}, bf16[1,32,1920]{2,1,0:T(8,128)(2,1)S(1)}, u32[]{:S(2)}, u32[]{:S(2)}) collective-permute-start(bf16[1,32,1920]{2,1,0:T(8,128)(2,1)S(1)} %fusion.4), channel_id=1, source_target_pairs={{0,8},{1,9},{2,10},{3,11},{4,12},{5,13},{6,14},{7,15},{8,0},{9,1},... | collective-permute-start | bytes 368648 | tf_op jit(solution)/shard_map/q_far/ppermute | solution.py:204
  26.2 2.5 %collective-permute-start.14 = (bf16[1,32,1920]{2,1,0:T(8,128)(2,1)S(1)}, bf16[1,32,1920]{2,1,0:T(8,128)(2,1)S(1)}, u32[]{:S(2)}, u32[]{:S(2)}) collective-permute-start(bf16[1,32,1920]{2,1,0:T(8,128)(2,1)S(1)} %add_convert_fusion), channel_id=1, source_target_pairs={{0,4},{1,5},{2,6},{3,7},{4,0},{5,1},{6,2},{7,3},{8,12},{9,13},{10,... | collective-permute-start | bytes 368648 | tf_op jit(solution)/shard_map/p_ag/ppermute | solution.py:204
  28.8 1.3 %collective-permute-start.13 = (bf16[1,32,1920]{2,1,0:T(8,128)(2,1)S(1)}, bf16[1,32,1920]{2,1,0:T(8,128)(2,1)S(1)}, u32[]{:S(2)}, u32[]{:S(2)}) collective-permute-start(bf16[1,32,1920]{2,1,0:T(8,128)(2,1)S(1)} %add_convert_fusion), channel_id=1, source_target_pairs={{0,2},{1,3},{2,0},{3,1},{4,6},{5,7},{6,4},{7,5},{8,10},{9,11},{10,... | collective-permute-start | bytes 368648 | tf_op jit(solution)/shard_map/p_ag/ppermute | solution.py:204
  30.1 0.2 collective-permute-start.12
  30.3 1.1 %collective-permute-done.5 = bf16[1,32,1920]{2,1,0:T(8,128)(2,1)S(1)} collective-permute-done((bf16[1,32,1920]{2,1,0:T(8,128)(2,1)S(1)}, bf16[1,32,1920]{2,1,0:T(8,128)(2,1)S(1)}, u32[]{:S(2)}, u32[]{:S(2)}) %collective-permute-start.5) | collective-permute-done | bytes 122912 | tf_op jit(solution)/shard_map/q_far/ppermute | solution.py:204
  31.5 1.3 %collective-permute-start.15 = (bf16[1,32,1920]{2,1,0:T(8,128)(2,1)S(1)}, bf16[1,32,1920]{2,1,0:T(8,128)(2,1)S(1)}, u32[]{:S(2)}, u32[]{:S(2)}) collective-permute-start(bf16[1,32,1920]{2,1,0:T(8,128)(2,1)S(1)} %add_convert_fusion.1), channel_id=1, source_target_pairs={{0,4},{1,5},{2,6},{3,7},{4,0},{5,1},{6,2},{7,3},{8,12},{9,13},{10,... | collective-permute-start | bytes 368648 | tf_op jit(solution)/shard_map/q_ag/ppermute | solution.py:204
  32.7 1.4 %collective-permute-start.7 = (bf16[1,32,1920]{2,1,0:T(8,128)(2,1)S(1)}, bf16[1,32,1920]{2,1,0:T(8,128)(2,1)S(1)}, u32[]{:S(2)}, u32[]{:S(2)}) collective-permute-start(bf16[1,32,1920]{2,1,0:T(8,128)(2,1)S(1)} %add_convert_fusion.1), channel_id=1, source_target_pairs={{0,2},{1,3},{2,0},{3,1},{4,6},{5,7},{6,4},{7,5},{8,10},{9,11},{10,... | collective-permute-start | bytes 368648 | tf_op jit(solution)/shard_map/q_ag/ppermute | solution.py:204
  34.1 1.7 %collective-permute-start.6 = (bf16[1,32,1920]{2,1,0:T(8,128)(2,1)S(1)}, bf16[1,32,1920]{2,1,0:T(8,128)(2,1)S(1)}, u32[]{:S(2)}, u32[]{:S(2)}) collective-permute-start(bf16[1,32,1920]{2,1,0:T(8,128)(2,1)S(1)} %add_convert_fusion.1), channel_id=1, source_target_pairs={{0,6},{1,7},{2,4},{3,5},{4,2},{5,3},{6,0},{7,1},{8,14},{9,15},{10,... | collective-permute-start | bytes 368648 | tf_op jit(solution)/shard_map/q_ag/ppermute | solution.py:204
  35.8 1.0 %collective-permute-done.13 = bf16[1,32,1920]{2,1,0:T(8,128)(2,1)S(1)} collective-permute-done((bf16[1,32,1920]{2,1,0:T(8,128)(2,1)S(1)}, bf16[1,32,1920]{2,1,0:T(8,128)(2,1)S(1)}, u32[]{:S(2)}, u32[]{:S(2)}) %collective-permute-start.13) | collective-permute-done | bytes 122912 | tf_op jit(solution)/shard_map/p_ag/ppermute | solution.py:204
  36.8 0.5 %collective-permute-done.12 = bf16[1,32,1920]{2,1,0:T(8,128)(2,1)S(1)} collective-permute-done((bf16[1,32,1920]{2,1,0:T(8,128)(2,1)S(1)}, bf16[1,32,1920]{2,1,0:T(8,128)(2,1)S(1)}, u32[]{:S(2)}, u32[]{:S(2)}) %collective-permute-start.12) | collective-permute-done | bytes 122912 | tf_op jit(solution)/shard_map/p_ag/ppermute | solution.py:204
  37.5 1.2 %shard_map.68.refs_4_ = bf16[2,32,30720]{2,1,0:T(8,128)(2,1)} custom-call(s32[1]{0:T(128)} %bitcast.refs_0_, bf16[64,32]{1,0:T(8,128)(2,1)S(1)} %shard_map.66.refs_1_, bf16[4,32,1920]{2,1,0:T(8,128)(2,1)S(1)} %pad_maximum_fusion.refs_2_), custom_call_target="tpu_custom_call" | custom-call | flops 31457280 | bytes 983040 | tf_op jit(solution)/shard_map/pallas_call | solution.py:174
  38.6 1.0 %collective-permute-done.7 = bf16[1,32,1920]{2,1,0:T(8,128)(2,1)S(1)} collective-permute-done((bf16[1,32,1920]{2,1,0:T(8,128)(2,1)S(1)}, bf16[1,32,1920]{2,1,0:T(8,128)(2,1)S(1)}, u32[]{:S(2)}, u32[]{:S(2)}) %collective-permute-start.7) | collective-permute-done | bytes 122912 | tf_op jit(solution)/shard_map/q_ag/ppermute | solution.py:204
  39.7 1.4 %collective-permute-done.6 = bf16[1,32,1920]{2,1,0:T(8,128)(2,1)S(1)} collective-permute-done((bf16[1,32,1920]{2,1,0:T(8,128)(2,1)S(1)}, bf16[1,32,1920]{2,1,0:T(8,128)(2,1)S(1)}, u32[]{:S(2)}, u32[]{:S(2)}) %collective-permute-start.6) | collective-permute-done | bytes 122912 | tf_op jit(solution)/shard_map/q_ag/ppermute | solution.py:204
  41.2 1.5 %shard_map.69.refs_3_ = bf16[2,32,30720]{2,1,0:T(8,128)(2,1)} custom-call(s32[1]{0:T(128)} %bitcast.refs_0_, bf16[64,32]{1,0:T(8,128)(2,1)S(1)} %shard_map.66.refs_1_, bf16[4,32,1920]{2,1,0:T(8,128)(2,1)S(1)} %collective-permute-done.17.refs_2_, bf16[4,32,1920]{2,1,0:T(8,128)(2,1)S(1)} %pad_maximum_fusion.1.refs_3_, ...), custom_call_target="tpu_custom_call", output_to_operand_aliasing={{}: (4, {})} | custom-call | flops 62914560 | bytes 1966080 | tf_op jit(solution)/shard_map/pallas_call | solution.py:174
  42.8 0.3 collective-permute-done.16.refs_2_
  43.1 1.2 %shard_map.70 = bf16[2,32,30720]{2,1,0:T(8,128)(2,1)} custom-call(s32[1]{0:T(128)} %bitcast.refs_0_, bf16[64,32]{1,0:T(8,128)(2,1)S(1)} %shard_map.66.refs_1_, bf16[4,32,1920]{2,1,0:T(8,128)(2,1)S(1)} %collective-permute-done.16.refs_2_, bf16[2,32,30720]{2,1,0:T(8,128)(2,1)} %shard_map.69.refs_3_), custom_call_target="tpu_custom_call", output_to_operand_aliasing={{}: (3, {})} | custom-call | flops 31457280 | bytes 983040 | tf_op jit(solution)/shard_map/pallas_call | solution.py:174
  (27 shorter events, 0.8 us)
Async XLA Ops:
  2.3 3.4 %collective-permute-start = (bf16[4,32,1920]{2,1,0:T(8,128)(2,1)S(1)}, bf16[4,32,1920]{2,1,0:T(8,128)(2,1)S(1)}, u32[]{:S(2)}, u32[]{:S(2)}) collective-permute-start(bf16[4,32,1920]{2,1,0:T(8,128)(2,1)S(1)} %get-tuple-element.15), channel_id=1, source_target_pairs={{0,1},{1,0},{2,3},{3,2},{4,5},{5,4},{6,7},{7,6},{8,9},{9,8},{10,11... | collective-permute-start | bytes 1474568 | tf_op jit(solution)/shard_map/p_core/ppermute | solution.py:204
  2.8 7.8 %copy-start = (s32[3,32]{1,0:T(4,128)S(1)}, s32[3,32]{1,0:T(4,128)}, u32[]{:S(2)}) copy-start(s32[3,32]{1,0:T(4,128)} %q_ref) | copy-start | bytes 1156
  2.8 7.8 %copy-start.1 = (s32[3,16]{1,0:T(4,128)S(1)}, s32[3,16]{1,0:T(4,128)}, u32[]{:S(2)}) copy-start(s32[3,16]{1,0:T(4,128)} %phon_ref.1) | copy-start | bytes 580
  2.8 7.8 %copy-start.2 = (s32[16]{0:T(128)S(1)}, s32[16]{0:T(128)}, u32[]{:S(2)}) copy-start(s32[16]{0:T(128)} %param.9) | copy-start | bytes 196
  5.6 7.2 %collective-permute-start.1 = (bf16[4,32,1920]{2,1,0:T(8,128)(2,1)S(1)}, bf16[4,32,1920]{2,1,0:T(8,128)(2,1)S(1)}, u32[]{:S(2)}, u32[]{:S(2)}) collective-permute-start(bf16[4,32,1920]{2,1,0:T(8,128)(2,1)S(1)} %get-tuple-element.19), channel_id=1, source_target_pairs={{0,1},{1,0},{2,3},{3,2},{4,5},{5,4},{6,7},{7,6},{8,9},{9,8},{10,11... | collective-permute-start | bytes 1474568 | tf_op jit(solution)/shard_map/q_core/ppermute | solution.py:204
  5.9 10.8 %collective-permute-start.8 = (bf16[1,32,1920]{2,1,0:T(8,128)(2,1)S(1)}, bf16[1,32,1920]{2,1,0:T(8,128)(2,1)S(1)}, u32[]{:S(2)}, u32[]{:S(2)}) collective-permute-start(bf16[1,32,1920]{2,1,0:T(8,128)(2,1)S(1)} %get-tuple-element.27), channel_id=1, source_target_pairs={{0,2},{1,3},{2,0},{3,1},{4,6},{5,7},{6,4},{7,5},{8,10},{9,11},{10,... | collective-permute-start | bytes 368648 | tf_op jit(solution)/shard_map/p_rs/ppermute | solution.py:204
  9.0 7.5 %collective-permute-start.9 = (bf16[1,32,1920]{2,1,0:T(8,128)(2,1)S(1)}, bf16[1,32,1920]{2,1,0:T(8,128)(2,1)S(1)}, u32[]{:S(2)}, u32[]{:S(2)}) collective-permute-start(bf16[1,32,1920]{2,1,0:T(8,128)(2,1)S(1)} %get-tuple-element.25), channel_id=1, source_target_pairs={{0,4},{1,5},{2,6},{3,7},{4,0},{5,1},{6,2},{7,3},{8,12},{9,13},{10,... | collective-permute-start | bytes 368648 | tf_op jit(solution)/shard_map/p_rs/ppermute | solution.py:204
  10.5 6.2 %collective-permute-start.10 = (bf16[1,32,1920]{2,1,0:T(8,128)(2,1)S(1)}, bf16[1,32,1920]{2,1,0:T(8,128)(2,1)S(1)}, u32[]{:S(2)}, u32[]{:S(2)}) collective-permute-start(bf16[1,32,1920]{2,1,0:T(8,128)(2,1)S(1)} %get-tuple-element.26), channel_id=1, source_target_pairs={{0,6},{1,7},{2,4},{3,5},{4,2},{5,3},{6,0},{7,1},{8,14},{9,15},{10,... | collective-permute-start | bytes 368648 | tf_op jit(solution)/shard_map/p_rs/ppermute | solution.py:204
  13.0 7.7 %collective-permute-start.2 = (bf16[1,32,1920]{2,1,0:T(8,128)(2,1)S(1)}, bf16[1,32,1920]{2,1,0:T(8,128)(2,1)S(1)}, u32[]{:S(2)}, u32[]{:S(2)}) collective-permute-start(bf16[1,32,1920]{2,1,0:T(8,128)(2,1)S(1)} %get-tuple-element.28), channel_id=1, source_target_pairs={{0,2},{1,3},{2,0},{3,1},{4,6},{5,7},{6,4},{7,5},{8,10},{9,11},{10,... | collective-permute-start | bytes 368648 | tf_op jit(solution)/shard_map/q_rs/ppermute | solution.py:204
  15.0 8.1 %collective-permute-start.4 = (bf16[1,32,1920]{2,1,0:T(8,128)(2,1)S(1)}, bf16[1,32,1920]{2,1,0:T(8,128)(2,1)S(1)}, u32[]{:S(2)}, u32[]{:S(2)}) collective-permute-start(bf16[1,32,1920]{2,1,0:T(8,128)(2,1)S(1)} %get-tuple-element.29), channel_id=1, source_target_pairs={{0,6},{1,7},{2,4},{3,5},{4,2},{5,3},{6,0},{7,1},{8,14},{9,15},{10,... | collective-permute-start | bytes 368648 | tf_op jit(solution)/shard_map/q_rs/ppermute | solution.py:204
  16.5 8.1 %collective-permute-start.3 = (bf16[1,32,1920]{2,1,0:T(8,128)(2,1)S(1)}, bf16[1,32,1920]{2,1,0:T(8,128)(2,1)S(1)}, u32[]{:S(2)}, u32[]{:S(2)}) collective-permute-start(bf16[1,32,1920]{2,1,0:T(8,128)(2,1)S(1)} %get-tuple-element.30), channel_id=1, source_target_pairs={{0,4},{1,5},{2,6},{3,7},{4,0},{5,1},{6,2},{7,3},{8,12},{9,13},{10,... | collective-permute-start | bytes 368648 | tf_op jit(solution)/shard_map/q_rs/ppermute | solution.py:204
  16.8 9.3 %collective-permute-start.11 = (bf16[1,32,1920]{2,1,0:T(8,128)(2,1)S(1)}, bf16[1,32,1920]{2,1,0:T(8,128)(2,1)S(1)}, u32[]{:S(2)}, u32[]{:S(2)}) collective-permute-start(bf16[1,32,1920]{2,1,0:T(8,128)(2,1)S(1)} %fusion.5), channel_id=1, source_target_pairs={{0,8},{1,9},{2,10},{3,11},{4,12},{5,13},{6,14},{7,15},{8,0},{9,1},... | collective-permute-start | bytes 368648 | tf_op jit(solution)/shard_map/p_far/ppermute | solution.py:204
  24.6 6.8 %collective-permute-start.5 = (bf16[1,32,1920]{2,1,0:T(8,128)(2,1)S(1)}, bf16[1,32,1920]{2,1,0:T(8,128)(2,1)S(1)}, u32[]{:S(2)}, u32[]{:S(2)}) collective-permute-start(bf16[1,32,1920]{2,1,0:T(8,128)(2,1)S(1)} %fusion.4), channel_id=1, source_target_pairs={{0,8},{1,9},{2,10},{3,11},{4,12},{5,13},{6,14},{7,15},{8,0},{9,1},... | collective-permute-start | bytes 368648 | tf_op jit(solution)/shard_map/q_far/ppermute | solution.py:204
  26.2 7.9 %collective-permute-start.14 = (bf16[1,32,1920]{2,1,0:T(8,128)(2,1)S(1)}, bf16[1,32,1920]{2,1,0:T(8,128)(2,1)S(1)}, u32[]{:S(2)}, u32[]{:S(2)}) collective-permute-start(bf16[1,32,1920]{2,1,0:T(8,128)(2,1)S(1)} %add_convert_fusion), channel_id=1, source_target_pairs={{0,4},{1,5},{2,6},{3,7},{4,0},{5,1},{6,2},{7,3},{8,12},{9,13},{10,... | collective-permute-start | bytes 368648 | tf_op jit(solution)/shard_map/p_ag/ppermute | solution.py:204
  28.8 8.0 %collective-permute-start.13 = (bf16[1,32,1920]{2,1,0:T(8,128)(2,1)S(1)}, bf16[1,32,1920]{2,1,0:T(8,128)(2,1)S(1)}, u32[]{:S(2)}, u32[]{:S(2)}) collective-permute-start(bf16[1,32,1920]{2,1,0:T(8,128)(2,1)S(1)} %add_convert_fusion), channel_id=1, source_target_pairs={{0,2},{1,3},{2,0},{3,1},{4,6},{5,7},{6,4},{7,5},{8,10},{9,11},{10,... | collective-permute-start | bytes 368648 | tf_op jit(solution)/shard_map/p_ag/ppermute | solution.py:204
  30.1 7.2 %collective-permute-start.12 = (bf16[1,32,1920]{2,1,0:T(8,128)(2,1)S(1)}, bf16[1,32,1920]{2,1,0:T(8,128)(2,1)S(1)}, u32[]{:S(2)}, u32[]{:S(2)}) collective-permute-start(bf16[1,32,1920]{2,1,0:T(8,128)(2,1)S(1)} %add_convert_fusion), channel_id=1, source_target_pairs={{0,6},{1,7},{2,4},{3,5},{4,2},{5,3},{6,0},{7,1},{8,14},{9,15},{10,... | collective-permute-start | bytes 368648 | tf_op jit(solution)/shard_map/p_ag/ppermute | solution.py:204
  31.5 8.2 %collective-permute-start.15 = (bf16[1,32,1920]{2,1,0:T(8,128)(2,1)S(1)}, bf16[1,32,1920]{2,1,0:T(8,128)(2,1)S(1)}, u32[]{:S(2)}, u32[]{:S(2)}) collective-permute-start(bf16[1,32,1920]{2,1,0:T(8,128)(2,1)S(1)} %add_convert_fusion.1), channel_id=1, source_target_pairs={{0,4},{1,5},{2,6},{3,7},{4,0},{5,1},{6,2},{7,3},{8,12},{9,13},{10,... | collective-permute-start | bytes 368648 | tf_op jit(solution)/shard_map/q_ag/ppermute | solution.py:204
  32.7 6.9 %collective-permute-start.7 = (bf16[1,32,1920]{2,1,0:T(8,128)(2,1)S(1)}, bf16[1,32,1920]{2,1,0:T(8,128)(2,1)S(1)}, u32[]{:S(2)}, u32[]{:S(2)}) collective-permute-start(bf16[1,32,1920]{2,1,0:T(8,128)(2,1)S(1)} %add_convert_fusion.1), channel_id=1, source_target_pairs={{0,2},{1,3},{2,0},{3,1},{4,6},{5,7},{6,4},{7,5},{8,10},{9,11},{10,... | collective-permute-start | bytes 368648 | tf_op jit(solution)/shard_map/q_ag/ppermute | solution.py:204
  34.1 6.9 %collective-permute-start.6 = (bf16[1,32,1920]{2,1,0:T(8,128)(2,1)S(1)}, bf16[1,32,1920]{2,1,0:T(8,128)(2,1)S(1)}, u32[]{:S(2)}, u32[]{:S(2)}) collective-permute-start(bf16[1,32,1920]{2,1,0:T(8,128)(2,1)S(1)} %add_convert_fusion.1), channel_id=1, source_target_pairs={{0,6},{1,7},{2,4},{3,5},{4,2},{5,3},{6,0},{7,1},{8,14},{9,15},{10,... | collective-permute-start | bytes 368648 | tf_op jit(solution)/shard_map/q_ag/ppermute | solution.py:204
  37.4 3.8 %collective-permute-start.17 = (bf16[4,32,1920]{2,1,0:T(8,128)(2,1)S(1)}, bf16[4,32,1920]{2,1,0:T(8,128)(2,1)S(1)}, u32[]{:S(2)}, u32[]{:S(2)}) collective-permute-start(bf16[4,32,1920]{2,1,0:T(8,128)(2,1)S(1)} %pad_maximum_fusion.refs_2_), channel_id=1, source_target_pairs={{0,1},{1,0},{2,3},{3,2},{4,5},{5,4},{6,7},{7,6},{8,9},{9,8},{10,11... | collective-permute-start | bytes 1474568 | tf_op jit(solution)/shard_map/p_core2/ppermute | solution.py:204
  41.1 1.9 %collective-permute-start.16 = (bf16[4,32,1920]{2,1,0:T(8,128)(2,1)S(1)}, bf16[4,32,1920]{2,1,0:T(8,128)(2,1)S(1)}, u32[]{:S(2)}, u32[]{:S(2)}) collective-permute-start(bf16[4,32,1920]{2,1,0:T(8,128)(2,1)S(1)} %pad_maximum_fusion.1.refs_3_), channel_id=1, source_target_pairs={{0,1},{1,0},{2,3},{3,2},{4,5},{5,4},{6,7},{7,6},{8,9},{9,8},{10,11... | collective-permute-start | bytes 1474568 | tf_op jit(solution)/shard_map/q_core2/ppermute | solution.py:204

commit v4 on v3

v4 whole, which is shorter than its diff:
```python
import math

import jax
import jax.numpy as jnp
from jax import lax
from jax.experimental import pallas as pl
from jax.experimental.pallas import tpu as pltpu
from jax.sharding import PartitionSpec as P

NG = 16
STREAMS = (1, 1)
BLOCKS = 8
SHARE = (1, 3)
LANES = 128
VMEM_LIMIT = 24 * 2**20

CHIPS = ("across", "x", "z", "own")
SQUARE = (6, 2, 4)
SUM_ORDER = (1, 2, 0)
GATHER_ORDER = (1, 2, 0)


def block_of(me, place):
    other, chip = place
    core, x, z = me % 2, (me // 2) % 2, (me // 4) % 2
    flip_x, flip_z = {"across": (1, 1), "x": (1, 0), "z": (0, 1), "own": (0, 0)}[chip]
    return (core + other) % 2 * 4 + (x + flip_x) % 2 * 2 + (z + flip_z) % 2


def stream_columns(width, stream):
    unit = width // BLOCKS // sum(STREAMS)
    return sum(STREAMS[:stream]) * unit * BLOCKS, STREAMS[stream] * unit


def columns_at(me, place, stream, width):
    start, columns = stream_columns(width, stream)
    start = start + block_of(me, place) * columns
    return pl.ds(pl.multiple_of(start, 128), columns)


def phase_matrix(k_row, elec_vectors, shape, slab, parts):
    rows, depth = shape
    terms = [k_row[:, d : d + 1] * elec_vectors[d : d + 1, :].astype(jnp.float32) for d in range(3)]
    theta_here = 2.0 * math.pi * (terms[0] + terms[1] + terms[2])
    vector = lax.broadcasted_iota(jnp.int32, (8, depth), 1) // (parts * slab)
    theta = jnp.zeros((8, depth), jnp.float32)
    for e in range(elec_vectors.shape[1]):
        theta = jnp.where(vector == e, theta_here[:, e : e + 1], theta)
    cos = jnp.cos(theta)[:1]
    sin = jnp.sin(theta)[:1]
    row = lax.broadcasted_iota(jnp.int32, shape, 0)
    col = lax.broadcasted_iota(jnp.int32, shape, 1)
    out_part, in_part = row // slab, (col // slab) % parts
    value = jnp.where(out_part == in_part, cos, jnp.where(out_part == 1, sin, -sin))
    return jnp.where(row % slab == col % slab, value, 0.0).astype(jnp.bfloat16)


def partial_kernel(pieces, given, me_ref, *refs):
    *refs, sems = refs
    refs, tables = refs[: -len(pieces)], refs[-len(pieces) :]
    if given:
        kmat_in, couplings_hbm, *outs = refs
    else:
        k_hbm, elec_hbm, couplings_hbm, kmat_out, *outs, k_buf, elec_buf, small = refs
        small_copies = [
            pltpu.make_async_copy(k_hbm, k_buf, small.at[0]),
            pltpu.make_async_copy(elec_hbm, elec_buf, small.at[1]),
        ]
        for copy in small_copies:
            copy.start()
    re_here, parts, slab = couplings_hbm.shape[:3]
    rows, depth = parts * slab, re_here * parts * slab
    width = couplings_hbm.shape[3]
    copies = []
    for piece, (other, stream, _) in enumerate(pieces):
        for j, chip in enumerate(CHIPS):
            place = columns_at(me_ref[0], (other, chip), stream, width)
            n = len(copies)
            copies.append(pltpu.make_async_copy(couplings_hbm.at[:, :, :, place], tables[piece].at[j], sems.at[n]))
            copies[-1].start()
    if given:
        kmat = kmat_in[...]
    else:
        for copy in small_copies:
            copy.wait()
        kmat = phase_matrix(k_buf[...], elec_buf[...], (rows, depth), slab, parts)
        kmat_out[...] = kmat
    here = [
        tuple(kmat[r : r + 1, e * rows : e * rows + 1].astype(jnp.float32) for r in (0, slab)) for e in range(re_here)
    ]
    for n, copy in enumerate(copies):
        out_ref, table = outs[n // len(CHIPS)], tables[n // len(CHIPS)]
        columns = out_ref.shape[-1]
        split = columns * SHARE[0] // SHARE[1] // 128 * 128
        copy.wait()
        if split:
            flat = table[n % len(CHIPS), :, :, :, :split].reshape(depth, split)
            out_ref[n % len(CHIPS), :, :split] = jnp.dot(kmat, flat, preferred_element_type=jnp.float32).astype(out_ref.dtype)
        for low in range(split, columns, LANES):
            place = pl.ds(low, min(LANES, columns - low))
            real = imag = 0.0
            for e, (cos, sin) in enumerate(here):
                a = table[n % len(CHIPS), e, 0, :, place].astype(jnp.float32)
                b = table[n % len(CHIPS), e, 1, :, place].astype(jnp.float32)
                real, imag = real + (cos * a - sin * b), imag + (sin * a + cos * b)
            out_ref[n % len(CHIPS), :slab, place] = real.astype(out_ref.dtype)
            out_ref[n % len(CHIPS), slab:, place] = imag.astype(out_ref.dtype)


def partial_sums(me, phases, couplings, pieces):
    re_here, parts, slab, width = couplings.shape
    sizes = [stream_columns(width, stream)[1] for _, stream, _ in pieces]
    rows, depth = parts * slab, re_here * parts * slab
    hbm, vmem = pl.BlockSpec(memory_space=pltpu.HBM), pl.BlockSpec(memory_space=pltpu.VMEM)
    given = not isinstance(phases, tuple)
    if given:
        operands, specs, first_out, small = [phases], [vmem], [], []
    else:
        k_point, elec_vectors = phases
        operands = [pltpu.with_memory_space_constraint(a, pltpu.HBM) for a in (k_point.reshape(1, 3), elec_vectors)]
        specs, first_out = [hbm, hbm], [jax.ShapeDtypeStruct((rows, depth), jnp.bfloat16)]
        small = [
            pltpu.VMEM((1, 3), jnp.float32),
            pltpu.VMEM(elec_vectors.shape, jnp.int32),
            pltpu.SemaphoreType.DMA((2,)),
        ]
    copies = len(CHIPS) * len(pieces)
    outs = first_out + [jax.ShapeDtypeStruct((len(CHIPS), rows, n), dtype) for (_, _, dtype), n in zip(pieces, sizes)]
    return pl.pallas_call(
        lambda *refs: partial_kernel(pieces, given, *refs),
        in_specs=[pl.BlockSpec(memory_space=pltpu.SMEM), *specs, hbm],
        out_specs=[vmem] * len(outs),
        out_shape=outs,
        scratch_shapes=small
        + [pltpu.VMEM((len(CHIPS), re_here, parts, slab, n), couplings.dtype) for n in sizes]
        + [pltpu.SemaphoreType.DMA((copies,))],
        compiler_params=pltpu.CompilerParams(vmem_limit_bytes=VMEM_LIMIT),
        cost_estimate=pl.CostEstimate(
            flops=2 * rows * depth * len(CHIPS) * sum(sizes),
            bytes_accessed=2 * depth * len(CHIPS) * sum(sizes),
            transcendentals=0,
        ),
    )(me, *operands, pltpu.with_memory_space_constraint(couplings, pltpu.HBM))


def q_matrix_kernel(q_ref, phon_ref, degeneracy_ref, out_ref):
    points, slab = out_ref.shape[0] // 2, out_ref.shape[1] // 2
    dots = lax.dot_general(
        q_ref[...].astype(jnp.float32),
        phon_ref[...].astype(jnp.float32),
        (((0,), (0,)), ((), ())),
        preferred_element_type=jnp.float32,
    )
    wound = jnp.bitwise_and(dots.astype(jnp.int32), NG - 1).astype(jnp.float32)
    angle = 2.0 * math.pi * wound / NG
    weight = 1.0 / degeneracy_ref[...].astype(jnp.float32)
    qcos = jnp.cos(angle) * weight
    qsin = jnp.sin(angle) * weight
    out_ref[:points, :slab] = qcos.astype(out_ref.dtype)
    out_ref[:points, slab:] = (-qsin).astype(out_ref.dtype)
    out_ref[points:, :slab] = qsin.astype(out_ref.dtype)
    out_ref[points:, slab:] = qcos.astype(out_ref.dtype)


def q_matrix(q_index, phon_vectors, degeneracy):
    points, slab = q_index.shape[1], phon_vectors.shape[1]
    return pl.pallas_call(
        q_matrix_kernel,
        out_shape=jax.ShapeDtypeStruct((2 * points, 2 * slab), jnp.bfloat16),
        compiler_params=pltpu.CompilerParams(vmem_limit_bytes=VMEM_LIMIT),
    )(q_index, phon_vectors, degeneracy.reshape(1, slab))


def bloch_kernel(places, me_ref, qmat_ref, *refs):
    count = len(places)
    slabs, out_hbm, buffers, sems = refs[:count], refs[-count - 2], refs[-count - 1 : -1], refs[-1]
    points, width = out_hbm.shape[1:]
    copies = []
    for (other, stream), slab_ref, buffer in zip(places, slabs, buffers):
        for j, chip in enumerate(CHIPS):
            result = jnp.dot(qmat_ref[...], slab_ref[j], preferred_element_type=jnp.float32).astype(buffer.dtype)
            buffer[j, 0] = result[:points]
            buffer[j, 1] = result[points:]
            place = columns_at(me_ref[0], (other, chip), stream, width)
            copies.append(pltpu.make_async_copy(buffer.at[j], out_hbm.at[:, :, place], sems.at[len(copies)]))
            copies[-1].start()
    for copy in copies:
        copy.wait()


def bloch(me, qmat, pieces, width, out=None):
    slabs = [slab for slab, _, _ in pieces]
    places = [(other, stream) for _, other, stream in pieces]
    columns = sum(slab.shape[0] * slab.shape[2] for slab in slabs)
    points = qmat.shape[0] // 2
    vmem, hbm = pl.BlockSpec(memory_space=pltpu.VMEM), pl.BlockSpec(memory_space=pltpu.HBM)
    before = () if out is None else (out,)
    return pl.pallas_call(
        lambda *refs: bloch_kernel(places, *refs),
        in_specs=[pl.BlockSpec(memory_space=pltpu.SMEM), vmem] + [vmem] * len(slabs) + [hbm] * len(before),
        out_specs=hbm,
        out_shape=jax.ShapeDtypeStruct((2, points, width), jnp.bfloat16),
        scratch_shapes=[pltpu.VMEM((slab.shape[0], 2, points, slab.shape[2]), jnp.bfloat16) for slab in slabs]
        + [pltpu.SemaphoreType.DMA((sum(slab.shape[0] for slab in slabs),))],
        input_output_aliases={2 + len(slabs): 0} if before else {},
        compiler_params=pltpu.CompilerParams(vmem_limit_bytes=VMEM_LIMIT),
        cost_estimate=pl.CostEstimate(
            flops=2 * qmat.size * columns,
            bytes_accessed=4 * points * columns,
            transcendentals=0,
        ),
    )(me, qmat, *slabs, *before)


def after(value, *others):
    return lax.optimization_barrier((value, *others))[0]


def on_device(devices, couplings, elec_vectors, phon_vectors, degeneracy, k_point, q_index):
    width = couplings.shape[3]
    wire, full = jnp.bfloat16, jnp.float32
    me = lax.axis_index("blk").astype(jnp.int32).reshape(1)
    streams = range(len(STREAMS))
    last = len(STREAMS) - 1

    def send(array, bits, name):
        with jax.named_scope(name):
            return lax.ppermute(array, "blk", [(i, i ^ bits) for i in range(devices)])

    def to_core(array, name):
        return send(array, 1, name)

    got, first, total, block = {}, {}, {}, {}
    kmat, theirs = partial_sums(me, (k_point, elec_vectors), couplings, [(1, 0, wire)])
    got[0] = to_core(theirs, "core_sum0")
    for s in streams:
        here = me if s == 0 else after(me, first[s - 1])
        pieces = [(0, s, full)] + [(1, s + 1, wire)] * (s < last)
        own, *theirs = partial_sums(here, kmat, couplings, pieces)
        if theirs:
            got[s + 1] = to_core(theirs[0], f"core_sum{s + 1}")
        total[s] = own + got[s].astype(full)
        parts = [total[s][i : i + 1].astype(wire) for i in SUM_ORDER]
        first[s] = parts[0]
        got[s] = [send(part, SQUARE[i], f"square_sum{s}") for i, part in zip(SUM_ORDER, parts)]
    qmat = q_matrix(after(q_index, first[last]), phon_vectors, degeneracy)
    total[last] = after(total[last], qmat)

    for s in streams:
        own = total[s][3:]
        for array in got[s]:
            own = own + array.astype(full)
        step = 8
        while step < devices:
            own = own + send(own.astype(wire), step, f"far_sum{s}").astype(full)
            step *= 2
        block[s] = own.astype(wire)

    for s in streams:
        back = {i: send(block[s], SQUARE[i], f"square_gather{s}") for i in GATHER_ORDER}
        got[s] = [back[i] for i in range(3)]

    out = None
    for s in streams:
        if s:
            got[s][0] = after(got[s][0], out)
        mine = jnp.concatenate([*got[s], block[s]])
        pieces = [(mine, 0, s)] if s == 0 else [(theirs, 1, s - 1), (mine, 0, s)]
        theirs = to_core(mine, f"core_gather{s}")
        out = bloch(me, qmat, pieces, width, out)
    return bloch(me, qmat, [(theirs, 1, last)], width, out)


def solution(mesh):
    placed = (
        P("blk", None, "grp", None),
        P(None, "blk"),
        P(None, "grp"),
        P("grp"),
        P("grp"),
        P(None, "blk"),
    )
    devices = mesh.shape["blk"]
    return jax.shard_map(
        lambda *arrays: on_device(devices, *arrays),
        mesh=mesh,
        in_specs=placed,
        out_specs=P(None, ("grp", "blk"), None),
        check_vma=False,
    )
```

time: 44.4 us -> 43.7 us (0.984)
  Pallas kernels: 11.2 us -> 10.5 us
    pallas_call x3, Pallas kernels: 6.97 us -> 6.34 us  [partial_sums(): pl.pallas_call(lambda *refs: partial_kernel(pieces, given, *refs), in_spe...]
  transfers between devices with their start and end apart: 18 -> 18, of which waited for: 9 -> 7; matrix products, arithmetic and copies ran while one was open for 2% -> 2% of each run, Pallas kernels for 17% -> 17%
where the time goes in v4:
time: 43.7 us; the launch traced here: 43.5 us
  starting transfers between devices  21.9 us (50%)
  Pallas kernels  10.5 us (24%)
  waiting for transfers between devices  10.2 us (23%)
  other arithmetic  0.69 us (2%)
    ppermute x18, starting transfers between devices, send(): return lax.ppermute(array, 'blk', [(i, i ^ bits) for i in range(devices)])  21.9 us
    ppermute x18, waiting for transfers between devices, send(): return lax.ppermute(array, 'blk', [(i, i ^ bits) for i in range(devices)])  10.2 us
    pallas_call x3, Pallas kernels, partial_sums(): pl.pallas_call(lambda *refs: partial_kernel(pieces, given, *refs), in_spe...  6.34 us
    pallas_call x3, Pallas kernels, bloch(): pl.pallas_call(lambda *refs: bloch_kernel(places, *refs), in_specs=[pl.Bl...  3.87 us
  transfers between devices with their start and end apart: 18, of which 7 were waited for; matrix products, arithmetic and copies ran while one was open for 2% of the time, Pallas kernels for 17%

profile of v4, /device:TPU:0, one launch (start us, length us, event | category | flops | bytes accessed | tf_op | source)
XLA Modules:
  0.0 43.5 jit_solution(9937764090408983879)
XLA Ops:
  0.0 2.2 %shard_map.64 = (bf16[32,128]{1,0:T(8,128)(2,1)S(1)}, bf16[4,32,1920]{2,1,0:T(8,128)(2,1)S(1)}) custom-call(s32[1]{0:T(128)} %bitcast.refs_0_, f32[1,3]{1,0:T(1,128)} %bitcast.4, s32[3,4]{1,0:T(4,128)} %refs_2_.3, bf16[4,2,16,30720]{3,2,1,0:T(8,128)(2,1)} %refs_2_.5), custom_call_target="tpu_custom_call" | custom-call | flops 62914560 | bytes 1966080 | tf_op jit(solution)/shard_map/pallas_call | solution.py:129
  2.2 0.5 %collective-permute-start = (bf16[4,32,1920]{2,1,0:T(8,128)(2,1)S(1)}, bf16[4,32,1920]{2,1,0:T(8,128)(2,1)S(1)}, u32[]{:S(2)}, u32[]{:S(2)}) collective-permute-start(bf16[4,32,1920]{2,1,0:T(8,128)(2,1)S(1)} %get-tuple-element.15), channel_id=1, source_target_pairs={{0,1},{1,0},{2,3},{3,2},{4,5},{5,4},{6,7},{7,6},{8,9},{9,8},{10,11... | collective-permute-start | bytes 1474568 | tf_op jit(solution)/shard_map/core_sum0/ppermute | solution.py:228
  2.6 2.4 %shard_map.65 = (f32[4,32,1920]{2,1,0:T(8,128)S(1)}, bf16[4,32,1920]{2,1,0:T(8,128)(2,1)S(1)}) custom-call(s32[1]{0:T(128)} %bitcast.refs_0_, bf16[32,128]{1,0:T(8,128)(2,1)S(1)} %get-tuple-element.13.refs_1_, bf16[4,2,16,30720]{3,2,1,0:T(8,128)(2,1)} %refs_2_.5), custom_call_target="tpu_custom_call" | custom-call | flops 125829120 | bytes 3932160 | tf_op jit(solution)/shard_map/pallas_call | solution.py:129
  5.1 0.2 collective-permute-start.1
  5.3 0.1 fusion.5
  5.4 3.1 %collective-permute-start.7 = (bf16[1,32,1920]{2,1,0:T(8,128)(2,1)S(1)}, bf16[1,32,1920]{2,1,0:T(8,128)(2,1)S(1)}, u32[]{:S(2)}, u32[]{:S(2)}) collective-permute-start(bf16[1,32,1920]{2,1,0:T(8,128)(2,1)S(1)} %get-tuple-element.27), channel_id=1, source_target_pairs={{0,2},{1,3},{2,0},{3,1},{4,6},{5,7},{6,4},{7,5},{8,10},{9,11},{10,... | collective-permute-start | bytes 368648 | tf_op jit(solution)/shard_map/square_sum0/ppermute | solution.py:228
  8.5 1.5 %collective-permute-start.8 = (bf16[1,32,1920]{2,1,0:T(8,128)(2,1)S(1)}, bf16[1,32,1920]{2,1,0:T(8,128)(2,1)S(1)}, u32[]{:S(2)}, u32[]{:S(2)}) collective-permute-start(bf16[1,32,1920]{2,1,0:T(8,128)(2,1)S(1)} %get-tuple-element.25), channel_id=1, source_target_pairs={{0,4},{1,5},{2,6},{3,7},{4,0},{5,1},{6,2},{7,3},{8,12},{9,13},{10,... | collective-permute-start | bytes 368648 | tf_op jit(solution)/shard_map/square_sum0/ppermute | solution.py:228
  10.1 1.7 %shard_map.66 = f32[4,32,1920]{2,1,0:T(8,128)S(1)} custom-call(s32[1]{0:T(128)} %bitcast.refs_0_, bf16[32,128]{1,0:T(8,128)(2,1)S(1)} %get-tuple-element.13.refs_1_, bf16[4,2,16,30720]{3,2,1,0:T(8,128)(2,1)} %refs_2_.5), custom_call_target="tpu_custom_call" | custom-call | flops 62914560 | bytes 1966080 | tf_op jit(solution)/shard_map/pallas_call | solution.py:129
  11.9 0.1 fusion.4
  12.0 2.0 %collective-permute-start.2 = (bf16[1,32,1920]{2,1,0:T(8,128)(2,1)S(1)}, bf16[1,32,1920]{2,1,0:T(8,128)(2,1)S(1)}, u32[]{:S(2)}, u32[]{:S(2)}) collective-permute-start(bf16[1,32,1920]{2,1,0:T(8,128)(2,1)S(1)} %get-tuple-element.30), channel_id=1, source_target_pairs={{0,2},{1,3},{2,0},{3,1},{4,6},{5,7},{6,4},{7,5},{8,10},{9,11},{10,... | collective-permute-start | bytes 368648 | tf_op jit(solution)/shard_map/square_sum1/ppermute | solution.py:228
  14.0 0.3 shard_map.67.refs_1_
  14.3 1.6 %collective-permute-start.3 = (bf16[1,32,1920]{2,1,0:T(8,128)(2,1)S(1)}, bf16[1,32,1920]{2,1,0:T(8,128)(2,1)S(1)}, u32[]{:S(2)}, u32[]{:S(2)}) collective-permute-start(bf16[1,32,1920]{2,1,0:T(8,128)(2,1)S(1)} %get-tuple-element.28), channel_id=1, source_target_pairs={{0,4},{1,5},{2,6},{3,7},{4,0},{5,1},{6,2},{7,3},{8,12},{9,13},{10,... | collective-permute-start | bytes 368648 | tf_op jit(solution)/shard_map/square_sum1/ppermute | solution.py:228
  15.9 0.3 collective-permute-start.4
  16.3 2.7 %collective-permute-start.10 = (bf16[1,32,1920]{2,1,0:T(8,128)(2,1)S(1)}, bf16[1,32,1920]{2,1,0:T(8,128)(2,1)S(1)}, u32[]{:S(2)}, u32[]{:S(2)}) collective-permute-start(bf16[1,32,1920]{2,1,0:T(8,128)(2,1)S(1)} %fusion.3), channel_id=1, source_target_pairs={{0,8},{1,9},{2,10},{3,11},{4,12},{5,13},{6,14},{7,15},{8,0},{9,1},... | collective-permute-start | bytes 368648 | tf_op jit(solution)/shard_map/far_sum0/ppermute | solution.py:228
  19.0 3.7 %collective-permute-done.3 = bf16[1,32,1920]{2,1,0:T(8,128)(2,1)S(1)} collective-permute-done((bf16[1,32,1920]{2,1,0:T(8,128)(2,1)S(1)}, bf16[1,32,1920]{2,1,0:T(8,128)(2,1)S(1)}, u32[]{:S(2)}, u32[]{:S(2)}) %collective-permute-start.3) | collective-permute-done | bytes 122912 | tf_op jit(solution)/shard_map/square_sum1/ppermute | solution.py:228
  22.8 1.3 %collective-permute-done.4 = bf16[1,32,1920]{2,1,0:T(8,128)(2,1)S(1)} collective-permute-done((bf16[1,32,1920]{2,1,0:T(8,128)(2,1)S(1)}, bf16[1,32,1920]{2,1,0:T(8,128)(2,1)S(1)}, u32[]{:S(2)}, u32[]{:S(2)}) %collective-permute-start.4) | collective-permute-done | bytes 122912 | tf_op jit(solution)/shard_map/square_sum1/ppermute | solution.py:228
  24.1 1.6 %collective-permute-start.5 = (bf16[1,32,1920]{2,1,0:T(8,128)(2,1)S(1)}, bf16[1,32,1920]{2,1,0:T(8,128)(2,1)S(1)}, u32[]{:S(2)}, u32[]{:S(2)}) collective-permute-start(bf16[1,32,1920]{2,1,0:T(8,128)(2,1)S(1)} %fusion.2), channel_id=1, source_target_pairs={{0,8},{1,9},{2,10},{3,11},{4,12},{5,13},{6,14},{7,15},{8,0},{9,1},... | collective-permute-start | bytes 368648 | tf_op jit(solution)/shard_map/far_sum1/ppermute | solution.py:228
  25.9 2.6 %collective-permute-start.13 = (bf16[1,32,1920]{2,1,0:T(8,128)(2,1)S(1)}, bf16[1,32,1920]{2,1,0:T(8,128)(2,1)S(1)}, u32[]{:S(2)}, u32[]{:S(2)}) collective-permute-start(bf16[1,32,1920]{2,1,0:T(8,128)(2,1)S(1)} %add_convert_fusion), channel_id=1, source_target_pairs={{0,4},{1,5},{2,6},{3,7},{4,0},{5,1},{6,2},{7,3},{8,12},{9,13},{10,... | collective-permute-start | bytes 368648 | tf_op jit(solution)/shard_map/square_gather0/ppermute | solution.py:228
  28.5 1.4 %collective-permute-start.12 = (bf16[1,32,1920]{2,1,0:T(8,128)(2,1)S(1)}, bf16[1,32,1920]{2,1,0:T(8,128)(2,1)S(1)}, u32[]{:S(2)}, u32[]{:S(2)}) collective-permute-start(bf16[1,32,1920]{2,1,0:T(8,128)(2,1)S(1)} %add_convert_fusion), channel_id=1, source_target_pairs={{0,2},{1,3},{2,0},{3,1},{4,6},{5,7},{6,4},{7,5},{8,10},{9,11},{10,... | collective-permute-start | bytes 368648 | tf_op jit(solution)/shard_map/square_gather0/ppermute | solution.py:228
  29.9 0.1 collective-permute-start.11
  30.0 1.4 %collective-permute-done.5 = bf16[1,32,1920]{2,1,0:T(8,128)(2,1)S(1)} collective-permute-done((bf16[1,32,1920]{2,1,0:T(8,128)(2,1)S(1)}, bf16[1,32,1920]{2,1,0:T(8,128)(2,1)S(1)}, u32[]{:S(2)}, u32[]{:S(2)}) %collective-permute-start.5) | collective-permute-done | bytes 122912 | tf_op jit(solution)/shard_map/far_sum1/ppermute | solution.py:228
  31.4 0.1 add_convert_fusion.1
  31.4 0.6 %collective-permute-start.15 = (bf16[1,32,1920]{2,1,0:T(8,128)(2,1)S(1)}, bf16[1,32,1920]{2,1,0:T(8,128)(2,1)S(1)}, u32[]{:S(2)}, u32[]{:S(2)}) collective-permute-start(bf16[1,32,1920]{2,1,0:T(8,128)(2,1)S(1)} %add_convert_fusion.1), channel_id=1, source_target_pairs={{0,4},{1,5},{2,6},{3,7},{4,0},{5,1},{6,2},{7,3},{8,12},{9,13},{10,... | collective-permute-start | bytes 368648 | tf_op jit(solution)/shard_map/square_gather1/ppermute | solution.py:228
  32.1 1.5 %collective-permute-start.14 = (bf16[1,32,1920]{2,1,0:T(8,128)(2,1)S(1)}, bf16[1,32,1920]{2,1,0:T(8,128)(2,1)S(1)}, u32[]{:S(2)}, u32[]{:S(2)}) collective-permute-start(bf16[1,32,1920]{2,1,0:T(8,128)(2,1)S(1)} %add_convert_fusion.1), channel_id=1, source_target_pairs={{0,2},{1,3},{2,0},{3,1},{4,6},{5,7},{6,4},{7,5},{8,10},{9,11},{10,... | collective-permute-start | bytes 368648 | tf_op jit(solution)/shard_map/square_gather1/ppermute | solution.py:228
  33.6 1.9 %collective-permute-start.6 = (bf16[1,32,1920]{2,1,0:T(8,128)(2,1)S(1)}, bf16[1,32,1920]{2,1,0:T(8,128)(2,1)S(1)}, u32[]{:S(2)}, u32[]{:S(2)}) collective-permute-start(bf16[1,32,1920]{2,1,0:T(8,128)(2,1)S(1)} %add_convert_fusion.1), channel_id=1, source_target_pairs={{0,6},{1,7},{2,4},{3,5},{4,2},{5,3},{6,0},{7,1},{8,14},{9,15},{10,... | collective-permute-start | bytes 368648 | tf_op jit(solution)/shard_map/square_gather1/ppermute | solution.py:228
  35.6 2.0 %collective-permute-done.12 = bf16[1,32,1920]{2,1,0:T(8,128)(2,1)S(1)} collective-permute-done((bf16[1,32,1920]{2,1,0:T(8,128)(2,1)S(1)}, bf16[1,32,1920]{2,1,0:T(8,128)(2,1)S(1)}, u32[]{:S(2)}, u32[]{:S(2)}) %collective-permute-start.12) | collective-permute-done | bytes 122912 | tf_op jit(solution)/shard_map/square_gather0/ppermute | solution.py:228
  37.7 1.2 %shard_map.68.refs_4_ = bf16[2,32,30720]{2,1,0:T(8,128)(2,1)} custom-call(s32[1]{0:T(128)} %bitcast.refs_0_, bf16[64,32]{1,0:T(8,128)(2,1)S(1)} %shard_map.67.refs_1_, bf16[4,32,1920]{2,1,0:T(8,128)(2,1)S(1)} %pad_maximum_fusion.refs_2_), custom_call_target="tpu_custom_call" | custom-call | flops 31457280 | bytes 983040 | tf_op jit(solution)/shard_map/pallas_call | solution.py:198
  38.9 1.3 %collective-permute-done.6 = bf16[1,32,1920]{2,1,0:T(8,128)(2,1)S(1)} collective-permute-done((bf16[1,32,1920]{2,1,0:T(8,128)(2,1)S(1)}, bf16[1,32,1920]{2,1,0:T(8,128)(2,1)S(1)}, u32[]{:S(2)}, u32[]{:S(2)}) %collective-permute-start.6) | collective-permute-done | bytes 122912 | tf_op jit(solution)/shard_map/square_gather1/ppermute | solution.py:228
  40.2 0.2 collective-permute-done.14
  40.5 1.5 %shard_map.69.refs_3_ = bf16[2,32,30720]{2,1,0:T(8,128)(2,1)} custom-call(s32[1]{0:T(128)} %bitcast.refs_0_, bf16[64,32]{1,0:T(8,128)(2,1)S(1)} %shard_map.67.refs_1_, bf16[4,32,1920]{2,1,0:T(8,128)(2,1)S(1)} %collective-permute-done.17.refs_2_, bf16[4,32,1920]{2,1,0:T(8,128)(2,1)S(1)} %pad_maximum_fusion.1.refs_3_, ...), custom_call_target="tpu_custom_call", output_to_operand_aliasing={{}: (4, {})} | custom-call | flops 62914560 | bytes 1966080 | tf_op jit(solution)/shard_map/pallas_call | solution.py:198
  42.0 0.3 collective-permute-done.16.refs_2_
  42.4 1.2 %shard_map.70 = bf16[2,32,30720]{2,1,0:T(8,128)(2,1)} custom-call(s32[1]{0:T(128)} %bitcast.refs_0_, bf16[64,32]{1,0:T(8,128)(2,1)S(1)} %shard_map.67.refs_1_, bf16[4,32,1920]{2,1,0:T(8,128)(2,1)S(1)} %collective-permute-done.16.refs_2_, bf16[2,32,30720]{2,1,0:T(8,128)(2,1)} %shard_map.69.refs_3_), custom_call_target="tpu_custom_call", output_to_operand_aliasing={{}: (3, {})} | custom-call | flops 31457280 | bytes 983040 | tf_op jit(solution)/shard_map/pallas_call | solution.py:198
  (27 shorter events, 0.6 us)
Async XLA Ops:
  2.2 3.1 %collective-permute-start = (bf16[4,32,1920]{2,1,0:T(8,128)(2,1)S(1)}, bf16[4,32,1920]{2,1,0:T(8,128)(2,1)S(1)}, u32[]{:S(2)}, u32[]{:S(2)}) collective-permute-start(bf16[4,32,1920]{2,1,0:T(8,128)(2,1)S(1)} %get-tuple-element.15), channel_id=1, source_target_pairs={{0,1},{1,0},{2,3},{3,2},{4,5},{5,4},{6,7},{7,6},{8,9},{9,8},{10,11... | collective-permute-start | bytes 1474568 | tf_op jit(solution)/shard_map/core_sum0/ppermute | solution.py:228
  5.1 6.8 %collective-permute-start.1 = (bf16[4,32,1920]{2,1,0:T(8,128)(2,1)S(1)}, bf16[4,32,1920]{2,1,0:T(8,128)(2,1)S(1)}, u32[]{:S(2)}, u32[]{:S(2)}) collective-permute-start(bf16[4,32,1920]{2,1,0:T(8,128)(2,1)S(1)} %get-tuple-element.17), channel_id=1, source_target_pairs={{0,1},{1,0},{2,3},{3,2},{4,5},{5,4},{6,7},{7,6},{8,9},{9,8},{10,11... | collective-permute-start | bytes 1474568 | tf_op jit(solution)/shard_map/core_sum1/ppermute | solution.py:228
  5.4 10.8 %collective-permute-start.7 = (bf16[1,32,1920]{2,1,0:T(8,128)(2,1)S(1)}, bf16[1,32,1920]{2,1,0:T(8,128)(2,1)S(1)}, u32[]{:S(2)}, u32[]{:S(2)}) collective-permute-start(bf16[1,32,1920]{2,1,0:T(8,128)(2,1)S(1)} %get-tuple-element.27), channel_id=1, source_target_pairs={{0,2},{1,3},{2,0},{3,1},{4,6},{5,7},{6,4},{7,5},{8,10},{9,11},{10,... | collective-permute-start | bytes 368648 | tf_op jit(solution)/shard_map/square_sum0/ppermute | solution.py:228
  8.5 7.4 %collective-permute-start.8 = (bf16[1,32,1920]{2,1,0:T(8,128)(2,1)S(1)}, bf16[1,32,1920]{2,1,0:T(8,128)(2,1)S(1)}, u32[]{:S(2)}, u32[]{:S(2)}) collective-permute-start(bf16[1,32,1920]{2,1,0:T(8,128)(2,1)S(1)} %get-tuple-element.25), channel_id=1, source_target_pairs={{0,4},{1,5},{2,6},{3,7},{4,0},{5,1},{6,2},{7,3},{8,12},{9,13},{10,... | collective-permute-start | bytes 368648 | tf_op jit(solution)/shard_map/square_sum0/ppermute | solution.py:228
  10.0 4.0 %copy-start = (s32[3,32]{1,0:T(4,128)S(1)}, s32[3,32]{1,0:T(4,128)}, u32[]{:S(2)}) copy-start(s32[3,32]{1,0:T(4,128)} %q_ref) | copy-start | bytes 1156
  10.0 4.0 %copy-start.1 = (s32[3,16]{1,0:T(4,128)S(1)}, s32[3,16]{1,0:T(4,128)}, u32[]{:S(2)}) copy-start(s32[3,16]{1,0:T(4,128)} %phon_ref.1) | copy-start | bytes 580
  10.0 4.0 %copy-start.2 = (s32[16]{0:T(128)S(1)}, s32[16]{0:T(128)}, u32[]{:S(2)}) copy-start(s32[16]{0:T(128)} %param.9) | copy-start | bytes 196
  10.0 6.2 %collective-permute-start.9 = (bf16[1,32,1920]{2,1,0:T(8,128)(2,1)S(1)}, bf16[1,32,1920]{2,1,0:T(8,128)(2,1)S(1)}, u32[]{:S(2)}, u32[]{:S(2)}) collective-permute-start(bf16[1,32,1920]{2,1,0:T(8,128)(2,1)S(1)} %get-tuple-element.26), channel_id=1, source_target_pairs={{0,6},{1,7},{2,4},{3,5},{4,2},{5,3},{6,0},{7,1},{8,14},{9,15},{10,... | collective-permute-start | bytes 368648 | tf_op jit(solution)/shard_map/square_sum0/ppermute | solution.py:228
  12.0 12.0 %collective-permute-start.2 = (bf16[1,32,1920]{2,1,0:T(8,128)(2,1)S(1)}, bf16[1,32,1920]{2,1,0:T(8,128)(2,1)S(1)}, u32[]{:S(2)}, u32[]{:S(2)}) collective-permute-start(bf16[1,32,1920]{2,1,0:T(8,128)(2,1)S(1)} %get-tuple-element.30), channel_id=1, source_target_pairs={{0,2},{1,3},{2,0},{3,1},{4,6},{5,7},{6,4},{7,5},{8,10},{9,11},{10,... | collective-permute-start | bytes 368648 | tf_op jit(solution)/shard_map/square_sum1/ppermute | solution.py:228
  14.3 8.4 %collective-permute-start.3 = (bf16[1,32,1920]{2,1,0:T(8,128)(2,1)S(1)}, bf16[1,32,1920]{2,1,0:T(8,128)(2,1)S(1)}, u32[]{:S(2)}, u32[]{:S(2)}) collective-permute-start(bf16[1,32,1920]{2,1,0:T(8,128)(2,1)S(1)} %get-tuple-element.28), channel_id=1, source_target_pairs={{0,4},{1,5},{2,6},{3,7},{4,0},{5,1},{6,2},{7,3},{8,12},{9,13},{10,... | collective-permute-start | bytes 368648 | tf_op jit(solution)/shard_map/square_sum1/ppermute | solution.py:228
  15.9 8.2 %collective-permute-start.4 = (bf16[1,32,1920]{2,1,0:T(8,128)(2,1)S(1)}, bf16[1,32,1920]{2,1,0:T(8,128)(2,1)S(1)}, u32[]{:S(2)}, u32[]{:S(2)}) collective-permute-start(bf16[1,32,1920]{2,1,0:T(8,128)(2,1)S(1)} %get-tuple-element.29), channel_id=1, source_target_pairs={{0,6},{1,7},{2,4},{3,5},{4,2},{5,3},{6,0},{7,1},{8,14},{9,15},{10,... | collective-permute-start | bytes 368648 | tf_op jit(solution)/shard_map/square_sum1/ppermute | solution.py:228
  16.3 9.5 %collective-permute-start.10 = (bf16[1,32,1920]{2,1,0:T(8,128)(2,1)S(1)}, bf16[1,32,1920]{2,1,0:T(8,128)(2,1)S(1)}, u32[]{:S(2)}, u32[]{:S(2)}) collective-permute-start(bf16[1,32,1920]{2,1,0:T(8,128)(2,1)S(1)} %fusion.3), channel_id=1, source_target_pairs={{0,8},{1,9},{2,10},{3,11},{4,12},{5,13},{6,14},{7,15},{8,0},{9,1},... | collective-permute-start | bytes 368648 | tf_op jit(solution)/shard_map/far_sum0/ppermute | solution.py:228
  24.1 7.2 %collective-permute-start.5 = (bf16[1,32,1920]{2,1,0:T(8,128)(2,1)S(1)}, bf16[1,32,1920]{2,1,0:T(8,128)(2,1)S(1)}, u32[]{:S(2)}, u32[]{:S(2)}) collective-permute-start(bf16[1,32,1920]{2,1,0:T(8,128)(2,1)S(1)} %fusion.2), channel_id=1, source_target_pairs={{0,8},{1,9},{2,10},{3,11},{4,12},{5,13},{6,14},{7,15},{8,0},{9,1},... | collective-permute-start | bytes 368648 | tf_op jit(solution)/shard_map/far_sum1/ppermute | solution.py:228
  25.9 7.8 %collective-permute-start.13 = (bf16[1,32,1920]{2,1,0:T(8,128)(2,1)S(1)}, bf16[1,32,1920]{2,1,0:T(8,128)(2,1)S(1)}, u32[]{:S(2)}, u32[]{:S(2)}) collective-permute-start(bf16[1,32,1920]{2,1,0:T(8,128)(2,1)S(1)} %add_convert_fusion), channel_id=1, source_target_pairs={{0,4},{1,5},{2,6},{3,7},{4,0},{5,1},{6,2},{7,3},{8,12},{9,13},{10,... | collective-permute-start | bytes 368648 | tf_op jit(solution)/shard_map/square_gather0/ppermute | solution.py:228
  28.5 9.1 %collective-permute-start.12 = (bf16[1,32,1920]{2,1,0:T(8,128)(2,1)S(1)}, bf16[1,32,1920]{2,1,0:T(8,128)(2,1)S(1)}, u32[]{:S(2)}, u32[]{:S(2)}) collective-permute-start(bf16[1,32,1920]{2,1,0:T(8,128)(2,1)S(1)} %add_convert_fusion), channel_id=1, source_target_pairs={{0,2},{1,3},{2,0},{3,1},{4,6},{5,7},{6,4},{7,5},{8,10},{9,11},{10,... | collective-permute-start | bytes 368648 | tf_op jit(solution)/shard_map/square_gather0/ppermute | solution.py:228
  29.9 7.7 %collective-permute-start.11 = (bf16[1,32,1920]{2,1,0:T(8,128)(2,1)S(1)}, bf16[1,32,1920]{2,1,0:T(8,128)(2,1)S(1)}, u32[]{:S(2)}, u32[]{:S(2)}) collective-permute-start(bf16[1,32,1920]{2,1,0:T(8,128)(2,1)S(1)} %add_convert_fusion), channel_id=1, source_target_pairs={{0,6},{1,7},{2,4},{3,5},{4,2},{5,3},{6,0},{7,1},{8,14},{9,15},{10,... | collective-permute-start | bytes 368648 | tf_op jit(solution)/shard_map/square_gather0/ppermute | solution.py:228
  31.4 8.7 %collective-permute-start.15 = (bf16[1,32,1920]{2,1,0:T(8,128)(2,1)S(1)}, bf16[1,32,1920]{2,1,0:T(8,128)(2,1)S(1)}, u32[]{:S(2)}, u32[]{:S(2)}) collective-permute-start(bf16[1,32,1920]{2,1,0:T(8,128)(2,1)S(1)} %add_convert_fusion.1), channel_id=1, source_target_pairs={{0,4},{1,5},{2,6},{3,7},{4,0},{5,1},{6,2},{7,3},{8,12},{9,13},{10,... | collective-permute-start | bytes 368648 | tf_op jit(solution)/shard_map/square_gather1/ppermute | solution.py:228
  32.1 8.2 %collective-permute-start.14 = (bf16[1,32,1920]{2,1,0:T(8,128)(2,1)S(1)}, bf16[1,32,1920]{2,1,0:T(8,128)(2,1)S(1)}, u32[]{:S(2)}, u32[]{:S(2)}) collective-permute-start(bf16[1,32,1920]{2,1,0:T(8,128)(2,1)S(1)} %add_convert_fusion.1), channel_id=1, source_target_pairs={{0,2},{1,3},{2,0},{3,1},{4,6},{5,7},{6,4},{7,5},{8,10},{9,11},{10,... | collective-permute-start | bytes 368648 | tf_op jit(solution)/shard_map/square_gather1/ppermute | solution.py:228
  33.6 6.5 %collective-permute-start.6 = (bf16[1,32,1920]{2,1,0:T(8,128)(2,1)S(1)}, bf16[1,32,1920]{2,1,0:T(8,128)(2,1)S(1)}, u32[]{:S(2)}, u32[]{:S(2)}) collective-permute-start(bf16[1,32,1920]{2,1,0:T(8,128)(2,1)S(1)} %add_convert_fusion.1), channel_id=1, source_target_pairs={{0,6},{1,7},{2,4},{3,5},{4,2},{5,3},{6,0},{7,1},{8,14},{9,15},{10,... | collective-permute-start | bytes 368648 | tf_op jit(solution)/shard_map/square_gather1/ppermute | solution.py:228
  37.6 2.9 %collective-permute-start.17 = (bf16[4,32,1920]{2,1,0:T(8,128)(2,1)S(1)}, bf16[4,32,1920]{2,1,0:T(8,128)(2,1)S(1)}, u32[]{:S(2)}, u32[]{:S(2)}) collective-permute-start(bf16[4,32,1920]{2,1,0:T(8,128)(2,1)S(1)} %pad_maximum_fusion.refs_2_), channel_id=1, source_target_pairs={{0,1},{1,0},{2,3},{3,2},{4,5},{5,4},{6,7},{7,6},{8,9},{9,8},{10,11... | collective-permute-start | bytes 1474568 | tf_op jit(solution)/shard_map/core_gather0/ppermute | solution.py:228
  40.4 1.9 %collective-permute-start.16 = (bf16[4,32,1920]{2,1,0:T(8,128)(2,1)S(1)}, bf16[4,32,1920]{2,1,0:T(8,128)(2,1)S(1)}, u32[]{:S(2)}, u32[]{:S(2)}) collective-permute-start(bf16[4,32,1920]{2,1,0:T(8,128)(2,1)S(1)} %pad_maximum_fusion.1.refs_3_), channel_id=1, source_target_pairs={{0,1},{1,0},{2,3},{3,2},{4,5},{5,4},{6,7},{7,6},{8,9},{9,8},{10,11... | collective-permute-start | bytes 1474568 | tf_op jit(solution)/shard_map/core_gather1/ppermute | solution.py:228

commit v5 on v4

--- a/solution.py
+++ b/solution.py
@@ -10,14 +10,14 @@
 NG = 16
 STREAMS = (1, 1)
 BLOCKS = 8
-SHARE = (1, 3)
+SHARE = (1, 4)
 LANES = 128
 VMEM_LIMIT = 24 * 2**20
 
 CHIPS = ("across", "x", "z", "own")
 SQUARE = (6, 2, 4)
-SUM_ORDER = (1, 2, 0)
-GATHER_ORDER = (1, 2, 0)
+SUM_ORDER = (2, 1, 0)
+GATHER_ORDER = (2, 1, 0)
 
 
 def block_of(me, place):
@@ -243,13 +243,14 @@
         parts = [total[s][i : i + 1].astype(wire) for i in SUM_ORDER]
         first[s] = parts[0]
         got[s] = [send(part, SQUARE[i], f"square_sum{s}") for i, part in zip(SUM_ORDER, parts)]
-    qmat = q_matrix(after(q_index, first[last]), phon_vectors, degeneracy)
-    total[last] = after(total[last], qmat)
-
     for s in streams:
         own = total[s][3:]
+        if s == last:
+            qmat = q_matrix(after(q_index, early), phon_vectors, degeneracy)
+            own = after(own, qmat)
         for array in got[s]:
             own = own + array.astype(full)
+        early = own.astype(wire)
         step = 8
         while step < devices:
             own = own + send(own.astype(wire), step, f"far_sum{s}").astype(full)

time: 43.7 us -> 43.2 us (0.989)
  starting transfers between devices: 21.9 us -> 21 us
  waiting for transfers between devices: 10.2 us -> 10.7 us
    ppermute x18, starting transfers between devices: 21.9 us -> 21 us  [send(): return lax.ppermute(array, 'blk', [(i, i ^ bits) for i in range(devices)])]
    ppermute x18, waiting for transfers between devices: 10.2 us -> 10.7 us  [send(): return lax.ppermute(array, 'blk', [(i, i ^ bits) for i in range(devices)])]
  transfers between devices with their start and end apart: 18 -> 18, of which waited for: 7 -> 10; matrix products, arithmetic and copies ran while one was open for 2% -> 2% of each run, Pallas kernels for 17% -> 17%
where the time goes in v5:
time: 43.2 us; the launch traced here: 43.1 us
  starting transfers between devices  21 us (49%)
  waiting for transfers between devices  10.7 us (25%)
  Pallas kernels  10.4 us (24%)
  other arithmetic  0.68 us (2%)
    ppermute x18, starting transfers between devices, send(): return lax.ppermute(array, 'blk', [(i, i ^ bits) for i in range(devices)])  21 us
    ppermute x18, waiting for transfers between devices, send(): return lax.ppermute(array, 'blk', [(i, i ^ bits) for i in range(devices)])  10.7 us
    pallas_call x3, Pallas kernels, partial_sums(): pl.pallas_call(lambda *refs: partial_kernel(pieces, given, *refs), in_spe...  6.23 us
    pallas_call x3, Pallas kernels, bloch(): pl.pallas_call(lambda *refs: bloch_kernel(places, *refs), in_specs=[pl.Bl...  3.86 us
  transfers between devices with their start and end apart: 18, of which 10 were waited for; matrix products, arithmetic and copies ran while one was open for 2% of the time, Pallas kernels for 17%

profile of v5, /device:TPU:0, one launch (start us, length us, event | category | flops | bytes accessed | tf_op | source)
XLA Modules:
  0.0 43.1 jit_solution(609403522816849519)
XLA Ops:
  0.0 2.1 %shard_map.64 = (bf16[32,128]{1,0:T(8,128)(2,1)S(1)}, bf16[4,32,1920]{2,1,0:T(8,128)(2,1)S(1)}) custom-call(s32[1]{0:T(128)} %bitcast.refs_0_, f32[1,3]{1,0:T(1,128)} %bitcast.4, s32[3,4]{1,0:T(4,128)} %refs_2_.3, bf16[4,2,16,30720]{3,2,1,0:T(8,128)(2,1)} %refs_2_.5), custom_call_target="tpu_custom_call" | custom-call | flops 62914560 | bytes 1966080 | tf_op jit(solution)/shard_map/pallas_call | solution.py:129
  2.1 0.5 %collective-permute-start = (bf16[4,32,1920]{2,1,0:T(8,128)(2,1)S(1)}, bf16[4,32,1920]{2,1,0:T(8,128)(2,1)S(1)}, u32[]{:S(2)}, u32[]{:S(2)}) collective-permute-start(bf16[4,32,1920]{2,1,0:T(8,128)(2,1)S(1)} %get-tuple-element.15), channel_id=1, source_target_pairs={{0,1},{1,0},{2,3},{3,2},{4,5},{5,4},{6,7},{7,6},{8,9},{9,8},{10,11... | collective-permute-start | bytes 1474568 | tf_op jit(solution)/shard_map/core_sum0/ppermute | solution.py:228
  2.6 2.4 %shard_map.65 = (f32[4,32,1920]{2,1,0:T(8,128)S(1)}, bf16[4,32,1920]{2,1,0:T(8,128)(2,1)S(1)}) custom-call(s32[1]{0:T(128)} %bitcast.refs_0_, bf16[32,128]{1,0:T(8,128)(2,1)S(1)} %get-tuple-element.13.refs_1_, bf16[4,2,16,30720]{3,2,1,0:T(8,128)(2,1)} %refs_2_.5), custom_call_target="tpu_custom_call" | custom-call | flops 125829120 | bytes 3932160 | tf_op jit(solution)/shard_map/pallas_call | solution.py:129
  5.0 0.2 collective-permute-start.4
  5.3 3.1 %collective-permute-start.1 = (bf16[1,32,1920]{2,1,0:T(8,128)(2,1)S(1)}, bf16[1,32,1920]{2,1,0:T(8,128)(2,1)S(1)}, u32[]{:S(2)}, u32[]{:S(2)}) collective-permute-start(bf16[1,32,1920]{2,1,0:T(8,128)(2,1)S(1)} %get-tuple-element.28), channel_id=1, source_target_pairs={{0,4},{1,5},{2,6},{3,7},{4,0},{5,1},{6,2},{7,3},{8,12},{9,13},{10,... | collective-permute-start | bytes 368648 | tf_op jit(solution)/shard_map/square_sum0/ppermute | solution.py:228
  8.5 1.4 %collective-permute-start.3 = (bf16[1,32,1920]{2,1,0:T(8,128)(2,1)S(1)}, bf16[1,32,1920]{2,1,0:T(8,128)(2,1)S(1)}, u32[]{:S(2)}, u32[]{:S(2)}) collective-permute-start(bf16[1,32,1920]{2,1,0:T(8,128)(2,1)S(1)} %get-tuple-element.29), channel_id=1, source_target_pairs={{0,6},{1,7},{2,4},{3,5},{4,2},{5,3},{6,0},{7,1},{8,14},{9,15},{10,... | collective-permute-start | bytes 368648 | tf_op jit(solution)/shard_map/square_sum0/ppermute | solution.py:228
  10.0 1.7 %shard_map.67 = f32[4,32,1920]{2,1,0:T(8,128)S(1)} custom-call(s32[1]{0:T(128)} %bitcast.refs_0_, bf16[32,128]{1,0:T(8,128)(2,1)S(1)} %get-tuple-element.13.refs_1_, bf16[4,2,16,30720]{3,2,1,0:T(8,128)(2,1)} %refs_2_.5), custom_call_target="tpu_custom_call" | custom-call | flops 62914560 | bytes 1966080 | tf_op jit(solution)/shard_map/pallas_call | solution.py:129
  12.0 2.0 %collective-permute-start.5 = (bf16[1,32,1920]{2,1,0:T(8,128)(2,1)S(1)}, bf16[1,32,1920]{2,1,0:T(8,128)(2,1)S(1)}, u32[]{:S(2)}, u32[]{:S(2)}) collective-permute-start(bf16[1,32,1920]{2,1,0:T(8,128)(2,1)S(1)} %get-tuple-element.25), channel_id=1, source_target_pairs={{0,4},{1,5},{2,6},{3,7},{4,0},{5,1},{6,2},{7,3},{8,12},{9,13},{10,... | collective-permute-start | bytes 368648 | tf_op jit(solution)/shard_map/square_sum1/ppermute | solution.py:228
  14.0 1.4 %collective-permute-start.7 = (bf16[1,32,1920]{2,1,0:T(8,128)(2,1)S(1)}, bf16[1,32,1920]{2,1,0:T(8,128)(2,1)S(1)}, u32[]{:S(2)}, u32[]{:S(2)}) collective-permute-start(bf16[1,32,1920]{2,1,0:T(8,128)(2,1)S(1)} %get-tuple-element.26), channel_id=1, source_target_pairs={{0,6},{1,7},{2,4},{3,5},{4,2},{5,3},{6,0},{7,1},{8,14},{9,15},{10,... | collective-permute-start | bytes 368648 | tf_op jit(solution)/shard_map/square_sum1/ppermute | solution.py:228
  15.4 1.0 %collective-permute-done.3 = bf16[1,32,1920]{2,1,0:T(8,128)(2,1)S(1)} collective-permute-done((bf16[1,32,1920]{2,1,0:T(8,128)(2,1)S(1)}, bf16[1,32,1920]{2,1,0:T(8,128)(2,1)S(1)}, u32[]{:S(2)}, u32[]{:S(2)}) %collective-permute-start.3) | collective-permute-done | bytes 122912 | tf_op jit(solution)/shard_map/square_sum0/ppermute | solution.py:228
  16.4 0.3 collective-permute-start.6
  16.7 0.5 %collective-permute-done.2 = bf16[1,32,1920]{2,1,0:T(8,128)(2,1)S(1)} collective-permute-done((bf16[1,32,1920]{2,1,0:T(8,128)(2,1)S(1)}, bf16[1,32,1920]{2,1,0:T(8,128)(2,1)S(1)}, u32[]{:S(2)}, u32[]{:S(2)}) %collective-permute-start.2) | collective-permute-done | bytes 122912 | tf_op jit(solution)/shard_map/square_sum0/ppermute | solution.py:228
  17.3 2.7 %collective-permute-start.10 = (bf16[1,32,1920]{2,1,0:T(8,128)(2,1)S(1)}, bf16[1,32,1920]{2,1,0:T(8,128)(2,1)S(1)}, u32[]{:S(2)}, u32[]{:S(2)}) collective-permute-start(bf16[1,32,1920]{2,1,0:T(8,128)(2,1)S(1)} %fusion.3), channel_id=1, source_target_pairs={{0,8},{1,9},{2,10},{3,11},{4,12},{5,13},{6,14},{7,15},{8,0},{9,1},... | collective-permute-start | bytes 368648 | tf_op jit(solution)/shard_map/far_sum0/ppermute | solution.py:228
  19.9 0.3 shard_map.66.refs_1_
  20.3 2.2 %collective-permute-done.7 = bf16[1,32,1920]{2,1,0:T(8,128)(2,1)S(1)} collective-permute-done((bf16[1,32,1920]{2,1,0:T(8,128)(2,1)S(1)}, bf16[1,32,1920]{2,1,0:T(8,128)(2,1)S(1)}, u32[]{:S(2)}, u32[]{:S(2)}) %collective-permute-start.7) | collective-permute-done | bytes 122912 | tf_op jit(solution)/shard_map/square_sum1/ppermute | solution.py:228
  22.5 0.2 collective-permute-done.6
  22.7 2.7 %collective-permute-start.8 = (bf16[1,32,1920]{2,1,0:T(8,128)(2,1)S(1)}, bf16[1,32,1920]{2,1,0:T(8,128)(2,1)S(1)}, u32[]{:S(2)}, u32[]{:S(2)}) collective-permute-start(bf16[1,32,1920]{2,1,0:T(8,128)(2,1)S(1)} %fusion.2), channel_id=1, source_target_pairs={{0,8},{1,9},{2,10},{3,11},{4,12},{5,13},{6,14},{7,15},{8,0},{9,1},... | collective-permute-start | bytes 368648 | tf_op jit(solution)/shard_map/far_sum1/ppermute | solution.py:228
  25.4 1.8 %collective-permute-done.10 = bf16[1,32,1920]{2,1,0:T(8,128)(2,1)S(1)} collective-permute-done((bf16[1,32,1920]{2,1,0:T(8,128)(2,1)S(1)}, bf16[1,32,1920]{2,1,0:T(8,128)(2,1)S(1)}, u32[]{:S(2)}, u32[]{:S(2)}) %collective-permute-start.10) | collective-permute-done | bytes 122912 | tf_op jit(solution)/shard_map/far_sum0/ppermute | solution.py:228
  27.2 0.7 %collective-permute-start.13 = (bf16[1,32,1920]{2,1,0:T(8,128)(2,1)S(1)}, bf16[1,32,1920]{2,1,0:T(8,128)(2,1)S(1)}, u32[]{:S(2)}, u32[]{:S(2)}) collective-permute-start(bf16[1,32,1920]{2,1,0:T(8,128)(2,1)S(1)} %add_convert_fusion), channel_id=1, source_target_pairs={{0,4},{1,5},{2,6},{3,7},{4,0},{5,1},{6,2},{7,3},{8,12},{9,13},{10,... | collective-permute-start | bytes 368648 | tf_op jit(solution)/shard_map/square_gather0/ppermute | solution.py:228
  28.0 0.6 %collective-permute-start.12 = (bf16[1,32,1920]{2,1,0:T(8,128)(2,1)S(1)}, bf16[1,32,1920]{2,1,0:T(8,128)(2,1)S(1)}, u32[]{:S(2)}, u32[]{:S(2)}) collective-permute-start(bf16[1,32,1920]{2,1,0:T(8,128)(2,1)S(1)} %add_convert_fusion), channel_id=1, source_target_pairs={{0,2},{1,3},{2,0},{3,1},{4,6},{5,7},{6,4},{7,5},{8,10},{9,11},{10,... | collective-permute-start | bytes 368648 | tf_op jit(solution)/shard_map/square_gather0/ppermute | solution.py:228
  28.5 2.2 %collective-permute-start.11 = (bf16[1,32,1920]{2,1,0:T(8,128)(2,1)S(1)}, bf16[1,32,1920]{2,1,0:T(8,128)(2,1)S(1)}, u32[]{:S(2)}, u32[]{:S(2)}) collective-permute-start(bf16[1,32,1920]{2,1,0:T(8,128)(2,1)S(1)} %add_convert_fusion), channel_id=1, source_target_pairs={{0,6},{1,7},{2,4},{3,5},{4,2},{5,3},{6,0},{7,1},{8,14},{9,15},{10,... | collective-permute-start | bytes 368648 | tf_op jit(solution)/shard_map/square_gather0/ppermute | solution.py:228
  30.8 0.7 %collective-permute-start.15 = (bf16[1,32,1920]{2,1,0:T(8,128)(2,1)S(1)}, bf16[1,32,1920]{2,1,0:T(8,128)(2,1)S(1)}, u32[]{:S(2)}, u32[]{:S(2)}) collective-permute-start(bf16[1,32,1920]{2,1,0:T(8,128)(2,1)S(1)} %add_convert_fusion.1), channel_id=1, source_target_pairs={{0,4},{1,5},{2,6},{3,7},{4,0},{5,1},{6,2},{7,3},{8,12},{9,13},{10,... | collective-permute-start | bytes 368648 | tf_op jit(solution)/shard_map/square_gather1/ppermute | solution.py:228
  31.6 0.6 %collective-permute-start.14 = (bf16[1,32,1920]{2,1,0:T(8,128)(2,1)S(1)}, bf16[1,32,1920]{2,1,0:T(8,128)(2,1)S(1)}, u32[]{:S(2)}, u32[]{:S(2)}) collective-permute-start(bf16[1,32,1920]{2,1,0:T(8,128)(2,1)S(1)} %add_convert_fusion.1), channel_id=1, source_target_pairs={{0,2},{1,3},{2,0},{3,1},{4,6},{5,7},{6,4},{7,5},{8,10},{9,11},{10,... | collective-permute-start | bytes 368648 | tf_op jit(solution)/shard_map/square_gather1/ppermute | solution.py:228
  32.2 0.6 %collective-permute-done.13 = bf16[1,32,1920]{2,1,0:T(8,128)(2,1)S(1)} collective-permute-done((bf16[1,32,1920]{2,1,0:T(8,128)(2,1)S(1)}, bf16[1,32,1920]{2,1,0:T(8,128)(2,1)S(1)}, u32[]{:S(2)}, u32[]{:S(2)}) %collective-permute-start.13) | collective-permute-done | bytes 122912 | tf_op jit(solution)/shard_map/square_gather0/ppermute | solution.py:228
  32.7 1.7 %collective-permute-start.9 = (bf16[1,32,1920]{2,1,0:T(8,128)(2,1)S(1)}, bf16[1,32,1920]{2,1,0:T(8,128)(2,1)S(1)}, u32[]{:S(2)}, u32[]{:S(2)}) collective-permute-start(bf16[1,32,1920]{2,1,0:T(8,128)(2,1)S(1)} %add_convert_fusion.1), channel_id=1, source_target_pairs={{0,6},{1,7},{2,4},{3,5},{4,2},{5,3},{6,0},{7,1},{8,14},{9,15},{10,... | collective-permute-start | bytes 368648 | tf_op jit(solution)/shard_map/square_gather1/ppermute | solution.py:228
  34.4 0.3 collective-permute-done.12
  34.7 0.5 %collective-permute-done.11 = bf16[1,32,1920]{2,1,0:T(8,128)(2,1)S(1)} collective-permute-done((bf16[1,32,1920]{2,1,0:T(8,128)(2,1)S(1)}, bf16[1,32,1920]{2,1,0:T(8,128)(2,1)S(1)}, u32[]{:S(2)}, u32[]{:S(2)}) %collective-permute-start.11) | collective-permute-done | bytes 122912 | tf_op jit(solution)/shard_map/square_gather0/ppermute | solution.py:228
  35.4 1.2 %shard_map.68.refs_4_ = bf16[2,32,30720]{2,1,0:T(8,128)(2,1)} custom-call(s32[1]{0:T(128)} %bitcast.refs_0_, bf16[64,32]{1,0:T(8,128)(2,1)S(1)} %shard_map.66.refs_1_, bf16[4,32,1920]{2,1,0:T(8,128)(2,1)S(1)} %pad_maximum_fusion.refs_2_), custom_call_target="tpu_custom_call" | custom-call | flops 31457280 | bytes 983040 | tf_op jit(solution)/shard_map/pallas_call | solution.py:198
  36.5 3.4 %collective-permute-done.9 = bf16[1,32,1920]{2,1,0:T(8,128)(2,1)S(1)} collective-permute-done((bf16[1,32,1920]{2,1,0:T(8,128)(2,1)S(1)}, bf16[1,32,1920]{2,1,0:T(8,128)(2,1)S(1)}, u32[]{:S(2)}, u32[]{:S(2)}) %collective-permute-start.9) | collective-permute-done | bytes 122912 | tf_op jit(solution)/shard_map/square_gather1/ppermute | solution.py:228
  40.1 1.5 %shard_map.69.refs_3_ = bf16[2,32,30720]{2,1,0:T(8,128)(2,1)} custom-call(s32[1]{0:T(128)} %bitcast.refs_0_, bf16[64,32]{1,0:T(8,128)(2,1)S(1)} %shard_map.66.refs_1_, bf16[4,32,1920]{2,1,0:T(8,128)(2,1)S(1)} %collective-permute-done.17.refs_2_, bf16[4,32,1920]{2,1,0:T(8,128)(2,1)S(1)} %pad_maximum_fusion.1.refs_3_, ...), custom_call_target="tpu_custom_call", output_to_operand_aliasing={{}: (4, {})} | custom-call | flops 62914560 | bytes 1966080 | tf_op jit(solution)/shard_map/pallas_call | solution.py:198
  41.6 0.3 collective-permute-done.16.refs_2_
  41.9 1.2 %shard_map.70 = bf16[2,32,30720]{2,1,0:T(8,128)(2,1)} custom-call(s32[1]{0:T(128)} %bitcast.refs_0_, bf16[64,32]{1,0:T(8,128)(2,1)S(1)} %shard_map.66.refs_1_, bf16[4,32,1920]{2,1,0:T(8,128)(2,1)S(1)} %collective-permute-done.16.refs_2_, bf16[2,32,30720]{2,1,0:T(8,128)(2,1)} %shard_map.69.refs_3_), custom_call_target="tpu_custom_call", output_to_operand_aliasing={{}: (3, {})} | custom-call | flops 31457280 | bytes 983040 | tf_op jit(solution)/shard_map/pallas_call | solution.py:198
  (28 shorter events, 1.1 us)
Async XLA Ops:
  2.1 3.0 %collective-permute-start = (bf16[4,32,1920]{2,1,0:T(8,128)(2,1)S(1)}, bf16[4,32,1920]{2,1,0:T(8,128)(2,1)S(1)}, u32[]{:S(2)}, u32[]{:S(2)}) collective-permute-start(bf16[4,32,1920]{2,1,0:T(8,128)(2,1)S(1)} %get-tuple-element.15), channel_id=1, source_target_pairs={{0,1},{1,0},{2,3},{3,2},{4,5},{5,4},{6,7},{7,6},{8,9},{9,8},{10,11... | collective-permute-start | bytes 1474568 | tf_op jit(solution)/shard_map/core_sum0/ppermute | solution.py:228
  5.0 6.8 %collective-permute-start.4 = (bf16[4,32,1920]{2,1,0:T(8,128)(2,1)S(1)}, bf16[4,32,1920]{2,1,0:T(8,128)(2,1)S(1)}, u32[]{:S(2)}, u32[]{:S(2)}) collective-permute-start(bf16[4,32,1920]{2,1,0:T(8,128)(2,1)S(1)} %get-tuple-element.18), channel_id=1, source_target_pairs={{0,1},{1,0},{2,3},{3,2},{4,5},{5,4},{6,7},{7,6},{8,9},{9,8},{10,11... | collective-permute-start | bytes 1474568 | tf_op jit(solution)/shard_map/core_sum1/ppermute | solution.py:228
  5.3 11.9 %collective-permute-start.1 = (bf16[1,32,1920]{2,1,0:T(8,128)(2,1)S(1)}, bf16[1,32,1920]{2,1,0:T(8,128)(2,1)S(1)}, u32[]{:S(2)}, u32[]{:S(2)}) collective-permute-start(bf16[1,32,1920]{2,1,0:T(8,128)(2,1)S(1)} %get-tuple-element.28), channel_id=1, source_target_pairs={{0,4},{1,5},{2,6},{3,7},{4,0},{5,1},{6,2},{7,3},{8,12},{9,13},{10,... | collective-permute-start | bytes 368648 | tf_op jit(solution)/shard_map/square_sum0/ppermute | solution.py:228
  8.5 7.9 %collective-permute-start.3 = (bf16[1,32,1920]{2,1,0:T(8,128)(2,1)S(1)}, bf16[1,32,1920]{2,1,0:T(8,128)(2,1)S(1)}, u32[]{:S(2)}, u32[]{:S(2)}) collective-permute-start(bf16[1,32,1920]{2,1,0:T(8,128)(2,1)S(1)} %get-tuple-element.29), channel_id=1, source_target_pairs={{0,6},{1,7},{2,4},{3,5},{4,2},{5,3},{6,0},{7,1},{8,14},{9,15},{10,... | collective-permute-start | bytes 368648 | tf_op jit(solution)/shard_map/square_sum0/ppermute | solution.py:228
  9.9 7.3 %collective-permute-start.2 = (bf16[1,32,1920]{2,1,0:T(8,128)(2,1)S(1)}, bf16[1,32,1920]{2,1,0:T(8,128)(2,1)S(1)}, u32[]{:S(2)}, u32[]{:S(2)}) collective-permute-start(bf16[1,32,1920]{2,1,0:T(8,128)(2,1)S(1)} %get-tuple-element.30), channel_id=1, source_target_pairs={{0,2},{1,3},{2,0},{3,1},{4,6},{5,7},{6,4},{7,5},{8,10},{9,11},{10,... | collective-permute-start | bytes 368648 | tf_op jit(solution)/shard_map/square_sum0/ppermute | solution.py:228
  11.7 8.2 %copy-start = (s32[3,32]{1,0:T(4,128)S(1)}, s32[3,32]{1,0:T(4,128)}, u32[]{:S(2)}) copy-start(s32[3,32]{1,0:T(4,128)} %q_ref) | copy-start | bytes 1156
  11.7 8.2 %copy-start.1 = (s32[3,16]{1,0:T(4,128)S(1)}, s32[3,16]{1,0:T(4,128)}, u32[]{:S(2)}) copy-start(s32[3,16]{1,0:T(4,128)} %phon_ref.1) | copy-start | bytes 580
  11.8 8.2 %copy-start.2 = (s32[16]{0:T(128)S(1)}, s32[16]{0:T(128)}, u32[]{:S(2)}) copy-start(s32[16]{0:T(128)} %param.9) | copy-start | bytes 196
  12.0 8.3 %collective-permute-start.5 = (bf16[1,32,1920]{2,1,0:T(8,128)(2,1)S(1)}, bf16[1,32,1920]{2,1,0:T(8,128)(2,1)S(1)}, u32[]{:S(2)}, u32[]{:S(2)}) collective-permute-start(bf16[1,32,1920]{2,1,0:T(8,128)(2,1)S(1)} %get-tuple-element.25), channel_id=1, source_target_pairs={{0,4},{1,5},{2,6},{3,7},{4,0},{5,1},{6,2},{7,3},{8,12},{9,13},{10,... | collective-permute-start | bytes 368648 | tf_op jit(solution)/shard_map/square_sum1/ppermute | solution.py:228
  14.0 8.5 %collective-permute-start.7 = (bf16[1,32,1920]{2,1,0:T(8,128)(2,1)S(1)}, bf16[1,32,1920]{2,1,0:T(8,128)(2,1)S(1)}, u32[]{:S(2)}, u32[]{:S(2)}) collective-permute-start(bf16[1,32,1920]{2,1,0:T(8,128)(2,1)S(1)} %get-tuple-element.26), channel_id=1, source_target_pairs={{0,6},{1,7},{2,4},{3,5},{4,2},{5,3},{6,0},{7,1},{8,14},{9,15},{10,... | collective-permute-start | bytes 368648 | tf_op jit(solution)/shard_map/square_sum1/ppermute | solution.py:228
  16.4 6.3 %collective-permute-start.6 = (bf16[1,32,1920]{2,1,0:T(8,128)(2,1)S(1)}, bf16[1,32,1920]{2,1,0:T(8,128)(2,1)S(1)}, u32[]{:S(2)}, u32[]{:S(2)}) collective-permute-start(bf16[1,32,1920]{2,1,0:T(8,128)(2,1)S(1)} %get-tuple-element.27), channel_id=1, source_target_pairs={{0,2},{1,3},{2,0},{3,1},{4,6},{5,7},{6,4},{7,5},{8,10},{9,11},{10,... | collective-permute-start | bytes 368648 | tf_op jit(solution)/shard_map/square_sum1/ppermute | solution.py:228
  17.3 9.8 %collective-permute-start.10 = (bf16[1,32,1920]{2,1,0:T(8,128)(2,1)S(1)}, bf16[1,32,1920]{2,1,0:T(8,128)(2,1)S(1)}, u32[]{:S(2)}, u32[]{:S(2)}) collective-permute-start(bf16[1,32,1920]{2,1,0:T(8,128)(2,1)S(1)} %fusion.3), channel_id=1, source_target_pairs={{0,8},{1,9},{2,10},{3,11},{4,12},{5,13},{6,14},{7,15},{8,0},{9,1},... | collective-permute-start | bytes 368648 | tf_op jit(solution)/shard_map/far_sum0/ppermute | solution.py:228
  22.7 8.0 %collective-permute-start.8 = (bf16[1,32,1920]{2,1,0:T(8,128)(2,1)S(1)}, bf16[1,32,1920]{2,1,0:T(8,128)(2,1)S(1)}, u32[]{:S(2)}, u32[]{:S(2)}) collective-permute-start(bf16[1,32,1920]{2,1,0:T(8,128)(2,1)S(1)} %fusion.2), channel_id=1, source_target_pairs={{0,8},{1,9},{2,10},{3,11},{4,12},{5,13},{6,14},{7,15},{8,0},{9,1},... | collective-permute-start | bytes 368648 | tf_op jit(solution)/shard_map/far_sum1/ppermute | solution.py:228
  27.2 5.5 %collective-permute-start.13 = (bf16[1,32,1920]{2,1,0:T(8,128)(2,1)S(1)}, bf16[1,32,1920]{2,1,0:T(8,128)(2,1)S(1)}, u32[]{:S(2)}, u32[]{:S(2)}) collective-permute-start(bf16[1,32,1920]{2,1,0:T(8,128)(2,1)S(1)} %add_convert_fusion), channel_id=1, source_target_pairs={{0,4},{1,5},{2,6},{3,7},{4,0},{5,1},{6,2},{7,3},{8,12},{9,13},{10,... | collective-permute-start | bytes 368648 | tf_op jit(solution)/shard_map/square_gather0/ppermute | solution.py:228
  28.0 6.7 %collective-permute-start.12 = (bf16[1,32,1920]{2,1,0:T(8,128)(2,1)S(1)}, bf16[1,32,1920]{2,1,0:T(8,128)(2,1)S(1)}, u32[]{:S(2)}, u32[]{:S(2)}) collective-permute-start(bf16[1,32,1920]{2,1,0:T(8,128)(2,1)S(1)} %add_convert_fusion), channel_id=1, source_target_pairs={{0,2},{1,3},{2,0},{3,1},{4,6},{5,7},{6,4},{7,5},{8,10},{9,11},{10,... | collective-permute-start | bytes 368648 | tf_op jit(solution)/shard_map/square_gather0/ppermute | solution.py:228
  28.5 6.7 %collective-permute-start.11 = (bf16[1,32,1920]{2,1,0:T(8,128)(2,1)S(1)}, bf16[1,32,1920]{2,1,0:T(8,128)(2,1)S(1)}, u32[]{:S(2)}, u32[]{:S(2)}) collective-permute-start(bf16[1,32,1920]{2,1,0:T(8,128)(2,1)S(1)} %add_convert_fusion), channel_id=1, source_target_pairs={{0,6},{1,7},{2,4},{3,5},{4,2},{5,3},{6,0},{7,1},{8,14},{9,15},{10,... | collective-permute-start | bytes 368648 | tf_op jit(solution)/shard_map/square_gather0/ppermute | solution.py:228
  30.8 9.1 %collective-permute-start.15 = (bf16[1,32,1920]{2,1,0:T(8,128)(2,1)S(1)}, bf16[1,32,1920]{2,1,0:T(8,128)(2,1)S(1)}, u32[]{:S(2)}, u32[]{:S(2)}) collective-permute-start(bf16[1,32,1920]{2,1,0:T(8,128)(2,1)S(1)} %add_convert_fusion.1), channel_id=1, source_target_pairs={{0,4},{1,5},{2,6},{3,7},{4,0},{5,1},{6,2},{7,3},{8,12},{9,13},{10,... | collective-permute-start | bytes 368648 | tf_op jit(solution)/shard_map/square_gather1/ppermute | solution.py:228
  31.6 8.3 %collective-permute-start.14 = (bf16[1,32,1920]{2,1,0:T(8,128)(2,1)S(1)}, bf16[1,32,1920]{2,1,0:T(8,128)(2,1)S(1)}, u32[]{:S(2)}, u32[]{:S(2)}) collective-permute-start(bf16[1,32,1920]{2,1,0:T(8,128)(2,1)S(1)} %add_convert_fusion.1), channel_id=1, source_target_pairs={{0,2},{1,3},{2,0},{3,1},{4,6},{5,7},{6,4},{7,5},{8,10},{9,11},{10,... | collective-permute-start | bytes 368648 | tf_op jit(solution)/shard_map/square_gather1/ppermute | solution.py:228
  32.7 7.2 %collective-permute-start.9 = (bf16[1,32,1920]{2,1,0:T(8,128)(2,1)S(1)}, bf16[1,32,1920]{2,1,0:T(8,128)(2,1)S(1)}, u32[]{:S(2)}, u32[]{:S(2)}) collective-permute-start(bf16[1,32,1920]{2,1,0:T(8,128)(2,1)S(1)} %add_convert_fusion.1), channel_id=1, source_target_pairs={{0,6},{1,7},{2,4},{3,5},{4,2},{5,3},{6,0},{7,1},{8,14},{9,15},{10,... | collective-permute-start | bytes 368648 | tf_op jit(solution)/shard_map/square_gather1/ppermute | solution.py:228
  35.3 4.8 %collective-permute-start.17 = (bf16[4,32,1920]{2,1,0:T(8,128)(2,1)S(1)}, bf16[4,32,1920]{2,1,0:T(8,128)(2,1)S(1)}, u32[]{:S(2)}, u32[]{:S(2)}) collective-permute-start(bf16[4,32,1920]{2,1,0:T(8,128)(2,1)S(1)} %pad_maximum_fusion.refs_2_), channel_id=1, source_target_pairs={{0,1},{1,0},{2,3},{3,2},{4,5},{5,4},{6,7},{7,6},{8,9},{9,8},{10,11... | collective-permute-start | bytes 1474568 | tf_op jit(solution)/shard_map/core_gather0/ppermute | solution.py:228
  40.0 1.9 %collective-permute-start.16 = (bf16[4,32,1920]{2,1,0:T(8,128)(2,1)S(1)}, bf16[4,32,1920]{2,1,0:T(8,128)(2,1)S(1)}, u32[]{:S(2)}, u32[]{:S(2)}) collective-permute-start(bf16[4,32,1920]{2,1,0:T(8,128)(2,1)S(1)} %pad_maximum_fusion.1.refs_3_), channel_id=1, source_target_pairs={{0,1},{1,0},{2,3},{3,2},{4,5},{5,4},{6,7},{7,6},{8,9},{9,8},{10,11... | collective-permute-start | bytes 1474568 | tf_op jit(solution)/shard_map/core_gather1/ppermute | solution.py:228

commit v6 on v5

--- a/solution.py
+++ b/solution.py
@@ -16,13 +16,14 @@
 
 CHIPS = ("across", "x", "z", "own")
 SQUARE = (6, 2, 4)
-SUM_ORDER = (2, 1, 0)
-GATHER_ORDER = (2, 1, 0)
-
-
-def block_of(me, place):
+SUM_ORDER = (2, 0, 1)
+GATHER_ORDER = (2, 0, 1)
+MIRROR = (0, 1)
+
+
+def block_of(me, place, stream):
     other, chip = place
-    core, x, z = me % 2, (me // 2) % 2, (me // 4) % 2
+    core, x, z = me % 2, (me // 2) % 2, (me // 4 + MIRROR[stream] * (me // 8)) % 2
     flip_x, flip_z = {"across": (1, 1), "x": (1, 0), "z": (0, 1), "own": (0, 0)}[chip]
     return (core + other) % 2 * 4 + (x + flip_x) % 2 * 2 + (z + flip_z) % 2
 
@@ -34,7 +35,7 @@
 
 def columns_at(me, place, stream, width):
     start, columns = stream_columns(width, stream)
-    start = start + block_of(me, place) * columns
+    start = start + block_of(me, place, stream) * columns
     return pl.ds(pl.multiple_of(start, 128), columns)
 
 
@@ -253,7 +254,7 @@
         early = own.astype(wire)
         step = 8
         while step < devices:
-            own = own + send(own.astype(wire), step, f"far_sum{s}").astype(full)
+            own = own + send(own.astype(wire), step + 4 * MIRROR[s] * (step == 8), f"far_sum{s}").astype(full)
             step *= 2
         block[s] = own.astype(wire)
 

time: 43.2 us -> 42.6 us (0.986)
  waiting for transfers between devices: 10.7 us -> 7.19 us
  starting transfers between devices: 21 us -> 23.9 us
    ppermute x18, waiting for transfers between devices: 10.7 us -> 7.19 us  [send(): return lax.ppermute(array, 'blk', [(i, i ^ bits) for i in range(devices)])]
    ppermute x18, starting transfers between devices: 21 us -> 23.9 us  [send(): return lax.ppermute(array, 'blk', [(i, i ^ bits) for i in range(devices)])]
  transfers between devices with their start and end apart: 18 -> 18, of which waited for: 10 -> 7; matrix products, arithmetic and copies ran while one was open for 2% -> 2% of each run, Pallas kernels for 17% -> 17%
where the time goes in v6:
time: 42.6 us; the launch traced here: 42.5 us
  starting transfers between devices  23.9 us (56%)
  Pallas kernels  10.4 us (24%)
  waiting for transfers between devices  7.19 us (17%)
  other arithmetic  0.68 us (2%)
    ppermute x18, starting transfers between devices, send(): return lax.ppermute(array, 'blk', [(i, i ^ bits) for i in range(devices)])  23.9 us
    ppermute x18, waiting for transfers between devices, send(): return lax.ppermute(array, 'blk', [(i, i ^ bits) for i in range(devices)])  7.19 us
    pallas_call x3, Pallas kernels, partial_sums(): pl.pallas_call(lambda *refs: partial_kernel(pieces, given, *refs), in_spe...  6.23 us
    pallas_call x3, Pallas kernels, bloch(): pl.pallas_call(lambda *refs: bloch_kernel(places, *refs), in_specs=[pl.Bl...  3.86 us
  transfers between devices with their start and end apart: 18, of which 7 were waited for; matrix products, arithmetic and copies ran while one was open for 2% of the time, Pallas kernels for 17%

profile of v6, /device:TPU:0, one launch (start us, length us, event | category | flops | bytes accessed | tf_op | source)
XLA Modules:
  0.0 42.5 jit_solution(4272901985317206640)
XLA Ops:
  0.0 2.1 %shard_map.64 = (bf16[32,128]{1,0:T(8,128)(2,1)S(1)}, bf16[4,32,1920]{2,1,0:T(8,128)(2,1)S(1)}) custom-call(s32[1]{0:T(128)} %bitcast.refs_0_, f32[1,3]{1,0:T(1,128)} %bitcast.4, s32[3,4]{1,0:T(4,128)} %refs_2_.3, bf16[4,2,16,30720]{3,2,1,0:T(8,128)(2,1)} %refs_2_.5), custom_call_target="tpu_custom_call" | custom-call | flops 62914560 | bytes 1966080 | tf_op jit(solution)/shard_map/pallas_call | solution.py:130
  2.1 0.5 %collective-permute-start = (bf16[4,32,1920]{2,1,0:T(8,128)(2,1)S(1)}, bf16[4,32,1920]{2,1,0:T(8,128)(2,1)S(1)}, u32[]{:S(2)}, u32[]{:S(2)}) collective-permute-start(bf16[4,32,1920]{2,1,0:T(8,128)(2,1)S(1)} %get-tuple-element.15), channel_id=1, source_target_pairs={{0,1},{1,0},{2,3},{3,2},{4,5},{5,4},{6,7},{7,6},{8,9},{9,8},{10,11... | collective-permute-start | bytes 1474568 | tf_op jit(solution)/shard_map/core_sum0/ppermute | solution.py:229
  2.6 2.4 %shard_map.65 = (f32[4,32,1920]{2,1,0:T(8,128)S(1)}, bf16[4,32,1920]{2,1,0:T(8,128)(2,1)S(1)}) custom-call(s32[1]{0:T(128)} %bitcast.refs_0_, bf16[32,128]{1,0:T(8,128)(2,1)S(1)} %get-tuple-element.13.refs_1_, bf16[4,2,16,30720]{3,2,1,0:T(8,128)(2,1)} %refs_2_.5), custom_call_target="tpu_custom_call" | custom-call | flops 125829120 | bytes 3932160 | tf_op jit(solution)/shard_map/pallas_call | solution.py:130
  5.0 0.2 collective-permute-start.4
  5.2 0.1 fusion.5
  5.3 3.1 %collective-permute-start.1 = (bf16[1,32,1920]{2,1,0:T(8,128)(2,1)S(1)}, bf16[1,32,1920]{2,1,0:T(8,128)(2,1)S(1)}, u32[]{:S(2)}, u32[]{:S(2)}) collective-permute-start(bf16[1,32,1920]{2,1,0:T(8,128)(2,1)S(1)} %get-tuple-element.28), channel_id=1, source_target_pairs={{0,4},{1,5},{2,6},{3,7},{4,0},{5,1},{6,2},{7,3},{8,12},{9,13},{10,... | collective-permute-start | bytes 368648 | tf_op jit(solution)/shard_map/square_sum0/ppermute | solution.py:229
  8.5 1.5 %collective-permute-start.3 = (bf16[1,32,1920]{2,1,0:T(8,128)(2,1)S(1)}, bf16[1,32,1920]{2,1,0:T(8,128)(2,1)S(1)}, u32[]{:S(2)}, u32[]{:S(2)}) collective-permute-start(bf16[1,32,1920]{2,1,0:T(8,128)(2,1)S(1)} %get-tuple-element.29), channel_id=1, source_target_pairs={{0,2},{1,3},{2,0},{3,1},{4,6},{5,7},{6,4},{7,5},{8,10},{9,11},{10,... | collective-permute-start | bytes 368648 | tf_op jit(solution)/shard_map/square_sum0/ppermute | solution.py:229
  10.0 1.7 %shard_map.67 = f32[4,32,1920]{2,1,0:T(8,128)S(1)} custom-call(s32[1]{0:T(128)} %bitcast.refs_0_, bf16[32,128]{1,0:T(8,128)(2,1)S(1)} %get-tuple-element.13.refs_1_, bf16[4,2,16,30720]{3,2,1,0:T(8,128)(2,1)} %refs_2_.5), custom_call_target="tpu_custom_call" | custom-call | flops 62914560 | bytes 1966080 | tf_op jit(solution)/shard_map/pallas_call | solution.py:130
  11.8 0.1 fusion.4
  12.0 2.0 %collective-permute-start.5 = (bf16[1,32,1920]{2,1,0:T(8,128)(2,1)S(1)}, bf16[1,32,1920]{2,1,0:T(8,128)(2,1)S(1)}, u32[]{:S(2)}, u32[]{:S(2)}) collective-permute-start(bf16[1,32,1920]{2,1,0:T(8,128)(2,1)S(1)} %get-tuple-element.25), channel_id=1, source_target_pairs={{0,4},{1,5},{2,6},{3,7},{4,0},{5,1},{6,2},{7,3},{8,12},{9,13},{10,... | collective-permute-start | bytes 368648 | tf_op jit(solution)/shard_map/square_sum1/ppermute | solution.py:229
  14.0 1.5 %collective-permute-start.7 = (bf16[1,32,1920]{2,1,0:T(8,128)(2,1)S(1)}, bf16[1,32,1920]{2,1,0:T(8,128)(2,1)S(1)}, u32[]{:S(2)}, u32[]{:S(2)}) collective-permute-start(bf16[1,32,1920]{2,1,0:T(8,128)(2,1)S(1)} %get-tuple-element.26), channel_id=1, source_target_pairs={{0,2},{1,3},{2,0},{3,1},{4,6},{5,7},{6,4},{7,5},{8,10},{9,11},{10,... | collective-permute-start | bytes 368648 | tf_op jit(solution)/shard_map/square_sum1/ppermute | solution.py:229
  15.5 0.3 collective-permute-done.3
  15.7 1.4 %collective-permute-start.6 = (bf16[1,32,1920]{2,1,0:T(8,128)(2,1)S(1)}, bf16[1,32,1920]{2,1,0:T(8,128)(2,1)S(1)}, u32[]{:S(2)}, u32[]{:S(2)}) collective-permute-start(bf16[1,32,1920]{2,1,0:T(8,128)(2,1)S(1)} %get-tuple-element.27), channel_id=1, source_target_pairs={{0,6},{1,7},{2,4},{3,5},{4,2},{5,3},{6,0},{7,1},{8,14},{9,15},{10,... | collective-permute-start | bytes 368648 | tf_op jit(solution)/shard_map/square_sum1/ppermute | solution.py:229
  17.2 2.7 %collective-permute-start.10 = (bf16[1,32,1920]{2,1,0:T(8,128)(2,1)S(1)}, bf16[1,32,1920]{2,1,0:T(8,128)(2,1)S(1)}, u32[]{:S(2)}, u32[]{:S(2)}) collective-permute-start(bf16[1,32,1920]{2,1,0:T(8,128)(2,1)S(1)} %fusion.3), channel_id=1, source_target_pairs={{0,8},{1,9},{2,10},{3,11},{4,12},{5,13},{6,14},{7,15},{8,0},{9,1},... | collective-permute-start | bytes 368648 | tf_op jit(solution)/shard_map/far_sum0/ppermute | solution.py:229
  19.9 0.3 shard_map.66.refs_1_
  20.3 2.2 %collective-permute-done.6 = bf16[1,32,1920]{2,1,0:T(8,128)(2,1)S(1)} collective-permute-done((bf16[1,32,1920]{2,1,0:T(8,128)(2,1)S(1)}, bf16[1,32,1920]{2,1,0:T(8,128)(2,1)S(1)}, u32[]{:S(2)}, u32[]{:S(2)}) %collective-permute-start.6) | collective-permute-done | bytes 122912 | tf_op jit(solution)/shard_map/square_sum1/ppermute | solution.py:229
  22.5 3.8 %collective-permute-start.8 = (bf16[1,32,1920]{2,1,0:T(8,128)(2,1)S(1)}, bf16[1,32,1920]{2,1,0:T(8,128)(2,1)S(1)}, u32[]{:S(2)}, u32[]{:S(2)}) collective-permute-start(bf16[1,32,1920]{2,1,0:T(8,128)(2,1)S(1)} %fusion.2), channel_id=1, source_target_pairs={{0,12},{1,13},{2,14},{3,15},{4,8},{5,9},{6,10},{7,11},{8,4},{9,5},... | collective-permute-start | bytes 368648 | tf_op jit(solution)/shard_map/far_sum1/ppermute | solution.py:229
  26.3 0.2 collective-permute-start.13
  26.6 1.9 %collective-permute-start.12 = (bf16[1,32,1920]{2,1,0:T(8,128)(2,1)S(1)}, bf16[1,32,1920]{2,1,0:T(8,128)(2,1)S(1)}, u32[]{:S(2)}, u32[]{:S(2)}) collective-permute-start(bf16[1,32,1920]{2,1,0:T(8,128)(2,1)S(1)} %add_convert_fusion), channel_id=1, source_target_pairs={{0,2},{1,3},{2,0},{3,1},{4,6},{5,7},{6,4},{7,5},{8,10},{9,11},{10,... | collective-permute-start | bytes 368648 | tf_op jit(solution)/shard_map/square_gather0/ppermute | solution.py:229
  28.5 1.4 %collective-permute-start.11 = (bf16[1,32,1920]{2,1,0:T(8,128)(2,1)S(1)}, bf16[1,32,1920]{2,1,0:T(8,128)(2,1)S(1)}, u32[]{:S(2)}, u32[]{:S(2)}) collective-permute-start(bf16[1,32,1920]{2,1,0:T(8,128)(2,1)S(1)} %add_convert_fusion), channel_id=1, source_target_pairs={{0,6},{1,7},{2,4},{3,5},{4,2},{5,3},{6,0},{7,1},{8,14},{9,15},{10,... | collective-permute-start | bytes 368648 | tf_op jit(solution)/shard_map/square_gather0/ppermute | solution.py:229
  29.9 0.7 %collective-permute-done.8 = bf16[1,32,1920]{2,1,0:T(8,128)(2,1)S(1)} collective-permute-done((bf16[1,32,1920]{2,1,0:T(8,128)(2,1)S(1)}, bf16[1,32,1920]{2,1,0:T(8,128)(2,1)S(1)}, u32[]{:S(2)}, u32[]{:S(2)}) %collective-permute-start.8) | collective-permute-done | bytes 122912 | tf_op jit(solution)/shard_map/far_sum1/ppermute | solution.py:229
  30.6 0.1 add_convert_fusion.1
  30.7 0.3 collective-permute-start.15
  31.0 1.3 %collective-permute-start.14 = (bf16[1,32,1920]{2,1,0:T(8,128)(2,1)S(1)}, bf16[1,32,1920]{2,1,0:T(8,128)(2,1)S(1)}, u32[]{:S(2)}, u32[]{:S(2)}) collective-permute-start(bf16[1,32,1920]{2,1,0:T(8,128)(2,1)S(1)} %add_convert_fusion.1), channel_id=1, source_target_pairs={{0,2},{1,3},{2,0},{3,1},{4,6},{5,7},{6,4},{7,5},{8,10},{9,11},{10,... | collective-permute-start | bytes 368648 | tf_op jit(solution)/shard_map/square_gather1/ppermute | solution.py:229
  32.3 0.7 %collective-permute-done.13 = bf16[1,32,1920]{2,1,0:T(8,128)(2,1)S(1)} collective-permute-done((bf16[1,32,1920]{2,1,0:T(8,128)(2,1)S(1)}, bf16[1,32,1920]{2,1,0:T(8,128)(2,1)S(1)}, u32[]{:S(2)}, u32[]{:S(2)}) %collective-permute-start.13) | collective-permute-done | bytes 122912 | tf_op jit(solution)/shard_map/square_gather0/ppermute | solution.py:229
  33.0 2.0 %collective-permute-start.9 = (bf16[1,32,1920]{2,1,0:T(8,128)(2,1)S(1)}, bf16[1,32,1920]{2,1,0:T(8,128)(2,1)S(1)}, u32[]{:S(2)}, u32[]{:S(2)}) collective-permute-start(bf16[1,32,1920]{2,1,0:T(8,128)(2,1)S(1)} %add_convert_fusion.1), channel_id=1, source_target_pairs={{0,6},{1,7},{2,4},{3,5},{4,2},{5,3},{6,0},{7,1},{8,14},{9,15},{10,... | collective-permute-start | bytes 368648 | tf_op jit(solution)/shard_map/square_gather1/ppermute | solution.py:229
  35.0 1.7 %collective-permute-done.11 = bf16[1,32,1920]{2,1,0:T(8,128)(2,1)S(1)} collective-permute-done((bf16[1,32,1920]{2,1,0:T(8,128)(2,1)S(1)}, bf16[1,32,1920]{2,1,0:T(8,128)(2,1)S(1)}, u32[]{:S(2)}, u32[]{:S(2)}) %collective-permute-start.11) | collective-permute-done | bytes 122912 | tf_op jit(solution)/shard_map/square_gather0/ppermute | solution.py:229
  36.9 1.2 %shard_map.68.refs_4_ = bf16[2,32,30720]{2,1,0:T(8,128)(2,1)} custom-call(s32[1]{0:T(128)} %bitcast.refs_0_, bf16[64,32]{1,0:T(8,128)(2,1)S(1)} %shard_map.66.refs_1_, bf16[4,32,1920]{2,1,0:T(8,128)(2,1)S(1)} %pad_maximum_fusion.refs_2_), custom_call_target="tpu_custom_call" | custom-call | flops 31457280 | bytes 983040 | tf_op jit(solution)/shard_map/pallas_call | solution.py:199
  38.0 1.2 %collective-permute-done.9 = bf16[1,32,1920]{2,1,0:T(8,128)(2,1)S(1)} collective-permute-done((bf16[1,32,1920]{2,1,0:T(8,128)(2,1)S(1)}, bf16[1,32,1920]{2,1,0:T(8,128)(2,1)S(1)}, u32[]{:S(2)}, u32[]{:S(2)}) %collective-permute-start.9) | collective-permute-done | bytes 122912 | tf_op jit(solution)/shard_map/square_gather1/ppermute | solution.py:229
  39.5 1.5 %shard_map.69.refs_3_ = bf16[2,32,30720]{2,1,0:T(8,128)(2,1)} custom-call(s32[1]{0:T(128)} %bitcast.refs_0_, bf16[64,32]{1,0:T(8,128)(2,1)S(1)} %shard_map.66.refs_1_, bf16[4,32,1920]{2,1,0:T(8,128)(2,1)S(1)} %collective-permute-done.17.refs_2_, bf16[4,32,1920]{2,1,0:T(8,128)(2,1)S(1)} %pad_maximum_fusion.1.refs_3_, ...), custom_call_target="tpu_custom_call", output_to_operand_aliasing={{}: (4, {})} | custom-call | flops 62914560 | bytes 1966080 | tf_op jit(solution)/shard_map/pallas_call | solution.py:199
  41.0 0.3 collective-permute-done.16.refs_2_
  41.3 1.2 %shard_map.70 = bf16[2,32,30720]{2,1,0:T(8,128)(2,1)} custom-call(s32[1]{0:T(128)} %bitcast.refs_0_, bf16[64,32]{1,0:T(8,128)(2,1)S(1)} %shard_map.66.refs_1_, bf16[4,32,1920]{2,1,0:T(8,128)(2,1)S(1)} %collective-permute-done.16.refs_2_, bf16[2,32,30720]{2,1,0:T(8,128)(2,1)} %shard_map.69.refs_3_), custom_call_target="tpu_custom_call", output_to_operand_aliasing={{}: (3, {})} | custom-call | flops 31457280 | bytes 983040 | tf_op jit(solution)/shard_map/pallas_call | solution.py:199
  (28 shorter events, 0.7 us)
Async XLA Ops:
  2.1 3.0 %collective-permute-start = (bf16[4,32,1920]{2,1,0:T(8,128)(2,1)S(1)}, bf16[4,32,1920]{2,1,0:T(8,128)(2,1)S(1)}, u32[]{:S(2)}, u32[]{:S(2)}) collective-permute-start(bf16[4,32,1920]{2,1,0:T(8,128)(2,1)S(1)} %get-tuple-element.15), channel_id=1, source_target_pairs={{0,1},{1,0},{2,3},{3,2},{4,5},{5,4},{6,7},{7,6},{8,9},{9,8},{10,11... | collective-permute-start | bytes 1474568 | tf_op jit(solution)/shard_map/core_sum0/ppermute | solution.py:229
  5.0 6.8 %collective-permute-start.4 = (bf16[4,32,1920]{2,1,0:T(8,128)(2,1)S(1)}, bf16[4,32,1920]{2,1,0:T(8,128)(2,1)S(1)}, u32[]{:S(2)}, u32[]{:S(2)}) collective-permute-start(bf16[4,32,1920]{2,1,0:T(8,128)(2,1)S(1)} %get-tuple-element.18), channel_id=1, source_target_pairs={{0,1},{1,0},{2,3},{3,2},{4,5},{5,4},{6,7},{7,6},{8,9},{9,8},{10,11... | collective-permute-start | bytes 1474568 | tf_op jit(solution)/shard_map/core_sum1/ppermute | solution.py:229
  5.3 11.9 %collective-permute-start.1 = (bf16[1,32,1920]{2,1,0:T(8,128)(2,1)S(1)}, bf16[1,32,1920]{2,1,0:T(8,128)(2,1)S(1)}, u32[]{:S(2)}, u32[]{:S(2)}) collective-permute-start(bf16[1,32,1920]{2,1,0:T(8,128)(2,1)S(1)} %get-tuple-element.28), channel_id=1, source_target_pairs={{0,4},{1,5},{2,6},{3,7},{4,0},{5,1},{6,2},{7,3},{8,12},{9,13},{10,... | collective-permute-start | bytes 368648 | tf_op jit(solution)/shard_map/square_sum0/ppermute | solution.py:229
  8.5 7.3 %collective-permute-start.3 = (bf16[1,32,1920]{2,1,0:T(8,128)(2,1)S(1)}, bf16[1,32,1920]{2,1,0:T(8,128)(2,1)S(1)}, u32[]{:S(2)}, u32[]{:S(2)}) collective-permute-start(bf16[1,32,1920]{2,1,0:T(8,128)(2,1)S(1)} %get-tuple-element.29), channel_id=1, source_target_pairs={{0,2},{1,3},{2,0},{3,1},{4,6},{5,7},{6,4},{7,5},{8,10},{9,11},{10,... | collective-permute-start | bytes 368648 | tf_op jit(solution)/shard_map/square_sum0/ppermute | solution.py:229
  9.9 7.2 %collective-permute-start.2 = (bf16[1,32,1920]{2,1,0:T(8,128)(2,1)S(1)}, bf16[1,32,1920]{2,1,0:T(8,128)(2,1)S(1)}, u32[]{:S(2)}, u32[]{:S(2)}) collective-permute-start(bf16[1,32,1920]{2,1,0:T(8,128)(2,1)S(1)} %get-tuple-element.30), channel_id=1, source_target_pairs={{0,6},{1,7},{2,4},{3,5},{4,2},{5,3},{6,0},{7,1},{8,14},{9,15},{10,... | collective-permute-start | bytes 368648 | tf_op jit(solution)/shard_map/square_sum0/ppermute | solution.py:229
  11.7 8.2 %copy-start = (s32[3,32]{1,0:T(4,128)S(1)}, s32[3,32]{1,0:T(4,128)}, u32[]{:S(2)}) copy-start(s32[3,32]{1,0:T(4,128)} %q_ref) | copy-start | bytes 1156
  11.7 8.2 %copy-start.1 = (s32[3,16]{1,0:T(4,128)S(1)}, s32[3,16]{1,0:T(4,128)}, u32[]{:S(2)}) copy-start(s32[3,16]{1,0:T(4,128)} %phon_ref.1) | copy-start | bytes 580
  11.8 8.2 %copy-start.2 = (s32[16]{0:T(128)S(1)}, s32[16]{0:T(128)}, u32[]{:S(2)}) copy-start(s32[16]{0:T(128)} %param.9) | copy-start | bytes 196
  12.0 8.3 %collective-permute-start.5 = (bf16[1,32,1920]{2,1,0:T(8,128)(2,1)S(1)}, bf16[1,32,1920]{2,1,0:T(8,128)(2,1)S(1)}, u32[]{:S(2)}, u32[]{:S(2)}) collective-permute-start(bf16[1,32,1920]{2,1,0:T(8,128)(2,1)S(1)} %get-tuple-element.25), channel_id=1, source_target_pairs={{0,4},{1,5},{2,6},{3,7},{4,0},{5,1},{6,2},{7,3},{8,12},{9,13},{10,... | collective-permute-start | bytes 368648 | tf_op jit(solution)/shard_map/square_sum1/ppermute | solution.py:229
  14.0 6.3 %collective-permute-start.7 = (bf16[1,32,1920]{2,1,0:T(8,128)(2,1)S(1)}, bf16[1,32,1920]{2,1,0:T(8,128)(2,1)S(1)}, u32[]{:S(2)}, u32[]{:S(2)}) collective-permute-start(bf16[1,32,1920]{2,1,0:T(8,128)(2,1)S(1)} %get-tuple-element.26), channel_id=1, source_target_pairs={{0,2},{1,3},{2,0},{3,1},{4,6},{5,7},{6,4},{7,5},{8,10},{9,11},{10,... | collective-permute-start | bytes 368648 | tf_op jit(solution)/shard_map/square_sum1/ppermute | solution.py:229
  15.7 6.7 %collective-permute-start.6 = (bf16[1,32,1920]{2,1,0:T(8,128)(2,1)S(1)}, bf16[1,32,1920]{2,1,0:T(8,128)(2,1)S(1)}, u32[]{:S(2)}, u32[]{:S(2)}) collective-permute-start(bf16[1,32,1920]{2,1,0:T(8,128)(2,1)S(1)} %get-tuple-element.27), channel_id=1, source_target_pairs={{0,6},{1,7},{2,4},{3,5},{4,2},{5,3},{6,0},{7,1},{8,14},{9,15},{10,... | collective-permute-start | bytes 368648 | tf_op jit(solution)/shard_map/square_sum1/ppermute | solution.py:229
  17.2 9.0 %collective-permute-start.10 = (bf16[1,32,1920]{2,1,0:T(8,128)(2,1)S(1)}, bf16[1,32,1920]{2,1,0:T(8,128)(2,1)S(1)}, u32[]{:S(2)}, u32[]{:S(2)}) collective-permute-start(bf16[1,32,1920]{2,1,0:T(8,128)(2,1)S(1)} %fusion.3), channel_id=1, source_target_pairs={{0,8},{1,9},{2,10},{3,11},{4,12},{5,13},{6,14},{7,15},{8,0},{9,1},... | collective-permute-start | bytes 368648 | tf_op jit(solution)/shard_map/far_sum0/ppermute | solution.py:229
  22.5 8.1 %collective-permute-start.8 = (bf16[1,32,1920]{2,1,0:T(8,128)(2,1)S(1)}, bf16[1,32,1920]{2,1,0:T(8,128)(2,1)S(1)}, u32[]{:S(2)}, u32[]{:S(2)}) collective-permute-start(bf16[1,32,1920]{2,1,0:T(8,128)(2,1)S(1)} %fusion.2), channel_id=1, source_target_pairs={{0,12},{1,13},{2,14},{3,15},{4,8},{5,9},{6,10},{7,11},{8,4},{9,5},... | collective-permute-start | bytes 368648 | tf_op jit(solution)/shard_map/far_sum1/ppermute | solution.py:229
  26.3 6.7 %collective-permute-start.13 = (bf16[1,32,1920]{2,1,0:T(8,128)(2,1)S(1)}, bf16[1,32,1920]{2,1,0:T(8,128)(2,1)S(1)}, u32[]{:S(2)}, u32[]{:S(2)}) collective-permute-start(bf16[1,32,1920]{2,1,0:T(8,128)(2,1)S(1)} %add_convert_fusion), channel_id=1, source_target_pairs={{0,4},{1,5},{2,6},{3,7},{4,0},{5,1},{6,2},{7,3},{8,12},{9,13},{10,... | collective-permute-start | bytes 368648 | tf_op jit(solution)/shard_map/square_gather0/ppermute | solution.py:229
  26.6 8.4 %collective-permute-start.12 = (bf16[1,32,1920]{2,1,0:T(8,128)(2,1)S(1)}, bf16[1,32,1920]{2,1,0:T(8,128)(2,1)S(1)}, u32[]{:S(2)}, u32[]{:S(2)}) collective-permute-start(bf16[1,32,1920]{2,1,0:T(8,128)(2,1)S(1)} %add_convert_fusion), channel_id=1, source_target_pairs={{0,2},{1,3},{2,0},{3,1},{4,6},{5,7},{6,4},{7,5},{8,10},{9,11},{10,... | collective-permute-start | bytes 368648 | tf_op jit(solution)/shard_map/square_gather0/ppermute | solution.py:229
  28.5 8.2 %collective-permute-start.11 = (bf16[1,32,1920]{2,1,0:T(8,128)(2,1)S(1)}, bf16[1,32,1920]{2,1,0:T(8,128)(2,1)S(1)}, u32[]{:S(2)}, u32[]{:S(2)}) collective-permute-start(bf16[1,32,1920]{2,1,0:T(8,128)(2,1)S(1)} %add_convert_fusion), channel_id=1, source_target_pairs={{0,6},{1,7},{2,4},{3,5},{4,2},{5,3},{6,0},{7,1},{8,14},{9,15},{10,... | collective-permute-start | bytes 368648 | tf_op jit(solution)/shard_map/square_gather0/ppermute | solution.py:229
  30.7 8.6 %collective-permute-start.15 = (bf16[1,32,1920]{2,1,0:T(8,128)(2,1)S(1)}, bf16[1,32,1920]{2,1,0:T(8,128)(2,1)S(1)}, u32[]{:S(2)}, u32[]{:S(2)}) collective-permute-start(bf16[1,32,1920]{2,1,0:T(8,128)(2,1)S(1)} %add_convert_fusion.1), channel_id=1, source_target_pairs={{0,4},{1,5},{2,6},{3,7},{4,0},{5,1},{6,2},{7,3},{8,12},{9,13},{10,... | collective-permute-start | bytes 368648 | tf_op jit(solution)/shard_map/square_gather1/ppermute | solution.py:229
  31.0 8.3 %collective-permute-start.14 = (bf16[1,32,1920]{2,1,0:T(8,128)(2,1)S(1)}, bf16[1,32,1920]{2,1,0:T(8,128)(2,1)S(1)}, u32[]{:S(2)}, u32[]{:S(2)}) collective-permute-start(bf16[1,32,1920]{2,1,0:T(8,128)(2,1)S(1)} %add_convert_fusion.1), channel_id=1, source_target_pairs={{0,2},{1,3},{2,0},{3,1},{4,6},{5,7},{6,4},{7,5},{8,10},{9,11},{10,... | collective-permute-start | bytes 368648 | tf_op jit(solution)/shard_map/square_gather1/ppermute | solution.py:229
  33.0 6.3 %collective-permute-start.9 = (bf16[1,32,1920]{2,1,0:T(8,128)(2,1)S(1)}, bf16[1,32,1920]{2,1,0:T(8,128)(2,1)S(1)}, u32[]{:S(2)}, u32[]{:S(2)}) collective-permute-start(bf16[1,32,1920]{2,1,0:T(8,128)(2,1)S(1)} %add_convert_fusion.1), channel_id=1, source_target_pairs={{0,6},{1,7},{2,4},{3,5},{4,2},{5,3},{6,0},{7,1},{8,14},{9,15},{10,... | collective-permute-start | bytes 368648 | tf_op jit(solution)/shard_map/square_gather1/ppermute | solution.py:229
  36.8 2.7 %collective-permute-start.17 = (bf16[4,32,1920]{2,1,0:T(8,128)(2,1)S(1)}, bf16[4,32,1920]{2,1,0:T(8,128)(2,1)S(1)}, u32[]{:S(2)}, u32[]{:S(2)}) collective-permute-start(bf16[4,32,1920]{2,1,0:T(8,128)(2,1)S(1)} %pad_maximum_fusion.refs_2_), channel_id=1, source_target_pairs={{0,1},{1,0},{2,3},{3,2},{4,5},{5,4},{6,7},{7,6},{8,9},{9,8},{10,11... | collective-permute-start | bytes 1474568 | tf_op jit(solution)/shard_map/core_gather0/ppermute | solution.py:229
  39.4 1.9 %collective-permute-start.16 = (bf16[4,32,1920]{2,1,0:T(8,128)(2,1)S(1)}, bf16[4,32,1920]{2,1,0:T(8,128)(2,1)S(1)}, u32[]{:S(2)}, u32[]{:S(2)}) collective-permute-start(bf16[4,32,1920]{2,1,0:T(8,128)(2,1)S(1)} %pad_maximum_fusion.1.refs_3_), channel_id=1, source_target_pairs={{0,1},{1,0},{2,3},{3,2},{4,5},{5,4},{6,7},{7,6},{8,9},{9,8},{10,11... | collective-permute-start | bytes 1474568 | tf_op jit(solution)/shard_map/core_gather1/ppermute | solution.py:229

commit v7 on v6

--- a/solution.py
+++ b/solution.py
@@ -92,7 +92,7 @@
     for n, copy in enumerate(copies):
         out_ref, table = outs[n // len(CHIPS)], tables[n // len(CHIPS)]
         columns = out_ref.shape[-1]
-        split = columns * SHARE[0] // SHARE[1] // 128 * 128
+        split = columns * SHARE[0] // SHARE[1] // 128 * 128 if given else 0
         copy.wait()
         if split:
             flat = table[n % len(CHIPS), :, :, :, :split].reshape(depth, split)
@@ -238,12 +238,12 @@
         here = me if s == 0 else after(me, first[s - 1])
         pieces = [(0, s, full)] + [(1, s + 1, wire)] * (s < last)
         own, *theirs = partial_sums(here, kmat, couplings, pieces)
-        if theirs:
-            got[s + 1] = to_core(theirs[0], f"core_sum{s + 1}")
         total[s] = own + got[s].astype(full)
         parts = [total[s][i : i + 1].astype(wire) for i in SUM_ORDER]
         first[s] = parts[0]
         got[s] = [send(part, SQUARE[i], f"square_sum{s}") for i, part in zip(SUM_ORDER, parts)]
+        if theirs:
+            got[s + 1] = to_core(after(theirs[0], parts[0]), f"core_sum{s + 1}")
     for s in streams:
         own = total[s][3:]
         if s == last:

time: 42.6 us -> 42.6 us (level)
  transfers between devices with their start and end apart: 18 -> 18, of which waited for: 7 -> 7; matrix products, arithmetic and copies ran while one was open for 2% -> 1% of each run, Pallas kernels for 17% -> 17%
where the time goes in v7:
time: 42.6 us; the launch traced here: 42.4 us
  starting transfers between devices  23.6 us (55%)
  Pallas kernels  10.5 us (25%)
  waiting for transfers between devices  7.39 us (17%)
  other arithmetic  0.68 us (2%)
    ppermute x18, starting transfers between devices, send(): return lax.ppermute(array, 'blk', [(i, i ^ bits) for i in range(devices)])  23.6 us
    ppermute x18, waiting for transfers between devices, send(): return lax.ppermute(array, 'blk', [(i, i ^ bits) for i in range(devices)])  7.39 us
    pallas_call x3, Pallas kernels, partial_sums(): pl.pallas_call(lambda *refs: partial_kernel(pieces, given, *refs), in_spe...  6.28 us
    pallas_call x3, Pallas kernels, bloch(): pl.pallas_call(lambda *refs: bloch_kernel(places, *refs), in_specs=[pl.Bl...  3.86 us
  transfers between devices with their start and end apart: 18, of which 7 were waited for; matrix products, arithmetic and copies ran while one was open for 1% of the time, Pallas kernels for 17%

profile of v7, /device:TPU:0, one launch (start us, length us, event | category | flops | bytes accessed | tf_op | source)
XLA Modules:
  0.0 42.4 jit_solution(9364706535125192205)
XLA Ops:
  0.0 2.2 %shard_map.64 = (bf16[32,128]{1,0:T(8,128)(2,1)S(1)}, bf16[4,32,1920]{2,1,0:T(8,128)(2,1)S(1)}) custom-call(s32[1]{0:T(128)} %bitcast.refs_0_, f32[1,3]{1,0:T(1,128)} %bitcast.4, s32[3,4]{1,0:T(4,128)} %refs_2_.3, bf16[4,2,16,30720]{3,2,1,0:T(8,128)(2,1)} %refs_2_.5), custom_call_target="tpu_custom_call" | custom-call | flops 62914560 | bytes 1966080 | tf_op jit(solution)/shard_map/pallas_call | solution.py:130
  2.2 0.5 %collective-permute-start = (bf16[4,32,1920]{2,1,0:T(8,128)(2,1)S(1)}, bf16[4,32,1920]{2,1,0:T(8,128)(2,1)S(1)}, u32[]{:S(2)}, u32[]{:S(2)}) collective-permute-start(bf16[4,32,1920]{2,1,0:T(8,128)(2,1)S(1)} %get-tuple-element.16), channel_id=1, source_target_pairs={{0,1},{1,0},{2,3},{3,2},{4,5},{5,4},{6,7},{7,6},{8,9},{9,8},{10,11... | collective-permute-start | bytes 1474568 | tf_op jit(solution)/shard_map/core_sum0/ppermute | solution.py:229
  2.7 2.4 %shard_map.65 = (f32[4,32,1920]{2,1,0:T(8,128)S(1)}, bf16[4,32,1920]{2,1,0:T(8,128)(2,1)S(1)}) custom-call(s32[1]{0:T(128)} %bitcast.refs_0_, bf16[32,128]{1,0:T(8,128)(2,1)S(1)} %get-tuple-element.14.refs_1_, bf16[4,2,16,30720]{3,2,1,0:T(8,128)(2,1)} %refs_2_.5), custom_call_target="tpu_custom_call" | custom-call | flops 125829120 | bytes 3932160 | tf_op jit(solution)/shard_map/pallas_call | solution.py:130
  5.0 0.1 fusion.5
  5.2 0.2 collective-permute-start.4
  5.4 3.1 %collective-permute-start.1 = (bf16[1,32,1920]{2,1,0:T(8,128)(2,1)S(1)}, bf16[1,32,1920]{2,1,0:T(8,128)(2,1)S(1)}, u32[]{:S(2)}, u32[]{:S(2)}) collective-permute-start(bf16[1,32,1920]{2,1,0:T(8,128)(2,1)S(1)} %get-tuple-element.30), channel_id=1, source_target_pairs={{0,4},{1,5},{2,6},{3,7},{4,0},{5,1},{6,2},{7,3},{8,12},{9,13},{10,... | collective-permute-start | bytes 368648 | tf_op jit(solution)/shard_map/square_sum0/ppermute | solution.py:229
  8.5 1.5 %collective-permute-start.3 = (bf16[1,32,1920]{2,1,0:T(8,128)(2,1)S(1)}, bf16[1,32,1920]{2,1,0:T(8,128)(2,1)S(1)}, u32[]{:S(2)}, u32[]{:S(2)}) collective-permute-start(bf16[1,32,1920]{2,1,0:T(8,128)(2,1)S(1)} %get-tuple-element.31), channel_id=1, source_target_pairs={{0,2},{1,3},{2,0},{3,1},{4,6},{5,7},{6,4},{7,5},{8,10},{9,11},{10,... | collective-permute-start | bytes 368648 | tf_op jit(solution)/shard_map/square_sum0/ppermute | solution.py:229
  9.9 1.7 %shard_map.67 = f32[4,32,1920]{2,1,0:T(8,128)S(1)} custom-call(s32[1]{0:T(128)} %bitcast.refs_0_, bf16[32,128]{1,0:T(8,128)(2,1)S(1)} %get-tuple-element.14.refs_1_, bf16[4,2,16,30720]{3,2,1,0:T(8,128)(2,1)} %refs_2_.5), custom_call_target="tpu_custom_call" | custom-call | flops 62914560 | bytes 1966080 | tf_op jit(solution)/shard_map/pallas_call | solution.py:130
  11.7 0.1 fusion.4
  11.9 2.1 %collective-permute-start.5 = (bf16[1,32,1920]{2,1,0:T(8,128)(2,1)S(1)}, bf16[1,32,1920]{2,1,0:T(8,128)(2,1)S(1)}, u32[]{:S(2)}, u32[]{:S(2)}) collective-permute-start(bf16[1,32,1920]{2,1,0:T(8,128)(2,1)S(1)} %get-tuple-element.27), channel_id=1, source_target_pairs={{0,4},{1,5},{2,6},{3,7},{4,0},{5,1},{6,2},{7,3},{8,12},{9,13},{10,... | collective-permute-start | bytes 368648 | tf_op jit(solution)/shard_map/square_sum1/ppermute | solution.py:229
  14.0 1.5 %collective-permute-start.7 = (bf16[1,32,1920]{2,1,0:T(8,128)(2,1)S(1)}, bf16[1,32,1920]{2,1,0:T(8,128)(2,1)S(1)}, u32[]{:S(2)}, u32[]{:S(2)}) collective-permute-start(bf16[1,32,1920]{2,1,0:T(8,128)(2,1)S(1)} %get-tuple-element.28), channel_id=1, source_target_pairs={{0,2},{1,3},{2,0},{3,1},{4,6},{5,7},{6,4},{7,5},{8,10},{9,11},{10,... | collective-permute-start | bytes 368648 | tf_op jit(solution)/shard_map/square_sum1/ppermute | solution.py:229
  15.5 0.3 collective-permute-done.3
  15.8 1.4 %collective-permute-start.6 = (bf16[1,32,1920]{2,1,0:T(8,128)(2,1)S(1)}, bf16[1,32,1920]{2,1,0:T(8,128)(2,1)S(1)}, u32[]{:S(2)}, u32[]{:S(2)}) collective-permute-start(bf16[1,32,1920]{2,1,0:T(8,128)(2,1)S(1)} %get-tuple-element.29), channel_id=1, source_target_pairs={{0,6},{1,7},{2,4},{3,5},{4,2},{5,3},{6,0},{7,1},{8,14},{9,15},{10,... | collective-permute-start | bytes 368648 | tf_op jit(solution)/shard_map/square_sum1/ppermute | solution.py:229
  17.3 2.7 %collective-permute-start.10 = (bf16[1,32,1920]{2,1,0:T(8,128)(2,1)S(1)}, bf16[1,32,1920]{2,1,0:T(8,128)(2,1)S(1)}, u32[]{:S(2)}, u32[]{:S(2)}) collective-permute-start(bf16[1,32,1920]{2,1,0:T(8,128)(2,1)S(1)} %fusion.3), channel_id=1, source_target_pairs={{0,8},{1,9},{2,10},{3,11},{4,12},{5,13},{6,14},{7,15},{8,0},{9,1},... | collective-permute-start | bytes 368648 | tf_op jit(solution)/shard_map/far_sum0/ppermute | solution.py:229
  19.9 0.3 shard_map.66.refs_1_
  20.3 2.2 %collective-permute-done.6 = bf16[1,32,1920]{2,1,0:T(8,128)(2,1)S(1)} collective-permute-done((bf16[1,32,1920]{2,1,0:T(8,128)(2,1)S(1)}, bf16[1,32,1920]{2,1,0:T(8,128)(2,1)S(1)}, u32[]{:S(2)}, u32[]{:S(2)}) %collective-permute-start.6) | collective-permute-done | bytes 122912 | tf_op jit(solution)/shard_map/square_sum1/ppermute | solution.py:229
  22.5 3.7 %collective-permute-start.8 = (bf16[1,32,1920]{2,1,0:T(8,128)(2,1)S(1)}, bf16[1,32,1920]{2,1,0:T(8,128)(2,1)S(1)}, u32[]{:S(2)}, u32[]{:S(2)}) collective-permute-start(bf16[1,32,1920]{2,1,0:T(8,128)(2,1)S(1)} %fusion.2), channel_id=1, source_target_pairs={{0,12},{1,13},{2,14},{3,15},{4,8},{5,9},{6,10},{7,11},{8,4},{9,5},... | collective-permute-start | bytes 368648 | tf_op jit(solution)/shard_map/far_sum1/ppermute | solution.py:229
  26.4 0.2 collective-permute-start.13
  26.6 1.9 %collective-permute-start.12 = (bf16[1,32,1920]{2,1,0:T(8,128)(2,1)S(1)}, bf16[1,32,1920]{2,1,0:T(8,128)(2,1)S(1)}, u32[]{:S(2)}, u32[]{:S(2)}) collective-permute-start(bf16[1,32,1920]{2,1,0:T(8,128)(2,1)S(1)} %add_convert_fusion), channel_id=1, source_target_pairs={{0,2},{1,3},{2,0},{3,1},{4,6},{5,7},{6,4},{7,5},{8,10},{9,11},{10,... | collective-permute-start | bytes 368648 | tf_op jit(solution)/shard_map/square_gather0/ppermute | solution.py:229
  28.5 1.4 %collective-permute-start.11 = (bf16[1,32,1920]{2,1,0:T(8,128)(2,1)S(1)}, bf16[1,32,1920]{2,1,0:T(8,128)(2,1)S(1)}, u32[]{:S(2)}, u32[]{:S(2)}) collective-permute-start(bf16[1,32,1920]{2,1,0:T(8,128)(2,1)S(1)} %add_convert_fusion), channel_id=1, source_target_pairs={{0,6},{1,7},{2,4},{3,5},{4,2},{5,3},{6,0},{7,1},{8,14},{9,15},{10,... | collective-permute-start | bytes 368648 | tf_op jit(solution)/shard_map/square_gather0/ppermute | solution.py:229
  29.9 0.7 %collective-permute-done.8 = bf16[1,32,1920]{2,1,0:T(8,128)(2,1)S(1)} collective-permute-done((bf16[1,32,1920]{2,1,0:T(8,128)(2,1)S(1)}, bf16[1,32,1920]{2,1,0:T(8,128)(2,1)S(1)}, u32[]{:S(2)}, u32[]{:S(2)}) %collective-permute-start.8) | collective-permute-done | bytes 122912 | tf_op jit(solution)/shard_map/far_sum1/ppermute | solution.py:229
  30.7 0.1 add_convert_fusion.1
  30.7 0.5 %collective-permute-start.15 = (bf16[1,32,1920]{2,1,0:T(8,128)(2,1)S(1)}, bf16[1,32,1920]{2,1,0:T(8,128)(2,1)S(1)}, u32[]{:S(2)}, u32[]{:S(2)}) collective-permute-start(bf16[1,32,1920]{2,1,0:T(8,128)(2,1)S(1)} %add_convert_fusion.1), channel_id=1, source_target_pairs={{0,4},{1,5},{2,6},{3,7},{4,0},{5,1},{6,2},{7,3},{8,12},{9,13},{10,... | collective-permute-start | bytes 368648 | tf_op jit(solution)/shard_map/square_gather1/ppermute | solution.py:229
  31.2 1.0 %collective-permute-start.14 = (bf16[1,32,1920]{2,1,0:T(8,128)(2,1)S(1)}, bf16[1,32,1920]{2,1,0:T(8,128)(2,1)S(1)}, u32[]{:S(2)}, u32[]{:S(2)}) collective-permute-start(bf16[1,32,1920]{2,1,0:T(8,128)(2,1)S(1)} %add_convert_fusion.1), channel_id=1, source_target_pairs={{0,2},{1,3},{2,0},{3,1},{4,6},{5,7},{6,4},{7,5},{8,10},{9,11},{10,... | collective-permute-start | bytes 368648 | tf_op jit(solution)/shard_map/square_gather1/ppermute | solution.py:229
  32.2 0.8 %collective-permute-done.13 = bf16[1,32,1920]{2,1,0:T(8,128)(2,1)S(1)} collective-permute-done((bf16[1,32,1920]{2,1,0:T(8,128)(2,1)S(1)}, bf16[1,32,1920]{2,1,0:T(8,128)(2,1)S(1)}, u32[]{:S(2)}, u32[]{:S(2)}) %collective-permute-start.13) | collective-permute-done | bytes 122912 | tf_op jit(solution)/shard_map/square_gather0/ppermute | solution.py:229
  33.0 1.9 %collective-permute-start.9 = (bf16[1,32,1920]{2,1,0:T(8,128)(2,1)S(1)}, bf16[1,32,1920]{2,1,0:T(8,128)(2,1)S(1)}, u32[]{:S(2)}, u32[]{:S(2)}) collective-permute-start(bf16[1,32,1920]{2,1,0:T(8,128)(2,1)S(1)} %add_convert_fusion.1), channel_id=1, source_target_pairs={{0,6},{1,7},{2,4},{3,5},{4,2},{5,3},{6,0},{7,1},{8,14},{9,15},{10,... | collective-permute-start | bytes 368648 | tf_op jit(solution)/shard_map/square_gather1/ppermute | solution.py:229
  34.9 1.8 %collective-permute-done.11 = bf16[1,32,1920]{2,1,0:T(8,128)(2,1)S(1)} collective-permute-done((bf16[1,32,1920]{2,1,0:T(8,128)(2,1)S(1)}, bf16[1,32,1920]{2,1,0:T(8,128)(2,1)S(1)}, u32[]{:S(2)}, u32[]{:S(2)}) %collective-permute-start.11) | collective-permute-done | bytes 122912 | tf_op jit(solution)/shard_map/square_gather0/ppermute | solution.py:229
  36.8 1.2 %shard_map.68.refs_4_ = bf16[2,32,30720]{2,1,0:T(8,128)(2,1)} custom-call(s32[1]{0:T(128)} %bitcast.refs_0_, bf16[64,32]{1,0:T(8,128)(2,1)S(1)} %shard_map.66.refs_1_, bf16[4,32,1920]{2,1,0:T(8,128)(2,1)S(1)} %pad_maximum_fusion.refs_2_), custom_call_target="tpu_custom_call" | custom-call | flops 31457280 | bytes 983040 | tf_op jit(solution)/shard_map/pallas_call | solution.py:199
  38.0 1.2 %collective-permute-done.9 = bf16[1,32,1920]{2,1,0:T(8,128)(2,1)S(1)} collective-permute-done((bf16[1,32,1920]{2,1,0:T(8,128)(2,1)S(1)}, bf16[1,32,1920]{2,1,0:T(8,128)(2,1)S(1)}, u32[]{:S(2)}, u32[]{:S(2)}) %collective-permute-start.9) | collective-permute-done | bytes 122912 | tf_op jit(solution)/shard_map/square_gather1/ppermute | solution.py:229
  39.4 1.5 %shard_map.69.refs_3_ = bf16[2,32,30720]{2,1,0:T(8,128)(2,1)} custom-call(s32[1]{0:T(128)} %bitcast.refs_0_, bf16[64,32]{1,0:T(8,128)(2,1)S(1)} %shard_map.66.refs_1_, bf16[4,32,1920]{2,1,0:T(8,128)(2,1)S(1)} %collective-permute-done.17.refs_2_, bf16[4,32,1920]{2,1,0:T(8,128)(2,1)S(1)} %pad_maximum_fusion.1.refs_3_, ...), custom_call_target="tpu_custom_call", output_to_operand_aliasing={{}: (4, {})} | custom-call | flops 62914560 | bytes 1966080 | tf_op jit(solution)/shard_map/pallas_call | solution.py:199
  41.0 0.3 collective-permute-done.16.refs_2_
  41.3 1.2 %shard_map.70 = bf16[2,32,30720]{2,1,0:T(8,128)(2,1)} custom-call(s32[1]{0:T(128)} %bitcast.refs_0_, bf16[64,32]{1,0:T(8,128)(2,1)S(1)} %shard_map.66.refs_1_, bf16[4,32,1920]{2,1,0:T(8,128)(2,1)S(1)} %collective-permute-done.16.refs_2_, bf16[2,32,30720]{2,1,0:T(8,128)(2,1)} %shard_map.69.refs_3_), custom_call_target="tpu_custom_call", output_to_operand_aliasing={{}: (3, {})} | custom-call | flops 31457280 | bytes 983040 | tf_op jit(solution)/shard_map/pallas_call | solution.py:199
  (28 shorter events, 0.6 us)
Async XLA Ops:
  2.2 2.8 %collective-permute-start = (bf16[4,32,1920]{2,1,0:T(8,128)(2,1)S(1)}, bf16[4,32,1920]{2,1,0:T(8,128)(2,1)S(1)}, u32[]{:S(2)}, u32[]{:S(2)}) collective-permute-start(bf16[4,32,1920]{2,1,0:T(8,128)(2,1)S(1)} %get-tuple-element.16), channel_id=1, source_target_pairs={{0,1},{1,0},{2,3},{3,2},{4,5},{5,4},{6,7},{7,6},{8,9},{9,8},{10,11... | collective-permute-start | bytes 1474568 | tf_op jit(solution)/shard_map/core_sum0/ppermute | solution.py:229
  5.2 6.5 %collective-permute-start.4 = (bf16[4,32,1920]{2,1,0:T(8,128)(2,1)S(1)}, bf16[4,32,1920]{2,1,0:T(8,128)(2,1)S(1)}, u32[]{:S(2)}, u32[]{:S(2)}) collective-permute-start(bf16[4,32,1920]{2,1,0:T(8,128)(2,1)S(1)} %get-tuple-element.20), channel_id=1, source_target_pairs={{0,1},{1,0},{2,3},{3,2},{4,5},{5,4},{6,7},{7,6},{8,9},{9,8},{10,11... | collective-permute-start | bytes 1474568 | tf_op jit(solution)/shard_map/core_sum1/ppermute | solution.py:229
  5.4 11.8 %collective-permute-start.1 = (bf16[1,32,1920]{2,1,0:T(8,128)(2,1)S(1)}, bf16[1,32,1920]{2,1,0:T(8,128)(2,1)S(1)}, u32[]{:S(2)}, u32[]{:S(2)}) collective-permute-start(bf16[1,32,1920]{2,1,0:T(8,128)(2,1)S(1)} %get-tuple-element.30), channel_id=1, source_target_pairs={{0,4},{1,5},{2,6},{3,7},{4,0},{5,1},{6,2},{7,3},{8,12},{9,13},{10,... | collective-permute-start | bytes 368648 | tf_op jit(solution)/shard_map/square_sum0/ppermute | solution.py:229
  8.5 7.3 %collective-permute-start.3 = (bf16[1,32,1920]{2,1,0:T(8,128)(2,1)S(1)}, bf16[1,32,1920]{2,1,0:T(8,128)(2,1)S(1)}, u32[]{:S(2)}, u32[]{:S(2)}) collective-permute-start(bf16[1,32,1920]{2,1,0:T(8,128)(2,1)S(1)} %get-tuple-element.31), channel_id=1, source_target_pairs={{0,2},{1,3},{2,0},{3,1},{4,6},{5,7},{6,4},{7,5},{8,10},{9,11},{10,... | collective-permute-start | bytes 368648 | tf_op jit(solution)/shard_map/square_sum0/ppermute | solution.py:229
  9.9 7.3 %collective-permute-start.2 = (bf16[1,32,1920]{2,1,0:T(8,128)(2,1)S(1)}, bf16[1,32,1920]{2,1,0:T(8,128)(2,1)S(1)}, u32[]{:S(2)}, u32[]{:S(2)}) collective-permute-start(bf16[1,32,1920]{2,1,0:T(8,128)(2,1)S(1)} %get-tuple-element.32), channel_id=1, source_target_pairs={{0,6},{1,7},{2,4},{3,5},{4,2},{5,3},{6,0},{7,1},{8,14},{9,15},{10,... | collective-permute-start | bytes 368648 | tf_op jit(solution)/shard_map/square_sum0/ppermute | solution.py:229
  11.7 8.2 %copy-start = (s32[3,32]{1,0:T(4,128)S(1)}, s32[3,32]{1,0:T(4,128)}, u32[]{:S(2)}) copy-start(s32[3,32]{1,0:T(4,128)} %q_ref) | copy-start | bytes 1156
  11.7 8.2 %copy-start.1 = (s32[3,16]{1,0:T(4,128)S(1)}, s32[3,16]{1,0:T(4,128)}, u32[]{:S(2)}) copy-start(s32[3,16]{1,0:T(4,128)} %phon_ref.1) | copy-start | bytes 580
  11.7 8.2 %copy-start.2 = (s32[16]{0:T(128)S(1)}, s32[16]{0:T(128)}, u32[]{:S(2)}) copy-start(s32[16]{0:T(128)} %param.9) | copy-start | bytes 196
  11.9 8.4 %collective-permute-start.5 = (bf16[1,32,1920]{2,1,0:T(8,128)(2,1)S(1)}, bf16[1,32,1920]{2,1,0:T(8,128)(2,1)S(1)}, u32[]{:S(2)}, u32[]{:S(2)}) collective-permute-start(bf16[1,32,1920]{2,1,0:T(8,128)(2,1)S(1)} %get-tuple-element.27), channel_id=1, source_target_pairs={{0,4},{1,5},{2,6},{3,7},{4,0},{5,1},{6,2},{7,3},{8,12},{9,13},{10,... | collective-permute-start | bytes 368648 | tf_op jit(solution)/shard_map/square_sum1/ppermute | solution.py:229
  14.0 6.3 %collective-permute-start.7 = (bf16[1,32,1920]{2,1,0:T(8,128)(2,1)S(1)}, bf16[1,32,1920]{2,1,0:T(8,128)(2,1)S(1)}, u32[]{:S(2)}, u32[]{:S(2)}) collective-permute-start(bf16[1,32,1920]{2,1,0:T(8,128)(2,1)S(1)} %get-tuple-element.28), channel_id=1, source_target_pairs={{0,2},{1,3},{2,0},{3,1},{4,6},{5,7},{6,4},{7,5},{8,10},{9,11},{10,... | collective-permute-start | bytes 368648 | tf_op jit(solution)/shard_map/square_sum1/ppermute | solution.py:229
  15.8 6.7 %collective-permute-start.6 = (bf16[1,32,1920]{2,1,0:T(8,128)(2,1)S(1)}, bf16[1,32,1920]{2,1,0:T(8,128)(2,1)S(1)}, u32[]{:S(2)}, u32[]{:S(2)}) collective-permute-start(bf16[1,32,1920]{2,1,0:T(8,128)(2,1)S(1)} %get-tuple-element.29), channel_id=1, source_target_pairs={{0,6},{1,7},{2,4},{3,5},{4,2},{5,3},{6,0},{7,1},{8,14},{9,15},{10,... | collective-permute-start | bytes 368648 | tf_op jit(solution)/shard_map/square_sum1/ppermute | solution.py:229
  17.3 9.0 %collective-permute-start.10 = (bf16[1,32,1920]{2,1,0:T(8,128)(2,1)S(1)}, bf16[1,32,1920]{2,1,0:T(8,128)(2,1)S(1)}, u32[]{:S(2)}, u32[]{:S(2)}) collective-permute-start(bf16[1,32,1920]{2,1,0:T(8,128)(2,1)S(1)} %fusion.3), channel_id=1, source_target_pairs={{0,8},{1,9},{2,10},{3,11},{4,12},{5,13},{6,14},{7,15},{8,0},{9,1},... | collective-permute-start | bytes 368648 | tf_op jit(solution)/shard_map/far_sum0/ppermute | solution.py:229
  22.5 8.1 %collective-permute-start.8 = (bf16[1,32,1920]{2,1,0:T(8,128)(2,1)S(1)}, bf16[1,32,1920]{2,1,0:T(8,128)(2,1)S(1)}, u32[]{:S(2)}, u32[]{:S(2)}) collective-permute-start(bf16[1,32,1920]{2,1,0:T(8,128)(2,1)S(1)} %fusion.2), channel_id=1, source_target_pairs={{0,12},{1,13},{2,14},{3,15},{4,8},{5,9},{6,10},{7,11},{8,4},{9,5},... | collective-permute-start | bytes 368648 | tf_op jit(solution)/shard_map/far_sum1/ppermute | solution.py:229
  26.4 6.7 %collective-permute-start.13 = (bf16[1,32,1920]{2,1,0:T(8,128)(2,1)S(1)}, bf16[1,32,1920]{2,1,0:T(8,128)(2,1)S(1)}, u32[]{:S(2)}, u32[]{:S(2)}) collective-permute-start(bf16[1,32,1920]{2,1,0:T(8,128)(2,1)S(1)} %add_convert_fusion), channel_id=1, source_target_pairs={{0,4},{1,5},{2,6},{3,7},{4,0},{5,1},{6,2},{7,3},{8,12},{9,13},{10,... | collective-permute-start | bytes 368648 | tf_op jit(solution)/shard_map/square_gather0/ppermute | solution.py:229
  26.6 8.3 %collective-permute-start.12 = (bf16[1,32,1920]{2,1,0:T(8,128)(2,1)S(1)}, bf16[1,32,1920]{2,1,0:T(8,128)(2,1)S(1)}, u32[]{:S(2)}, u32[]{:S(2)}) collective-permute-start(bf16[1,32,1920]{2,1,0:T(8,128)(2,1)S(1)} %add_convert_fusion), channel_id=1, source_target_pairs={{0,2},{1,3},{2,0},{3,1},{4,6},{5,7},{6,4},{7,5},{8,10},{9,11},{10,... | collective-permute-start | bytes 368648 | tf_op jit(solution)/shard_map/square_gather0/ppermute | solution.py:229
  28.5 8.1 %collective-permute-start.11 = (bf16[1,32,1920]{2,1,0:T(8,128)(2,1)S(1)}, bf16[1,32,1920]{2,1,0:T(8,128)(2,1)S(1)}, u32[]{:S(2)}, u32[]{:S(2)}) collective-permute-start(bf16[1,32,1920]{2,1,0:T(8,128)(2,1)S(1)} %add_convert_fusion), channel_id=1, source_target_pairs={{0,6},{1,7},{2,4},{3,5},{4,2},{5,3},{6,0},{7,1},{8,14},{9,15},{10,... | collective-permute-start | bytes 368648 | tf_op jit(solution)/shard_map/square_gather0/ppermute | solution.py:229
  30.7 8.5 %collective-permute-start.15 = (bf16[1,32,1920]{2,1,0:T(8,128)(2,1)S(1)}, bf16[1,32,1920]{2,1,0:T(8,128)(2,1)S(1)}, u32[]{:S(2)}, u32[]{:S(2)}) collective-permute-start(bf16[1,32,1920]{2,1,0:T(8,128)(2,1)S(1)} %add_convert_fusion.1), channel_id=1, source_target_pairs={{0,4},{1,5},{2,6},{3,7},{4,0},{5,1},{6,2},{7,3},{8,12},{9,13},{10,... | collective-permute-start | bytes 368648 | tf_op jit(solution)/shard_map/square_gather1/ppermute | solution.py:229
  31.2 8.0 %collective-permute-start.14 = (bf16[1,32,1920]{2,1,0:T(8,128)(2,1)S(1)}, bf16[1,32,1920]{2,1,0:T(8,128)(2,1)S(1)}, u32[]{:S(2)}, u32[]{:S(2)}) collective-permute-start(bf16[1,32,1920]{2,1,0:T(8,128)(2,1)S(1)} %add_convert_fusion.1), channel_id=1, source_target_pairs={{0,2},{1,3},{2,0},{3,1},{4,6},{5,7},{6,4},{7,5},{8,10},{9,11},{10,... | collective-permute-start | bytes 368648 | tf_op jit(solution)/shard_map/square_gather1/ppermute | solution.py:229
  33.0 6.2 %collective-permute-start.9 = (bf16[1,32,1920]{2,1,0:T(8,128)(2,1)S(1)}, bf16[1,32,1920]{2,1,0:T(8,128)(2,1)S(1)}, u32[]{:S(2)}, u32[]{:S(2)}) collective-permute-start(bf16[1,32,1920]{2,1,0:T(8,128)(2,1)S(1)} %add_convert_fusion.1), channel_id=1, source_target_pairs={{0,6},{1,7},{2,4},{3,5},{4,2},{5,3},{6,0},{7,1},{8,14},{9,15},{10,... | collective-permute-start | bytes 368648 | tf_op jit(solution)/shard_map/square_gather1/ppermute | solution.py:229
  36.8 2.7 %collective-permute-start.17 = (bf16[4,32,1920]{2,1,0:T(8,128)(2,1)S(1)}, bf16[4,32,1920]{2,1,0:T(8,128)(2,1)S(1)}, u32[]{:S(2)}, u32[]{:S(2)}) collective-permute-start(bf16[4,32,1920]{2,1,0:T(8,128)(2,1)S(1)} %pad_maximum_fusion.refs_2_), channel_id=1, source_target_pairs={{0,1},{1,0},{2,3},{3,2},{4,5},{5,4},{6,7},{7,6},{8,9},{9,8},{10,11... | collective-permute-start | bytes 1474568 | tf_op jit(solution)/shard_map/core_gather0/ppermute | solution.py:229
  39.3 1.9 %collective-permute-start.16 = (bf16[4,32,1920]{2,1,0:T(8,128)(2,1)S(1)}, bf16[4,32,1920]{2,1,0:T(8,128)(2,1)S(1)}, u32[]{:S(2)}, u32[]{:S(2)}) collective-permute-start(bf16[4,32,1920]{2,1,0:T(8,128)(2,1)S(1)} %pad_maximum_fusion.1.refs_3_), channel_id=1, source_target_pairs={{0,1},{1,0},{2,3},{3,2},{4,5},{5,4},{6,7},{7,6},{8,9},{9,8},{10,11... | collective-permute-start | bytes 1474568 | tf_op jit(solution)/shard_map/core_gather1/ppermute | solution.py:229

commit v8 on v6

--- a/solution.py
+++ b/solution.py
@@ -17,7 +17,7 @@
 CHIPS = ("across", "x", "z", "own")
 SQUARE = (6, 2, 4)
 SUM_ORDER = (2, 0, 1)
-GATHER_ORDER = (2, 0, 1)
+GATHER_ORDERS = ((2, 0, 1), (0, 2, 1))
 MIRROR = (0, 1)
 
 
@@ -259,7 +259,7 @@
         block[s] = own.astype(wire)
 
     for s in streams:
-        back = {i: send(block[s], SQUARE[i], f"square_gather{s}") for i in GATHER_ORDER}
+        back = {i: send(block[s], SQUARE[i], f"square_gather{s}") for i in GATHER_ORDERS[s]}
         got[s] = [back[i] for i in range(3)]
 
     out = None

time: 42.6 us -> 42.6 us (level)
  no operation moved by 1% of the time
where the time goes in v8:
time: 42.6 us; the launch traced here: 42.5 us
  starting transfers between devices  23.9 us (56%)
  Pallas kernels  10.4 us (24%)
  waiting for transfers between devices  7.19 us (17%)
  other arithmetic  0.68 us (2%)
    ppermute x18, starting transfers between devices, send(): return lax.ppermute(array, 'blk', [(i, i ^ bits) for i in range(devices)])  23.9 us
    ppermute x18, waiting for transfers between devices, send(): return lax.ppermute(array, 'blk', [(i, i ^ bits) for i in range(devices)])  7.19 us
    pallas_call x3, Pallas kernels, partial_sums(): pl.pallas_call(lambda *refs: partial_kernel(pieces, given, *refs), in_spe...  6.23 us
    pallas_call x3, Pallas kernels, bloch(): pl.pallas_call(lambda *refs: bloch_kernel(places, *refs), in_specs=[pl.Bl...  3.86 us
  transfers between devices with their start and end apart: 18, of which 7 were waited for; matrix products, arithmetic and copies ran while one was open for 2% of the time, Pallas kernels for 17%

profile of v8, /device:TPU:0, one launch (start us, length us, event | category | flops | bytes accessed | tf_op | source)
XLA Modules:
  0.0 42.5 jit_solution(4272901985317206640)
XLA Ops:
  0.0 2.1 %shard_map.64 = (bf16[32,128]{1,0:T(8,128)(2,1)S(1)}, bf16[4,32,1920]{2,1,0:T(8,128)(2,1)S(1)}) custom-call(s32[1]{0:T(128)} %bitcast.refs_0_, f32[1,3]{1,0:T(1,128)} %bitcast.4, s32[3,4]{1,0:T(4,128)} %refs_2_.3, bf16[4,2,16,30720]{3,2,1,0:T(8,128)(2,1)} %refs_2_.5), custom_call_target="tpu_custom_call" | custom-call | flops 62914560 | bytes 1966080 | tf_op jit(solution)/shard_map/pallas_call | solution.py:130
  2.1 0.5 %collective-permute-start = (bf16[4,32,1920]{2,1,0:T(8,128)(2,1)S(1)}, bf16[4,32,1920]{2,1,0:T(8,128)(2,1)S(1)}, u32[]{:S(2)}, u32[]{:S(2)}) collective-permute-start(bf16[4,32,1920]{2,1,0:T(8,128)(2,1)S(1)} %get-tuple-element.15), channel_id=1, source_target_pairs={{0,1},{1,0},{2,3},{3,2},{4,5},{5,4},{6,7},{7,6},{8,9},{9,8},{10,11... | collective-permute-start | bytes 1474568 | tf_op jit(solution)/shard_map/core_sum0/ppermute | solution.py:229
  2.6 2.4 %shard_map.65 = (f32[4,32,1920]{2,1,0:T(8,128)S(1)}, bf16[4,32,1920]{2,1,0:T(8,128)(2,1)S(1)}) custom-call(s32[1]{0:T(128)} %bitcast.refs_0_, bf16[32,128]{1,0:T(8,128)(2,1)S(1)} %get-tuple-element.13.refs_1_, bf16[4,2,16,30720]{3,2,1,0:T(8,128)(2,1)} %refs_2_.5), custom_call_target="tpu_custom_call" | custom-call | flops 125829120 | bytes 3932160 | tf_op jit(solution)/shard_map/pallas_call | solution.py:130
  5.0 0.2 collective-permute-start.4
  5.2 0.1 fusion.5
  5.3 3.1 %collective-permute-start.1 = (bf16[1,32,1920]{2,1,0:T(8,128)(2,1)S(1)}, bf16[1,32,1920]{2,1,0:T(8,128)(2,1)S(1)}, u32[]{:S(2)}, u32[]{:S(2)}) collective-permute-start(bf16[1,32,1920]{2,1,0:T(8,128)(2,1)S(1)} %get-tuple-element.28), channel_id=1, source_target_pairs={{0,4},{1,5},{2,6},{3,7},{4,0},{5,1},{6,2},{7,3},{8,12},{9,13},{10,... | collective-permute-start | bytes 368648 | tf_op jit(solution)/shard_map/square_sum0/ppermute | solution.py:229
  8.5 1.5 %collective-permute-start.3 = (bf16[1,32,1920]{2,1,0:T(8,128)(2,1)S(1)}, bf16[1,32,1920]{2,1,0:T(8,128)(2,1)S(1)}, u32[]{:S(2)}, u32[]{:S(2)}) collective-permute-start(bf16[1,32,1920]{2,1,0:T(8,128)(2,1)S(1)} %get-tuple-element.29), channel_id=1, source_target_pairs={{0,2},{1,3},{2,0},{3,1},{4,6},{5,7},{6,4},{7,5},{8,10},{9,11},{10,... | collective-permute-start | bytes 368648 | tf_op jit(solution)/shard_map/square_sum0/ppermute | solution.py:229
  10.0 1.7 %shard_map.67 = f32[4,32,1920]{2,1,0:T(8,128)S(1)} custom-call(s32[1]{0:T(128)} %bitcast.refs_0_, bf16[32,128]{1,0:T(8,128)(2,1)S(1)} %get-tuple-element.13.refs_1_, bf16[4,2,16,30720]{3,2,1,0:T(8,128)(2,1)} %refs_2_.5), custom_call_target="tpu_custom_call" | custom-call | flops 62914560 | bytes 1966080 | tf_op jit(solution)/shard_map/pallas_call | solution.py:130
  11.8 0.1 fusion.4
  12.0 2.0 %collective-permute-start.5 = (bf16[1,32,1920]{2,1,0:T(8,128)(2,1)S(1)}, bf16[1,32,1920]{2,1,0:T(8,128)(2,1)S(1)}, u32[]{:S(2)}, u32[]{:S(2)}) collective-permute-start(bf16[1,32,1920]{2,1,0:T(8,128)(2,1)S(1)} %get-tuple-element.25), channel_id=1, source_target_pairs={{0,4},{1,5},{2,6},{3,7},{4,0},{5,1},{6,2},{7,3},{8,12},{9,13},{10,... | collective-permute-start | bytes 368648 | tf_op jit(solution)/shard_map/square_sum1/ppermute | solution.py:229
  14.0 1.5 %collective-permute-start.7 = (bf16[1,32,1920]{2,1,0:T(8,128)(2,1)S(1)}, bf16[1,32,1920]{2,1,0:T(8,128)(2,1)S(1)}, u32[]{:S(2)}, u32[]{:S(2)}) collective-permute-start(bf16[1,32,1920]{2,1,0:T(8,128)(2,1)S(1)} %get-tuple-element.26), channel_id=1, source_target_pairs={{0,2},{1,3},{2,0},{3,1},{4,6},{5,7},{6,4},{7,5},{8,10},{9,11},{10,... | collective-permute-start | bytes 368648 | tf_op jit(solution)/shard_map/square_sum1/ppermute | solution.py:229
  15.5 0.3 collective-permute-done.3
  15.7 1.4 %collective-permute-start.6 = (bf16[1,32,1920]{2,1,0:T(8,128)(2,1)S(1)}, bf16[1,32,1920]{2,1,0:T(8,128)(2,1)S(1)}, u32[]{:S(2)}, u32[]{:S(2)}) collective-permute-start(bf16[1,32,1920]{2,1,0:T(8,128)(2,1)S(1)} %get-tuple-element.27), channel_id=1, source_target_pairs={{0,6},{1,7},{2,4},{3,5},{4,2},{5,3},{6,0},{7,1},{8,14},{9,15},{10,... | collective-permute-start | bytes 368648 | tf_op jit(solution)/shard_map/square_sum1/ppermute | solution.py:229
  17.2 2.7 %collective-permute-start.10 = (bf16[1,32,1920]{2,1,0:T(8,128)(2,1)S(1)}, bf16[1,32,1920]{2,1,0:T(8,128)(2,1)S(1)}, u32[]{:S(2)}, u32[]{:S(2)}) collective-permute-start(bf16[1,32,1920]{2,1,0:T(8,128)(2,1)S(1)} %fusion.3), channel_id=1, source_target_pairs={{0,8},{1,9},{2,10},{3,11},{4,12},{5,13},{6,14},{7,15},{8,0},{9,1},... | collective-permute-start | bytes 368648 | tf_op jit(solution)/shard_map/far_sum0/ppermute | solution.py:229
  19.9 0.3 shard_map.66.refs_1_
  20.3 2.2 %collective-permute-done.6 = bf16[1,32,1920]{2,1,0:T(8,128)(2,1)S(1)} collective-permute-done((bf16[1,32,1920]{2,1,0:T(8,128)(2,1)S(1)}, bf16[1,32,1920]{2,1,0:T(8,128)(2,1)S(1)}, u32[]{:S(2)}, u32[]{:S(2)}) %collective-permute-start.6) | collective-permute-done | bytes 122912 | tf_op jit(solution)/shard_map/square_sum1/ppermute | solution.py:229
  22.5 3.8 %collective-permute-start.8 = (bf16[1,32,1920]{2,1,0:T(8,128)(2,1)S(1)}, bf16[1,32,1920]{2,1,0:T(8,128)(2,1)S(1)}, u32[]{:S(2)}, u32[]{:S(2)}) collective-permute-start(bf16[1,32,1920]{2,1,0:T(8,128)(2,1)S(1)} %fusion.2), channel_id=1, source_target_pairs={{0,12},{1,13},{2,14},{3,15},{4,8},{5,9},{6,10},{7,11},{8,4},{9,5},... | collective-permute-start | bytes 368648 | tf_op jit(solution)/shard_map/far_sum1/ppermute | solution.py:229
  26.3 0.2 collective-permute-start.13
  26.6 1.9 %collective-permute-start.12 = (bf16[1,32,1920]{2,1,0:T(8,128)(2,1)S(1)}, bf16[1,32,1920]{2,1,0:T(8,128)(2,1)S(1)}, u32[]{:S(2)}, u32[]{:S(2)}) collective-permute-start(bf16[1,32,1920]{2,1,0:T(8,128)(2,1)S(1)} %add_convert_fusion), channel_id=1, source_target_pairs={{0,2},{1,3},{2,0},{3,1},{4,6},{5,7},{6,4},{7,5},{8,10},{9,11},{10,... | collective-permute-start | bytes 368648 | tf_op jit(solution)/shard_map/square_gather0/ppermute | solution.py:229
  28.5 1.4 %collective-permute-start.11 = (bf16[1,32,1920]{2,1,0:T(8,128)(2,1)S(1)}, bf16[1,32,1920]{2,1,0:T(8,128)(2,1)S(1)}, u32[]{:S(2)}, u32[]{:S(2)}) collective-permute-start(bf16[1,32,1920]{2,1,0:T(8,128)(2,1)S(1)} %add_convert_fusion), channel_id=1, source_target_pairs={{0,6},{1,7},{2,4},{3,5},{4,2},{5,3},{6,0},{7,1},{8,14},{9,15},{10,... | collective-permute-start | bytes 368648 | tf_op jit(solution)/shard_map/square_gather0/ppermute | solution.py:229
  29.9 0.7 %collective-permute-done.8 = bf16[1,32,1920]{2,1,0:T(8,128)(2,1)S(1)} collective-permute-done((bf16[1,32,1920]{2,1,0:T(8,128)(2,1)S(1)}, bf16[1,32,1920]{2,1,0:T(8,128)(2,1)S(1)}, u32[]{:S(2)}, u32[]{:S(2)}) %collective-permute-start.8) | collective-permute-done | bytes 122912 | tf_op jit(solution)/shard_map/far_sum1/ppermute | solution.py:229
  30.6 0.1 add_convert_fusion.1
  30.7 0.3 collective-permute-start.15
  31.0 1.3 %collective-permute-start.14 = (bf16[1,32,1920]{2,1,0:T(8,128)(2,1)S(1)}, bf16[1,32,1920]{2,1,0:T(8,128)(2,1)S(1)}, u32[]{:S(2)}, u32[]{:S(2)}) collective-permute-start(bf16[1,32,1920]{2,1,0:T(8,128)(2,1)S(1)} %add_convert_fusion.1), channel_id=1, source_target_pairs={{0,2},{1,3},{2,0},{3,1},{4,6},{5,7},{6,4},{7,5},{8,10},{9,11},{10,... | collective-permute-start | bytes 368648 | tf_op jit(solution)/shard_map/square_gather1/ppermute | solution.py:229
  32.3 0.7 %collective-permute-done.13 = bf16[1,32,1920]{2,1,0:T(8,128)(2,1)S(1)} collective-permute-done((bf16[1,32,1920]{2,1,0:T(8,128)(2,1)S(1)}, bf16[1,32,1920]{2,1,0:T(8,128)(2,1)S(1)}, u32[]{:S(2)}, u32[]{:S(2)}) %collective-permute-start.13) | collective-permute-done | bytes 122912 | tf_op jit(solution)/shard_map/square_gather0/ppermute | solution.py:229
  33.0 2.0 %collective-permute-start.9 = (bf16[1,32,1920]{2,1,0:T(8,128)(2,1)S(1)}, bf16[1,32,1920]{2,1,0:T(8,128)(2,1)S(1)}, u32[]{:S(2)}, u32[]{:S(2)}) collective-permute-start(bf16[1,32,1920]{2,1,0:T(8,128)(2,1)S(1)} %add_convert_fusion.1), channel_id=1, source_target_pairs={{0,6},{1,7},{2,4},{3,5},{4,2},{5,3},{6,0},{7,1},{8,14},{9,15},{10,... | collective-permute-start | bytes 368648 | tf_op jit(solution)/shard_map/square_gather1/ppermute | solution.py:229
  35.0 1.7 %collective-permute-done.11 = bf16[1,32,1920]{2,1,0:T(8,128)(2,1)S(1)} collective-permute-done((bf16[1,32,1920]{2,1,0:T(8,128)(2,1)S(1)}, bf16[1,32,1920]{2,1,0:T(8,128)(2,1)S(1)}, u32[]{:S(2)}, u32[]{:S(2)}) %collective-permute-start.11) | collective-permute-done | bytes 122912 | tf_op jit(solution)/shard_map/square_gather0/ppermute | solution.py:229
  36.9 1.2 %shard_map.68.refs_4_ = bf16[2,32,30720]{2,1,0:T(8,128)(2,1)} custom-call(s32[1]{0:T(128)} %bitcast.refs_0_, bf16[64,32]{1,0:T(8,128)(2,1)S(1)} %shard_map.66.refs_1_, bf16[4,32,1920]{2,1,0:T(8,128)(2,1)S(1)} %pad_maximum_fusion.refs_2_), custom_call_target="tpu_custom_call" | custom-call | flops 31457280 | bytes 983040 | tf_op jit(solution)/shard_map/pallas_call | solution.py:199
  38.0 1.2 %collective-permute-done.9 = bf16[1,32,1920]{2,1,0:T(8,128)(2,1)S(1)} collective-permute-done((bf16[1,32,1920]{2,1,0:T(8,128)(2,1)S(1)}, bf16[1,32,1920]{2,1,0:T(8,128)(2,1)S(1)}, u32[]{:S(2)}, u32[]{:S(2)}) %collective-permute-start.9) | collective-permute-done | bytes 122912 | tf_op jit(solution)/shard_map/square_gather1/ppermute | solution.py:229
  39.5 1.5 %shard_map.69.refs_3_ = bf16[2,32,30720]{2,1,0:T(8,128)(2,1)} custom-call(s32[1]{0:T(128)} %bitcast.refs_0_, bf16[64,32]{1,0:T(8,128)(2,1)S(1)} %shard_map.66.refs_1_, bf16[4,32,1920]{2,1,0:T(8,128)(2,1)S(1)} %collective-permute-done.17.refs_2_, bf16[4,32,1920]{2,1,0:T(8,128)(2,1)S(1)} %pad_maximum_fusion.1.refs_3_, ...), custom_call_target="tpu_custom_call", output_to_operand_aliasing={{}: (4, {})} | custom-call | flops 62914560 | bytes 1966080 | tf_op jit(solution)/shard_map/pallas_call | solution.py:199
  41.0 0.3 collective-permute-done.16.refs_2_
  41.3 1.2 %shard_map.70 = bf16[2,32,30720]{2,1,0:T(8,128)(2,1)} custom-call(s32[1]{0:T(128)} %bitcast.refs_0_, bf16[64,32]{1,0:T(8,128)(2,1)S(1)} %shard_map.66.refs_1_, bf16[4,32,1920]{2,1,0:T(8,128)(2,1)S(1)} %collective-permute-done.16.refs_2_, bf16[2,32,30720]{2,1,0:T(8,128)(2,1)} %shard_map.69.refs_3_), custom_call_target="tpu_custom_call", output_to_operand_aliasing={{}: (3, {})} | custom-call | flops 31457280 | bytes 983040 | tf_op jit(solution)/shard_map/pallas_call | solution.py:199
  (28 shorter events, 0.7 us)
Async XLA Ops:
  2.1 3.0 %collective-permute-start = (bf16[4,32,1920]{2,1,0:T(8,128)(2,1)S(1)}, bf16[4,32,1920]{2,1,0:T(8,128)(2,1)S(1)}, u32[]{:S(2)}, u32[]{:S(2)}) collective-permute-start(bf16[4,32,1920]{2,1,0:T(8,128)(2,1)S(1)} %get-tuple-element.15), channel_id=1, source_target_pairs={{0,1},{1,0},{2,3},{3,2},{4,5},{5,4},{6,7},{7,6},{8,9},{9,8},{10,11... | collective-permute-start | bytes 1474568 | tf_op jit(solution)/shard_map/core_sum0/ppermute | solution.py:229
  5.0 6.8 %collective-permute-start.4 = (bf16[4,32,1920]{2,1,0:T(8,128)(2,1)S(1)}, bf16[4,32,1920]{2,1,0:T(8,128)(2,1)S(1)}, u32[]{:S(2)}, u32[]{:S(2)}) collective-permute-start(bf16[4,32,1920]{2,1,0:T(8,128)(2,1)S(1)} %get-tuple-element.18), channel_id=1, source_target_pairs={{0,1},{1,0},{2,3},{3,2},{4,5},{5,4},{6,7},{7,6},{8,9},{9,8},{10,11... | collective-permute-start | bytes 1474568 | tf_op jit(solution)/shard_map/core_sum1/ppermute | solution.py:229
  5.3 11.9 %collective-permute-start.1 = (bf16[1,32,1920]{2,1,0:T(8,128)(2,1)S(1)}, bf16[1,32,1920]{2,1,0:T(8,128)(2,1)S(1)}, u32[]{:S(2)}, u32[]{:S(2)}) collective-permute-start(bf16[1,32,1920]{2,1,0:T(8,128)(2,1)S(1)} %get-tuple-element.28), channel_id=1, source_target_pairs={{0,4},{1,5},{2,6},{3,7},{4,0},{5,1},{6,2},{7,3},{8,12},{9,13},{10,... | collective-permute-start | bytes 368648 | tf_op jit(solution)/shard_map/square_sum0/ppermute | solution.py:229
  8.5 7.3 %collective-permute-start.3 = (bf16[1,32,1920]{2,1,0:T(8,128)(2,1)S(1)}, bf16[1,32,1920]{2,1,0:T(8,128)(2,1)S(1)}, u32[]{:S(2)}, u32[]{:S(2)}) collective-permute-start(bf16[1,32,1920]{2,1,0:T(8,128)(2,1)S(1)} %get-tuple-element.29), channel_id=1, source_target_pairs={{0,2},{1,3},{2,0},{3,1},{4,6},{5,7},{6,4},{7,5},{8,10},{9,11},{10,... | collective-permute-start | bytes 368648 | tf_op jit(solution)/shard_map/square_sum0/ppermute | solution.py:229
  9.9 7.2 %collective-permute-start.2 = (bf16[1,32,1920]{2,1,0:T(8,128)(2,1)S(1)}, bf16[1,32,1920]{2,1,0:T(8,128)(2,1)S(1)}, u32[]{:S(2)}, u32[]{:S(2)}) collective-permute-start(bf16[1,32,1920]{2,1,0:T(8,128)(2,1)S(1)} %get-tuple-element.30), channel_id=1, source_target_pairs={{0,6},{1,7},{2,4},{3,5},{4,2},{5,3},{6,0},{7,1},{8,14},{9,15},{10,... | collective-permute-start | bytes 368648 | tf_op jit(solution)/shard_map/square_sum0/ppermute | solution.py:229
  11.7 8.2 %copy-start = (s32[3,32]{1,0:T(4,128)S(1)}, s32[3,32]{1,0:T(4,128)}, u32[]{:S(2)}) copy-start(s32[3,32]{1,0:T(4,128)} %q_ref) | copy-start | bytes 1156
  11.7 8.2 %copy-start.1 = (s32[3,16]{1,0:T(4,128)S(1)}, s32[3,16]{1,0:T(4,128)}, u32[]{:S(2)}) copy-start(s32[3,16]{1,0:T(4,128)} %phon_ref.1) | copy-start | bytes 580
  11.8 8.2 %copy-start.2 = (s32[16]{0:T(128)S(1)}, s32[16]{0:T(128)}, u32[]{:S(2)}) copy-start(s32[16]{0:T(128)} %param.9) | copy-start | bytes 196
  12.0 8.3 %collective-permute-start.5 = (bf16[1,32,1920]{2,1,0:T(8,128)(2,1)S(1)}, bf16[1,32,1920]{2,1,0:T(8,128)(2,1)S(1)}, u32[]{:S(2)}, u32[]{:S(2)}) collective-permute-start(bf16[1,32,1920]{2,1,0:T(8,128)(2,1)S(1)} %get-tuple-element.25), channel_id=1, source_target_pairs={{0,4},{1,5},{2,6},{3,7},{4,0},{5,1},{6,2},{7,3},{8,12},{9,13},{10,... | collective-permute-start | bytes 368648 | tf_op jit(solution)/shard_map/square_sum1/ppermute | solution.py:229
  14.0 6.3 %collective-permute-start.7 = (bf16[1,32,1920]{2,1,0:T(8,128)(2,1)S(1)}, bf16[1,32,1920]{2,1,0:T(8,128)(2,1)S(1)}, u32[]{:S(2)}, u32[]{:S(2)}) collective-permute-start(bf16[1,32,1920]{2,1,0:T(8,128)(2,1)S(1)} %get-tuple-element.26), channel_id=1, source_target_pairs={{0,2},{1,3},{2,0},{3,1},{4,6},{5,7},{6,4},{7,5},{8,10},{9,11},{10,... | collective-permute-start | bytes 368648 | tf_op jit(solution)/shard_map/square_sum1/ppermute | solution.py:229
  15.7 6.7 %collective-permute-start.6 = (bf16[1,32,1920]{2,1,0:T(8,128)(2,1)S(1)}, bf16[1,32,1920]{2,1,0:T(8,128)(2,1)S(1)}, u32[]{:S(2)}, u32[]{:S(2)}) collective-permute-start(bf16[1,32,1920]{2,1,0:T(8,128)(2,1)S(1)} %get-tuple-element.27), channel_id=1, source_target_pairs={{0,6},{1,7},{2,4},{3,5},{4,2},{5,3},{6,0},{7,1},{8,14},{9,15},{10,... | collective-permute-start | bytes 368648 | tf_op jit(solution)/shard_map/square_sum1/ppermute | solution.py:229
  17.2 9.0 %collective-permute-start.10 = (bf16[1,32,1920]{2,1,0:T(8,128)(2,1)S(1)}, bf16[1,32,1920]{2,1,0:T(8,128)(2,1)S(1)}, u32[]{:S(2)}, u32[]{:S(2)}) collective-permute-start(bf16[1,32,1920]{2,1,0:T(8,128)(2,1)S(1)} %fusion.3), channel_id=1, source_target_pairs={{0,8},{1,9},{2,10},{3,11},{4,12},{5,13},{6,14},{7,15},{8,0},{9,1},... | collective-permute-start | bytes 368648 | tf_op jit(solution)/shard_map/far_sum0/ppermute | solution.py:229
  22.5 8.1 %collective-permute-start.8 = (bf16[1,32,1920]{2,1,0:T(8,128)(2,1)S(1)}, bf16[1,32,1920]{2,1,0:T(8,128)(2,1)S(1)}, u32[]{:S(2)}, u32[]{:S(2)}) collective-permute-start(bf16[1,32,1920]{2,1,0:T(8,128)(2,1)S(1)} %fusion.2), channel_id=1, source_target_pairs={{0,12},{1,13},{2,14},{3,15},{4,8},{5,9},{6,10},{7,11},{8,4},{9,5},... | collective-permute-start | bytes 368648 | tf_op jit(solution)/shard_map/far_sum1/ppermute | solution.py:229
  26.3 6.7 %collective-permute-start.13 = (bf16[1,32,1920]{2,1,0:T(8,128)(2,1)S(1)}, bf16[1,32,1920]{2,1,0:T(8,128)(2,1)S(1)}, u32[]{:S(2)}, u32[]{:S(2)}) collective-permute-start(bf16[1,32,1920]{2,1,0:T(8,128)(2,1)S(1)} %add_convert_fusion), channel_id=1, source_target_pairs={{0,4},{1,5},{2,6},{3,7},{4,0},{5,1},{6,2},{7,3},{8,12},{9,13},{10,... | collective-permute-start | bytes 368648 | tf_op jit(solution)/shard_map/square_gather0/ppermute | solution.py:229
  26.6 8.4 %collective-permute-start.12 = (bf16[1,32,1920]{2,1,0:T(8,128)(2,1)S(1)}, bf16[1,32,1920]{2,1,0:T(8,128)(2,1)S(1)}, u32[]{:S(2)}, u32[]{:S(2)}) collective-permute-start(bf16[1,32,1920]{2,1,0:T(8,128)(2,1)S(1)} %add_convert_fusion), channel_id=1, source_target_pairs={{0,2},{1,3},{2,0},{3,1},{4,6},{5,7},{6,4},{7,5},{8,10},{9,11},{10,... | collective-permute-start | bytes 368648 | tf_op jit(solution)/shard_map/square_gather0/ppermute | solution.py:229
  28.5 8.2 %collective-permute-start.11 = (bf16[1,32,1920]{2,1,0:T(8,128)(2,1)S(1)}, bf16[1,32,1920]{2,1,0:T(8,128)(2,1)S(1)}, u32[]{:S(2)}, u32[]{:S(2)}) collective-permute-start(bf16[1,32,1920]{2,1,0:T(8,128)(2,1)S(1)} %add_convert_fusion), channel_id=1, source_target_pairs={{0,6},{1,7},{2,4},{3,5},{4,2},{5,3},{6,0},{7,1},{8,14},{9,15},{10,... | collective-permute-start | bytes 368648 | tf_op jit(solution)/shard_map/square_gather0/ppermute | solution.py:229
  30.7 8.6 %collective-permute-start.15 = (bf16[1,32,1920]{2,1,0:T(8,128)(2,1)S(1)}, bf16[1,32,1920]{2,1,0:T(8,128)(2,1)S(1)}, u32[]{:S(2)}, u32[]{:S(2)}) collective-permute-start(bf16[1,32,1920]{2,1,0:T(8,128)(2,1)S(1)} %add_convert_fusion.1), channel_id=1, source_target_pairs={{0,4},{1,5},{2,6},{3,7},{4,0},{5,1},{6,2},{7,3},{8,12},{9,13},{10,... | collective-permute-start | bytes 368648 | tf_op jit(solution)/shard_map/square_gather1/ppermute | solution.py:229
  31.0 8.3 %collective-permute-start.14 = (bf16[1,32,1920]{2,1,0:T(8,128)(2,1)S(1)}, bf16[1,32,1920]{2,1,0:T(8,128)(2,1)S(1)}, u32[]{:S(2)}, u32[]{:S(2)}) collective-permute-start(bf16[1,32,1920]{2,1,0:T(8,128)(2,1)S(1)} %add_convert_fusion.1), channel_id=1, source_target_pairs={{0,2},{1,3},{2,0},{3,1},{4,6},{5,7},{6,4},{7,5},{8,10},{9,11},{10,... | collective-permute-start | bytes 368648 | tf_op jit(solution)/shard_map/square_gather1/ppermute | solution.py:229
  33.0 6.3 %collective-permute-start.9 = (bf16[1,32,1920]{2,1,0:T(8,128)(2,1)S(1)}, bf16[1,32,1920]{2,1,0:T(8,128)(2,1)S(1)}, u32[]{:S(2)}, u32[]{:S(2)}) collective-permute-start(bf16[1,32,1920]{2,1,0:T(8,128)(2,1)S(1)} %add_convert_fusion.1), channel_id=1, source_target_pairs={{0,6},{1,7},{2,4},{3,5},{4,2},{5,3},{6,0},{7,1},{8,14},{9,15},{10,... | collective-permute-start | bytes 368648 | tf_op jit(solution)/shard_map/square_gather1/ppermute | solution.py:229
  36.8 2.7 %collective-permute-start.17 = (bf16[4,32,1920]{2,1,0:T(8,128)(2,1)S(1)}, bf16[4,32,1920]{2,1,0:T(8,128)(2,1)S(1)}, u32[]{:S(2)}, u32[]{:S(2)}) collective-permute-start(bf16[4,32,1920]{2,1,0:T(8,128)(2,1)S(1)} %pad_maximum_fusion.refs_2_), channel_id=1, source_target_pairs={{0,1},{1,0},{2,3},{3,2},{4,5},{5,4},{6,7},{7,6},{8,9},{9,8},{10,11... | collective-permute-start | bytes 1474568 | tf_op jit(solution)/shard_map/core_gather0/ppermute | solution.py:229
  39.4 1.9 %collective-permute-start.16 = (bf16[4,32,1920]{2,1,0:T(8,128)(2,1)S(1)}, bf16[4,32,1920]{2,1,0:T(8,128)(2,1)S(1)}, u32[]{:S(2)}, u32[]{:S(2)}) collective-permute-start(bf16[4,32,1920]{2,1,0:T(8,128)(2,1)S(1)} %pad_maximum_fusion.1.refs_3_), channel_id=1, source_target_pairs={{0,1},{1,0},{2,3},{3,2},{4,5},{5,4},{6,7},{7,6},{8,9},{9,8},{10,11... | collective-permute-start | bytes 1474568 | tf_op jit(solution)/shard_map/core_gather1/ppermute | solution.py:229
